TPU v7x, 32 devices: a whole 2x2x4 slice. The times are simulated.
32 devices in a mesh: dp: 4 (over z), blk: 4 (over x, core), head: 2 (over y).
Axes of the slice: x: 2, y: 2, z: 4, core: 2. Of those that a mesh axis runs over, the one named last changes fastest.
Arguments:
- tokens: bfloat16 [4, 1024, 1024], P('dp', ('blk', 'head')), may hold values from -6 to 6
- segment_ids: int32 [4, 1024], P('dp', 'blk'), may hold values from -1 to 15, as said below
- cotangent: bfloat16 [4, 1024, 1024], P('dp', ('blk', 'head')), may hold values from -6 to 6
- w_query: bfloat16 [1024, 1024], P(('blk', 'head')), may hold values from -0.1875 to 0.1875
- w_key: bfloat16 [1024, 1024], P(('blk', 'head')), may hold values from -0.1875 to 0.1875
- w_value: bfloat16 [1024, 1024], P(('blk', 'head')), may hold values from -0.1875 to 0.1875
- w_out: bfloat16 [1024, 1024], P(('blk', 'head')), may hold values from -6 to 6
- w_in: bfloat16 [1024, 4096], P(('blk', 'head')), may hold values from -0.1875 to 0.1875
- w_back: bfloat16 [4096, 1024], P(('blk', 'head')), may hold values from -0.09375 to 0.09375
- bias_query: bfloat16 [1024], P(('blk', 'head')), may hold values from -3 to 3
- bias_value: bfloat16 [1024], P(('blk', 'head')), may hold values from -3 to 3
- bias_out: bfloat16 [1024], P(('blk', 'head')), may hold values from -3 to 3
- bias_in: bfloat16 [4096], P(('blk', 'head')), may hold values from -3 to 3
- bias_back: bfloat16 [1024], P(('blk', 'head')), may hold values from -3 to 3
- first_gain: bfloat16 [1024], P(('blk', 'head')), may hold values from 0.5 to 1.5
- first_shift: bfloat16 [1024], P(('blk', 'head')), may hold values from -3 to 3
- second_gain: bfloat16 [1024], P(('blk', 'head')), may hold values from 0.5 to 1.5
- second_shift: bfloat16 [1024], P(('blk', 'head')), may hold values from -3 to 3
Outputs:
- layer_output: bfloat16 [4, 1024, 1024], P('dp', ('blk', 'head'))
- input_grad: float32 [4, 1024, 1024], P('dp', ('blk', 'head'))
- grad_w_query: float32 [1024, 1024], P(('blk', 'head'))
- grad_w_key: float32 [1024, 1024], P(('blk', 'head'))
- grad_w_value: float32 [1024, 1024], P(('blk', 'head'))
- grad_w_out: float32 [1024, 1024], P(('blk', 'head'))
- grad_w_in: float32 [1024, 4096], P(('blk', 'head'))
- grad_w_back: float32 [4096, 1024], P(('blk', 'head'))
- grad_bias_query: float32 [1024], P(('blk', 'head'))
- grad_bias_value: float32 [1024], P(('blk', 'head'))
- grad_bias_out: float32 [1024], P(('blk', 'head'))
- grad_bias_in: float32 [4096], P(('blk', 'head'))
- grad_bias_back: float32 [1024], P(('blk', 'head'))
- grad_first_gain: float32 [1024], P(('blk', 'head'))
- grad_first_shift: float32 [1024], P(('blk', 'head'))
- grad_second_gain: float32 [1024], P(('blk', 'head'))
- grad_second_shift: float32 [1024], P(('blk', 'head'))
Inputs may be any that keep to these rules, and one draw needn't show every extreme that they name: `segment_ids`: within a sequence the ids start at 0 and rise by one from document to document before the slack; each document has 64 to 512 positions but for the last one, which the sequence's end or its slack cuts; the last 1 to 64 positions of every sequence are slack, marked -1; one sequence of the whole batch, drawn from the seed, is a single document up to its slack, and another one is packed with documents of exactly 64 positions and has a single slack position.
All inputs are finite; a program needn't handle non-finite values.
Results may differ from a plain program's by a relative error of at most 0.025.
Values may be sent and summed in bfloat16 or wider, within the bound.
A program may use at most 256 MiB of HBM per device.

v0:
```python
from functools import partial

import jax
import jax.numpy as jnp
from jax import lax
from jax.sharding import PartitionSpec as P

HD = 64


def flat_dot(left_side, right_side):
    return jnp.dot(
        left_side.reshape(-1, left_side.shape[-1]), right_side, preferred_element_type=jnp.float32
    )


def inner_dot(left_side, right_side):
    return jnp.einsum(
        "ra,rb->ab",
        left_side.reshape(-1, left_side.shape[-1]),
        right_side.reshape(-1, right_side.shape[-1]),
        preferred_element_type=jnp.float32,
    )


def layer_norm(value_rows, gain_row, shift_row):
    centre = jnp.mean(value_rows, -1, keepdims=True)
    centred = value_rows - centre
    spread = jnp.mean(centred * centred, -1, keepdims=True)
    return centred * lax.rsqrt(spread + 1e-05) * gain_row + shift_row


def head_view(array_in):
    return array_in.reshape(array_in.shape[0], array_in.shape[1], -1, HD)


def allowed_pairs(query_ids, key_ids):
    same_doc = (query_ids[:, :, None] == key_ids[:, None, :]) & (key_ids[:, None, :] >= 0)
    return same_doc[:, None]


def forward_step(state_now, arrived, local_data):
    running_max, running_sum, weighted = state_now
    key_block, value_block, key_ids = arrived
    query_block, query_ids = local_data
    scores = jnp.einsum(
        "gqhd,gkhd->ghqk",
        head_view(query_block),
        head_view(key_block),
        preferred_element_type=jnp.float32,
    )
    allowed = allowed_pairs(query_ids, key_ids)
    masked = jnp.where(allowed, scores, -1e30)
    new_max = jnp.maximum(running_max, jnp.max(masked, -1))
    exponents = jnp.where(allowed, jnp.exp(masked - new_max[..., None]), 0.0)
    running_sum = jnp.sum(exponents, -1)
    weighted = jnp.einsum(
        "ghqk,gkhd->ghqd",
        exponents.astype(jnp.bfloat16),
        head_view(value_block),
        preferred_element_type=jnp.float32,
    )
    return (new_max, running_sum, weighted)


def probabilities(query_block, key_block, query_ids, key_ids, log_sums):
    scores = jnp.einsum(
        "gqhd,gkhd->ghqk",
        head_view(query_block),
        head_view(key_block),
        preferred_element_type=jnp.float32,
    )
    allowed = allowed_pairs(query_ids, key_ids)
    masked = jnp.where(allowed, scores, -1e30)
    return jnp.where(allowed, jnp.exp(masked - log_sums.transpose(0, 2, 1)[..., None]), 0.0)


def score_grads(weights_now, grad_block, value_block, deltas):
    grad_weights = jnp.einsum(
        "gqhd,gkhd->ghqk",
        head_view(grad_block),
        head_view(value_block),
        preferred_element_type=jnp.float32,
    )
    return (weights_now * (grad_weights - deltas.transpose(0, 2, 1)[..., None])).astype(
        jnp.bfloat16
    )


def heads_to_rows(array_in):
    return array_in.transpose(0, 2, 1, 3).reshape(array_in.shape[0], array_in.shape[2], -1)


def per_device(
    tokens,
    segment_ids,
    cotangent,
    w_query,
    w_key,
    w_value,
    w_out,
    w_in,
    w_back,
    bias_query,
    bias_value,
    bias_out,
    bias_in,
    bias_back,
    first_gain,
    first_shift,
    second_gain,
    second_shift,
):
    (
        query_full,
        key_full,
        value_full,
        out_full,
        in_full,
        back_full,
        query_bias,
        value_bias,
        out_bias,
        in_bias,
        back_bias,
        gain_one,
        shift_one,
        gain_two,
        shift_two,
    ) = (
        lax.all_gather(w_query, ("blk", "head"), axis=0, tiled=True),
        lax.all_gather(w_key, ("blk", "head"), axis=0, tiled=True),
        lax.all_gather(w_value, ("blk", "head"), axis=0, tiled=True),
        lax.all_gather(w_out, ("blk", "head"), axis=0, tiled=True),
        lax.all_gather(w_in, ("blk", "head"), axis=0, tiled=True),
        lax.all_gather(w_back, ("blk", "head"), axis=0, tiled=True),
        lax.all_gather(bias_query, ("blk", "head"), axis=0, tiled=True),
        lax.all_gather(bias_value, ("blk", "head"), axis=0, tiled=True),
        lax.all_gather(bias_out, ("blk", "head"), axis=0, tiled=True),
        lax.all_gather(bias_in, ("blk", "head"), axis=0, tiled=True),
        lax.all_gather(bias_back, ("blk", "head"), axis=0, tiled=True),
        lax.all_gather(first_gain, ("blk", "head"), axis=0, tiled=True),
        lax.all_gather(first_shift, ("blk", "head"), axis=0, tiled=True),
        lax.all_gather(second_gain, ("blk", "head"), axis=0, tiled=True),
        lax.all_gather(second_shift, ("blk", "head"), axis=0, tiled=True),
    )
    query_bias = query_bias.astype(jnp.float32)
    value_bias = value_bias.astype(jnp.float32)
    out_bias = out_bias.astype(jnp.float32)
    in_bias = in_bias.astype(jnp.float32)
    back_bias = back_bias.astype(jnp.float32)
    gain_one = gain_one.astype(jnp.float32)
    shift_one = shift_one.astype(jnp.float32)
    gain_two = gain_two.astype(jnp.float32)
    shift_two = shift_two.astype(jnp.float32)
    seq_count = tokens.shape[0]
    query_tok = (
        ((flat_dot(tokens, query_full) + query_bias) * 0.125)
        .astype(jnp.bfloat16)
        .reshape(tokens.shape)
    )
    key_tok = flat_dot(tokens, key_full).astype(jnp.bfloat16).reshape(tokens.shape)
    value_tok = (
        (flat_dot(tokens, value_full) + value_bias).astype(jnp.bfloat16).reshape(tokens.shape)
    )
    query_heads, key_heads, value_heads = (
        lax.all_to_all(query_tok, "head", split_axis=2, concat_axis=1, tiled=True),
        lax.all_to_all(key_tok, "head", split_axis=2, concat_axis=1, tiled=True),
        lax.all_to_all(value_tok, "head", split_axis=2, concat_axis=1, tiled=True),
    )
    rows_here = query_heads.shape[1]
    width_heads = query_heads.shape[2]
    heads_here = width_heads // HD
    start_state = (
        jnp.full((seq_count, heads_here, rows_here), -1e30, jnp.float32),
        jnp.zeros((seq_count, heads_here, rows_here), jnp.float32),
        jnp.zeros((seq_count, heads_here, rows_here, HD), jnp.float32),
    )
    running_max, running_sum, weighted = forward_step(
        start_state,
        (
            lax.all_gather(key_heads, "blk", axis=1, tiled=True),
            lax.all_gather(value_heads, "blk", axis=1, tiled=True),
            lax.all_gather(segment_ids, "blk", axis=1, tiled=True),
        ),
        (query_heads, segment_ids),
    )
    floored = jnp.maximum(running_sum, 1.0)
    ctx_heads = heads_to_rows(weighted / floored[..., None])
    log_sums = (running_max + jnp.log(floored)).transpose(0, 2, 1)
    ctx_tok = lax.all_to_all(
        ctx_heads.astype(jnp.bfloat16), "head", split_axis=1, concat_axis=2, tiled=True
    )
    first_sum = tokens.astype(jnp.float32) + (flat_dot(ctx_tok, out_full) + out_bias).reshape(
        tokens.shape
    )
    first_norm = layer_norm(first_sum, gain_one, shift_one)
    first_low = first_norm.astype(jnp.bfloat16)
    inner_rows = flat_dot(first_low, in_full) + in_bias
    hidden_low = jax.nn.gelu(inner_rows, approximate=False).astype(jnp.bfloat16)
    second_sum = first_norm + (flat_dot(hidden_low, back_full) + back_bias).reshape(tokens.shape)
    output_now, second_pull = jax.vjp(layer_norm, second_sum, gain_two, shift_two)
    grad_second, grad_gain_two, grad_shift_two = second_pull(cotangent.astype(jnp.float32))
    grad_branch = grad_second.astype(jnp.bfloat16)
    grad_back_bias = jnp.sum(grad_branch.astype(jnp.float32), (0, 1))
    grad_back = inner_dot(hidden_low, grad_branch)
    grad_hidden = flat_dot(grad_branch, back_full.T)
    unused_value, gelu_pull = jax.vjp(partial(jax.nn.gelu, approximate=False), inner_rows)
    grad_inner = gelu_pull(grad_hidden)[0].astype(jnp.bfloat16)
    grad_in_bias = jnp.sum(grad_inner.astype(jnp.float32), 0)
    grad_in = inner_dot(first_low, grad_inner)
    grad_first_norm = grad_second + flat_dot(grad_inner, in_full.T).reshape(tokens.shape)
    unused_norm, first_pull = jax.vjp(layer_norm, first_sum, gain_one, shift_one)
    grad_first, grad_gain_one, grad_shift_one = first_pull(grad_first_norm)
    grad_attn = grad_first.astype(jnp.bfloat16)
    grad_out_bias = jnp.sum(grad_attn.astype(jnp.float32), (0, 1))
    grad_out = inner_dot(ctx_tok, grad_attn)
    grad_ctx_tok = flat_dot(grad_attn, out_full.T).astype(jnp.bfloat16).reshape(tokens.shape)
    grad_ctx = lax.all_to_all(grad_ctx_tok, "head", split_axis=2, concat_axis=1, tiled=True)
    deltas = jnp.sum(head_view(grad_ctx).astype(jnp.float32) * head_view(ctx_heads), -1)
    key_block = lax.all_gather(key_heads, "blk", axis=1, tiled=True)
    value_block = lax.all_gather(value_heads, "blk", axis=1, tiled=True)
    key_ids = lax.all_gather(segment_ids, "blk", axis=1, tiled=True)
    weights_now = probabilities(query_heads, key_block, segment_ids, key_ids, log_sums)
    dscores = score_grads(weights_now, grad_ctx, value_block, deltas)
    grad_query_heads = jnp.einsum(
        "ghqk,gkhd->ghqd", dscores, head_view(key_block), preferred_element_type=jnp.float32
    )
    key_part = jnp.einsum(
        "ghqk,gqhd->gkhd", dscores, head_view(query_heads), preferred_element_type=jnp.float32
    )
    value_part = jnp.einsum(
        "ghqk,gqhd->gkhd",
        weights_now.astype(jnp.bfloat16),
        head_view(grad_ctx),
        preferred_element_type=jnp.float32,
    )
    both_parts = jnp.concatenate(
        [
            key_part.reshape(key_part.shape[0], key_part.shape[1], -1),
            value_part.reshape(value_part.shape[0], value_part.shape[1], -1),
        ],
        2,
    )
    grad_query_heads, pair_grads = (grad_query_heads, both_parts)
    pair_home = lax.psum_scatter(
        pair_grads.astype(jnp.bfloat16), "blk", scatter_dimension=1, tiled=True
    ).astype(jnp.float32)
    grad_key_heads = pair_home[:, :, :width_heads].astype(jnp.bfloat16)
    grad_value_heads = pair_home[:, :, width_heads:].astype(jnp.bfloat16)
    grad_query_rows = heads_to_rows(grad_query_heads).astype(jnp.bfloat16)
    grad_query_tok, grad_key_tok, grad_value_tok = (
        lax.all_to_all(grad_query_rows, "head", split_axis=1, concat_axis=2, tiled=True),
        lax.all_to_all(grad_key_heads, "head", split_axis=1, concat_axis=2, tiled=True),
        lax.all_to_all(grad_value_heads, "head", split_axis=1, concat_axis=2, tiled=True),
    )
    grad_query_tok = grad_query_tok * 0.125
    grad_inputs = grad_first + (
        flat_dot(grad_query_tok, query_full.T)
        + flat_dot(grad_key_tok, key_full.T)
        + flat_dot(grad_value_tok, value_full.T)
    ).reshape(tokens.shape)
    (
        shard_wq,
        shard_wk,
        shard_wv,
        shard_wo,
        shard_wi,
        shard_wb,
        shard_bq,
        shard_bv,
        shard_bo,
        shard_bi,
        shard_bb,
        shard_g1,
        shard_s1,
        shard_g2,
        shard_s2,
    ) = (
        lax.psum_scatter(
            inner_dot(tokens, grad_query_tok), ("blk", "head"), scatter_dimension=0, tiled=True
        ),
        lax.psum_scatter(
            inner_dot(tokens, grad_key_tok), ("blk", "head"), scatter_dimension=0, tiled=True
        ),
        lax.psum_scatter(
            inner_dot(tokens, grad_value_tok), ("blk", "head"), scatter_dimension=0, tiled=True
        ),
        lax.psum_scatter(grad_out, ("blk", "head"), scatter_dimension=0, tiled=True),
        lax.psum_scatter(grad_in, ("blk", "head"), scatter_dimension=0, tiled=True),
        lax.psum_scatter(grad_back, ("blk", "head"), scatter_dimension=0, tiled=True),
        lax.psum_scatter(
            jnp.sum(grad_query_tok.astype(jnp.float32), (0, 1)),
            ("blk", "head"),
            scatter_dimension=0,
            tiled=True,
        ),
        lax.psum_scatter(
            jnp.sum(grad_value_tok.astype(jnp.float32), (0, 1)),
            ("blk", "head"),
            scatter_dimension=0,
            tiled=True,
        ),
        lax.psum_scatter(grad_out_bias, ("blk", "head"), scatter_dimension=0, tiled=True),
        lax.psum_scatter(grad_in_bias, ("blk", "head"), scatter_dimension=0, tiled=True),
        lax.psum_scatter(grad_back_bias, ("blk", "head"), scatter_dimension=0, tiled=True),
        lax.psum_scatter(grad_gain_one, ("blk", "head"), scatter_dimension=0, tiled=True),
        lax.psum_scatter(grad_shift_one, ("blk", "head"), scatter_dimension=0, tiled=True),
        lax.psum_scatter(grad_gain_two, ("blk", "head"), scatter_dimension=0, tiled=True),
        lax.psum_scatter(grad_shift_two, ("blk", "head"), scatter_dimension=0, tiled=True),
    )
    (
        total_wq,
        total_wk,
        total_wv,
        total_wo,
        total_wi,
        total_wb,
        total_bq,
        total_bv,
        total_bo,
        total_bi,
        total_bb,
        total_g1,
        total_s1,
        total_g2,
        total_s2,
    ) = (
        lax.psum(shard_wq.astype(jnp.bfloat16), "dp").astype(jnp.float32),
        lax.psum(shard_wk.astype(jnp.bfloat16), "dp").astype(jnp.float32),
        lax.psum(shard_wv.astype(jnp.bfloat16), "dp").astype(jnp.float32),
        lax.psum(shard_wo.astype(jnp.bfloat16), "dp").astype(jnp.float32),
        lax.psum(shard_wi.astype(jnp.bfloat16), "dp").astype(jnp.float32),
        lax.psum(shard_wb.astype(jnp.bfloat16), "dp").astype(jnp.float32),
        lax.psum(shard_bq.astype(jnp.bfloat16), "dp").astype(jnp.float32),
        lax.psum(shard_bv.astype(jnp.bfloat16), "dp").astype(jnp.float32),
        lax.psum(shard_bo.astype(jnp.bfloat16), "dp").astype(jnp.float32),
        lax.psum(shard_bi.astype(jnp.bfloat16), "dp").astype(jnp.float32),
        lax.psum(shard_bb.astype(jnp.bfloat16), "dp").astype(jnp.float32),
        lax.psum(shard_g1.astype(jnp.bfloat16), "dp").astype(jnp.float32),
        lax.psum(shard_s1.astype(jnp.bfloat16), "dp").astype(jnp.float32),
        lax.psum(shard_g2.astype(jnp.bfloat16), "dp").astype(jnp.float32),
        lax.psum(shard_s2.astype(jnp.bfloat16), "dp").astype(jnp.float32),
    )
    return (
        output_now.astype(jnp.bfloat16),
        grad_inputs,
        total_wq,
        total_wk,
        total_wv,
        total_wo,
        total_wi,
        total_wb,
        total_bq,
        total_bv,
        total_bo,
        total_bi,
        total_bb,
        total_g1,
        total_s1,
        total_g2,
        total_s2,
    )


def solution(mesh):
    in_specs = (
        P("dp", ("blk", "head"), None),
        P("dp", "blk"),
        P("dp", ("blk", "head"), None),
        P(("blk", "head"), None),
        P(("blk", "head"), None),
        P(("blk", "head"), None),
        P(("blk", "head"), None),
        P(("blk", "head"), None),
        P(("blk", "head"), None),
        P(("blk", "head")),
        P(("blk", "head")),
        P(("blk", "head")),
        P(("blk", "head")),
        P(("blk", "head")),
        P(("blk", "head")),
        P(("blk", "head")),
        P(("blk", "head")),
        P(("blk", "head")),
    )
    out_specs = (
        P("dp", ("blk", "head"), None),
        P("dp", ("blk", "head"), None),
        P(("blk", "head"), None),
        P(("blk", "head"), None),
        P(("blk", "head"), None),
        P(("blk", "head"), None),
        P(("blk", "head"), None),
        P(("blk", "head"), None),
        P(("blk", "head")),
        P(("blk", "head")),
        P(("blk", "head")),
        P(("blk", "head")),
        P(("blk", "head")),
        P(("blk", "head")),
        P(("blk", "head")),
        P(("blk", "head")),
        P(("blk", "head")),
    )
    return jax.shard_map(
        per_device, mesh=mesh, in_specs=in_specs, out_specs=out_specs, check_vma=False
    )
```

profile of v0, /device:TPU:0, one launch (start us, length us, event | category | flops | bytes accessed | tf_op | source)
XLA Modules:
  0.0 1062.4 jit_solution(12459817978749178414)
XLA Ops:
  9.5 31.1 %all-gather.20.cloned.1.call-done = bf16[1024,1024]{1,0:T(8,128)(2,1)} async-done(((bf16[128,1024]{1,0:T(8,128)(2,1)}), bf16[1024,1024]{1,0:T(8,128)(2,1)}) %all-gather.20.cloned.1.call-update) | async-done | bytes 2097168 | tf_op jit(solution)/shard_map/all_gather | solution.py:132
  43.6 2.3 reduce.20
  45.9 10.5 all_to_all.120
  57.7 11.8 %all-gather.1 = bf16[8,1,128]{2,1,0:T(2,128)(2,1)S(1)} all-gather(bf16[1,1,128]{2,1,0:T(2,128)(2,1)S(1)} %bitcast.268), channel_id=1, replica_groups=mesh['dp'=4,'blk'=4,'head'=2] {'blk','head'}, dimensions={0}, use_global_device_ids=true | all-gather | bytes 2304 | tf_op jit(solution)/shard_map/all_gather | solution.py:138
  69.5 2.4 all-gather.24.cloned.1.call-done
  74.3 2.2 reduce.21
  76.6 9.9 all_to_all.121
  89.8 11.8 %all-gather = bf16[8,1,128]{2,1,0:T(2,128)(2,1)S(1)} all-gather(bf16[1,1,128]{2,1,0:T(2,128)(2,1)S(1)} %bitcast.269), channel_id=1, replica_groups=mesh['dp'=4,'blk'=4,'head'=2] {'blk','head'}, dimensions={0}, use_global_device_ids=true | all-gather | bytes 2304 | tf_op jit(solution)/shard_map/all_gather | solution.py:137
  101.6 5.1 all_gather.59
  109.1 2.2 reduce.19
  112.1 3.7 all-to-all-start
  116.0 5.7 all-to-all-done
  124.0 16.1 %all-gather.26.cloned.1.call-done = bf16[1,1024,512]{2,1,0:T(8,128)(2,1)} async-done(((bf16[1,256,512]{2,1,0:T(8,128)(2,1)}), bf16[1,1024,512]{2,1,0:T(8,128)(2,1)}) %all-gather.26.cloned.1.call-update) | async-done | bytes 1048592 | tf_op jit(solution)/shard_map/all_gather | solution.py:183
  143.0 2.4 fusion
  146.2 3.1 fusion.70
  150.8 2.2 reduce.22
  153.9 3.4 all-to-all-start.3
  157.4 13.5 %all-gather.6 = bf16[8,1,128]{2,1,0:T(2,128)(2,1)S(1)} all-gather(bf16[1,1,128]{2,1,0:T(2,128)(2,1)S(1)} %bitcast.270), channel_id=1, replica_groups=mesh['dp'=4,'blk'=4,'head'=2] {'blk','head'}, dimensions={0}, use_global_device_ids=true | all-gather | bytes 2304 | tf_op jit(solution)/shard_map/all_gather | solution.py:141
  170.9 15.2 %all-gather.5 = bf16[8,1,512]{2,1,0:T(2,128)(2,1)S(1)} all-gather(bf16[1,1,512]{2,1,0:T(2,128)(2,1)S(1)} %reshape.540), channel_id=1, replica_groups=mesh['dp'=4,'blk'=4,'head'=2] {'blk','head'}, dimensions={0}, use_global_device_ids=true | all-gather | bytes 9216 | tf_op jit(solution)/shard_map/all_gather | solution.py:140
  186.1 12.7 %all-gather.2 = bf16[8,1,128]{2,1,0:T(2,128)(2,1)S(1)} all-gather(bf16[1,1,128]{2,1,0:T(2,128)(2,1)S(1)} %bitcast.271), channel_id=1, replica_groups=mesh['dp'=4,'blk'=4,'head'=2] {'blk','head'}, dimensions={0}, use_global_device_ids=true | all-gather | bytes 2304 | tf_op jit(solution)/shard_map/all_gather | solution.py:139
  198.7 11.8 %all-gather.4 = bf16[8,1,128]{2,1,0:T(2,128)(2,1)S(1)} all-gather(bf16[1,1,128]{2,1,0:T(2,128)(2,1)S(1)} %bitcast.272), channel_id=1, replica_groups=mesh['dp'=4,'blk'=4,'head'=2] {'blk','head'}, dimensions={0}, use_global_device_ids=true | all-gather | bytes 2304 | tf_op jit(solution)/shard_map/all_gather | solution.py:143
  210.5 12.3 %all-gather.3 = bf16[8,1,128]{2,1,0:T(2,128)(2,1)S(1)} all-gather(bf16[1,1,128]{2,1,0:T(2,128)(2,1)S(1)} %bitcast.273), channel_id=1, replica_groups=mesh['dp'=4,'blk'=4,'head'=2] {'blk','head'}, dimensions={0}, use_global_device_ids=true | all-gather | bytes 2304 | tf_op jit(solution)/shard_map/all_gather | solution.py:142
  222.8 10.9 %all-gather.7 = bf16[8,1,128]{2,1,0:T(2,128)(2,1)S(1)} all-gather(bf16[1,1,128]{2,1,0:T(2,128)(2,1)S(1)} %bitcast.274), channel_id=1, replica_groups=mesh['dp'=4,'blk'=4,'head'=2] {'blk','head'}, dimensions={0}, use_global_device_ids=true | all-gather | bytes 2304 | tf_op jit(solution)/shard_map/all_gather | solution.py:144
  233.8 12.3 %all-gather.8 = bf16[8,1,128]{2,1,0:T(2,128)(2,1)S(1)} all-gather(bf16[1,1,128]{2,1,0:T(2,128)(2,1)S(1)} %bitcast.275), channel_id=1, replica_groups=mesh['dp'=4,'blk'=4,'head'=2] {'blk','head'}, dimensions={0}, use_global_device_ids=true | all-gather | bytes 2304 | tf_op jit(solution)/shard_map/all_gather | solution.py:145
  249.0 6.0 convolution_add_fusion
  255.1 27.4 %all-gather.32.cloned.1.call-done = bf16[4096,1024]{1,0:T(8,128)(2,1)} async-done(((bf16[512,1024]{1,0:T(8,128)(2,1)}), bf16[4096,1024]{1,0:T(8,128)(2,1)}) %all-gather.32.cloned.1.call-update) | async-done | bytes 8388624 | tf_op jit(solution)/shard_map/all_gather | solution.py:136
  282.5 9.7 fusion.72
  293.9 7.5 convert_reduce_fusion
  301.5 3.1 multiply_reduce_fusion
  309.6 3.8 reduce.23
  315.2 10.2 all_to_all.122
  330.4 2.3 reshape.529
  335.8 6.8 fusion.15
  342.6 7.0 multiply_convert_fusion
  349.5 6.0 copy.126
  355.5 4.0 convolution_convert_fusion
  359.5 5.9 copy.125
  365.5 8.6 pad_maximum_fusion
  374.1 2.6 fusion.44
  377.0 3.6 convolution_convert_fusion.3
  383.5 7.6 all_to_all.123
  391.6 2.7 convolution_bitcast_fusion.2
  396.2 63.5 %all-reduce.16.cloned.1.call-done = bf16[1,1024,1024]{2,0,1:T(2,128)(2,1)} async-done(((bf16[1,1024,1024]{2,0,1:T(2,128)(2,1)}), bf16[1,1024,1024]{2,0,1:T(2,128)(2,1)}) %all-reduce.16.cloned.1.call-update) | async-done | bytes 2097168
  459.7 2.8 constant_dynamic-slice_fusion.1
  464.9 7.7 all_to_all.124
  473.1 2.6 convolution_bitcast_fusion.1
  475.8 2.2 reduce.26
  478.2 7.6 all_to_all.125
  486.3 2.6 convolution_bitcast_fusion
  490.1 8.2 fusion.65
  499.9 10.7 %fusion.47 = f32[4096,1024]{1,0:T(8,128)} fusion(bf16[1,128,1024]{2,1,0:T(8,128)(2,1)} %copy-done.19, f32[128,4096]{1,0:T(8,128)S(1)} %copy-done.11), kind=kOutput, calls=%fused_computation.90 | convolution fusion | flops 1107820544 | bytes 19136512 | tf_op jit(solution)/shard_map/ra,rb->ab/dot_general | solution.py:18
  510.6 4.2 reduce-scatter.13.cloned.1.call-done
  516.6 52.9 %reduce-scatter.7.cloned.1.call-done = f32[128,1024]{0,1:T(8,128)} async-done(((f32[1024,1024]{0,1:T(8,128)}), f32[128,1024]{0,1:T(8,128)}) %reduce-scatter.7.cloned.1.call-update) | async-done | bytes 524304 | tf_op jit(solution)/shard_map/reduce_scatter | solution.py:280
  571.3 53.2 %reduce-scatter.9.cloned.1.call-done = f32[128,1024]{0,1:T(8,128)} async-done(((f32[1024,1024]{0,1:T(8,128)}), f32[128,1024]{0,1:T(8,128)}) %reduce-scatter.9.cloned.1.call-update) | async-done | bytes 524304 | tf_op jit(solution)/shard_map/reduce_scatter | solution.py:283
  626.2 52.9 %reduce-scatter.11.cloned.1.call-done = f32[128,1024]{0,1:T(8,128)} async-done(((f32[1024,1024]{0,1:T(8,128)}), f32[128,1024]{0,1:T(8,128)}) %reduce-scatter.11.cloned.1.call-update) | async-done | bytes 524304 | tf_op jit(solution)/shard_map/reduce_scatter | solution.py:286
  680.9 118.1 %reduce-scatter.15.cloned.1.call-done = f32[128,4096]{1,0:T(8,128)} async-done(((f32[1024,4096]{1,0:T(8,128)}), f32[128,4096]{1,0:T(8,128)}) %reduce-scatter.15.cloned.1.call-update) | async-done | bytes 2097168 | tf_op jit(solution)/shard_map/reduce_scatter | solution.py:290
  799.0 2.7 convert_element_type.286
  801.7 117.1 %reduce-scatter.17.cloned.1.call-done = f32[512,1024]{1,0:T(8,128)} async-done(((f32[4096,1024]{1,0:T(8,128)}), f32[512,1024]{1,0:T(8,128)}) %reduce-scatter.17.cloned.1.call-update) | async-done | bytes 2097168 | tf_op jit(solution)/shard_map/reduce_scatter | solution.py:291
  918.8 2.7 convert_element_type.288
  924.2 2.6 fusion.73
  926.9 25.8 %all-reduce.10 = (bf16[1024]{0:T(1024)(128)(2,1)S(1)}, bf16[1024]{0:T(1024)(128)(2,1)S(1)}, bf16[1024]{0:T(1024)(128)(2,1)S(1)}, bf16[4096]{0:T(1024)(128)(2,1)S...) all-reduce(f32[1024]{0:T(1024)S(1)} %bitcast.263, ...), channel_id=9, replica_groups=mesh['dp'=4,'blk'=4,'head'=2] {'blk','head'}, use_global_device_ids=true, to_apply=%region_25.26.clone | all-reduce | flops 12288 | bytes 73728
  953.3 12.8 %all-reduce.11 = (bf16[128]{0:T(256)(128)(2,1)S(1)}, bf16[128]{0:T(256)(128)(2,1)S(1)}, bf16[128]{0:T(256)(128)(2,1)S(1)}, bf16[512]{0:T(512)(128)(2,1)S(1)}, bf...) all-reduce(bf16[128]{0:T(256)(128)(2,1)S(1)} %dynamic-slice.41, ...), channel_id=1, replica_groups=mesh['dp'=4,'blk'=4,'head'=2] {'dp'}, use_global_device_ids=true, to_apply=%region_26.27 | all-reduce | flops 1536 | bytes 6144 | tf_op jit(solution)/shard_map/psum | solution.py:335
  970.8 2.5 convolution_add_fusion.2
  975.0 70.7 %all-reduce.18.cloned.1.call-done = (bf16[128,1024]{0,1:T(8,128)(2,1)}, bf16[128,1024]{0,1:T(8,128)(2,1)}, bf16[128,1024]{0,1:T(8,128)(2,1)}, bf16[128,1024]{1,0...) async-done(((bf16[128,1024]{0,1:T(8,128)(2,1)}, bf16[128,1024]{0,1:T(8,128)(2,1)}, bf16[128,1024]{0,1:T(8,128)(2,1)}, bf16[128,1024]{1,0:T(8,128)(2,1)}, ...) | async-done | bytes 3145744 | tf_op jit(solution)/shard_map/psum | solution.py:329
  (228 shorter events, 80.0 us)
Async XLA Ops:
  7.2 33.3 %all-gather.20.cloned.1.call-start = ((), (), s32[]{:S(2)}) async-start(), calls=%async_computation.15 | async-start | bytes 2359296 | tf_op jit(solution)/shard_map/all_gather | solution.py:132
  7.9 63.9 %all-gather.24.cloned.1.call-start = ((), (), s32[]{:S(2)}) async-start(), calls=%async_computation.17 | async-start | bytes 2359296 | tf_op jit(solution)/shard_map/all_gather | solution.py:133
  8.7 98.0 %all-gather.18.cloned.1.call-start = ((), (), s32[]{:S(2)}) async-start(), calls=%async_computation.14 | async-start | bytes 2359296 | tf_op jit(solution)/shard_map/all_gather | solution.py:131
  9.4 113.0 %all-gather.22.cloned.1.call-start = ((), (), s32[]{:S(2)}) async-start(), calls=%async_computation.16 | async-start | bytes 1310720 | tf_op jit(solution)/shard_map/all_gather | solution.py:182
  43.6 14.1 %copy-start.22 = (bf16[128]{0:T(256)(128)(2,1)S(1)}, bf16[128]{0:T(256)(128)(2,1)}, u32[]{:S(2)}) copy-start(bf16[128]{0:T(256)(128)(2,1)} %param.28) | copy-start | bytes 772
  43.6 28.3 %copy-start.1 = (bf16[1,128,1024]{2,1,0:T(8,128)(2,1)S(1)}, bf16[1,128,1024]{2,1,0:T(8,128)(2,1)}, u32[]{:S(2)}) copy-start(bf16[1,128,1024]{2,1,0:T(8,128)(2,1)} %param.18) | copy-start | bytes 786436
  57.7 82.4 %all-gather.26.cloned.1.call-start = ((), (), s32[]{:S(2)}) async-start(), calls=%async_computation.18 | async-start | bytes 1310720 | tf_op jit(solution)/shard_map/all_gather | solution.py:183
  86.8 3.0 copy-start.23
  86.8 14.8 %copy-start.20 = (s32[1,256]{1,0:T(1,128)S(1)}, s32[1,256]{1,0:T(1,128)}, u32[]{:S(2)}) copy-start(s32[1,256]{1,0:T(1,128)} %param.19) | copy-start | bytes 3076
  87.7 158.9 %all-gather.28.cloned.1.call-start = ((), (), s32[]{:S(2)}) async-start(), calls=%async_computation.19 | async-start | bytes 2359296 | tf_op jit(solution)/shard_map/all_gather | solution.py:134
  88.3 160.7 %all-gather.30.cloned.1.call-start = ((), (), s32[]{:S(2)}) async-start(), calls=%async_computation.20 | async-start | bytes 9437184 | tf_op jit(solution)/shard_map/all_gather | solution.py:135
  89.1 193.4 %all-gather.32.cloned.1.call-start = ((), (), s32[]{:S(2)}) async-start(), calls=%async_computation.21 | async-start | bytes 9437184 | tf_op jit(solution)/shard_map/all_gather | solution.py:136
  112.1 9.6 all-to-all-start
  141.5 3.9 copy-start.14
  143.0 3.2 copy-start
  149.3 8.1 copy-start.24
  149.3 21.6 %copy-start.21 = (bf16[512]{0:T(512)(128)(2,1)S(1)}, bf16[512]{0:T(512)(128)(2,1)}, u32[]{:S(2)}) copy-start(bf16[512]{0:T(512)(128)(2,1)} %param.30) | copy-start | bytes 3076
  149.3 36.7 %copy-start.25 = (bf16[128]{0:T(256)(128)(2,1)S(1)}, bf16[128]{0:T(256)(128)(2,1)}, u32[]{:S(2)}) copy-start(bf16[128]{0:T(256)(128)(2,1)} %param.29) | copy-start | bytes 772
  149.3 49.4 %copy-start.26 = (bf16[128]{0:T(256)(128)(2,1)S(1)}, bf16[128]{0:T(256)(128)(2,1)}, u32[]{:S(2)}) copy-start(bf16[128]{0:T(256)(128)(2,1)} %param.33) | copy-start | bytes 772
  149.3 61.2 %copy-start.27 = (bf16[128]{0:T(256)(128)(2,1)S(1)}, bf16[128]{0:T(256)(128)(2,1)}, u32[]{:S(2)}) copy-start(bf16[128]{0:T(256)(128)(2,1)} %param.32) | copy-start | bytes 772
  149.3 73.5 %copy-start.28 = (bf16[128]{0:T(256)(128)(2,1)S(1)}, bf16[128]{0:T(256)(128)(2,1)}, u32[]{:S(2)}) copy-start(bf16[128]{0:T(256)(128)(2,1)} %param.34) | copy-start | bytes 772
  149.3 84.4 %copy-start.29 = (bf16[128]{0:T(256)(128)(2,1)S(1)}, bf16[128]{0:T(256)(128)(2,1)}, u32[]{:S(2)}) copy-start(bf16[128]{0:T(256)(128)(2,1)} %param.35) | copy-start | bytes 772
  153.9 92.2 %all-to-all-start.3 = ((bf16[2,2,32768]{2,1,0:T(2,128)(2,1)}), bf16[2,2,32768]{2,1,0:T(2,128)(2,1)S(1)}, u32[]{:S(2)}, u32[]{:S(2)}) async-start(bf16[2,2,32768]{2,1,0:T(2,128)(2,1)} %reshape.573), calls=%async_computation.3 | async-start | bytes 524288 | tf_op jit(solution)/shard_map/all_to_all | solution.py:191
  157.3 302.4 %all-reduce.16.cloned.1.call-start = ((), (), s32[]{:S(2)}) async-start(), calls=%async_computation.28 | async-start | bytes 8388608
  282.5 11.3 %slice-start.2 = ((s8[8388608]{0:T(1024)(128)(4,1)}), s8[4194304]{0:T(1024)(128)(4,1)S(1)}, s32[]{:S(2)}) async-start(s8[8388608]{0:T(1024)(128)(4,1)} %bitcast.276), calls=%async_computation.32 | async-start | bytes 8388608
  282.5 9.9 copy-start.16
  282.5 11.4 %slice-start.3 = ((s8[8388608]{0:T(1024)(128)(4,1)}), s8[4194304]{0:T(1024)(128)(4,1)S(1)}, s32[]{:S(2)}) async-start(s8[8388608]{0:T(1024)(128)(4,1)} %bitcast.276), calls=%async_computation.33 | async-start | bytes 8388608
  292.2 1.7 copy-start.10
  292.7 8.7 slice-start
  293.8 7.6 copy-start.19
  293.9 7.6 slice-start.1
  301.4 3.1 copy-start.5
  304.5 1.6 copy-start.4
  335.7 6.8 copy-start.15
  335.8 6.8 copy-start.18
  374.1 140.7 %reduce-scatter.13.cloned.1.call-start = ((), (), s32[]{:S(2)}) async-start(), calls=%async_computation.25 | async-start | bytes 4718592 | tf_op jit(solution)/shard_map/reduce_scatter | solution.py:289
  376.8 192.7 %reduce-scatter.7.cloned.1.call-start = ((), (), s32[]{:S(2)}) async-start(), calls=%async_computation.22 | async-start | bytes 4718592 | tf_op jit(solution)/shard_map/reduce_scatter | solution.py:280
  391.5 2.8 copy-start.9
  394.3 0.7 copy-start.31
  394.3 230.1 %reduce-scatter.9.cloned.1.call-start = ((), (), s32[]{:S(2)}) async-start(), calls=%async_computation.23 | async-start | bytes 4718592 | tf_op jit(solution)/shard_map/reduce_scatter | solution.py:283
  473.1 2.6 copy-start.7
  475.8 203.4 %reduce-scatter.11.cloned.1.call-start = ((), (), s32[]{:S(2)}) async-start(), calls=%async_computation.24 | async-start | bytes 4718592 | tf_op jit(solution)/shard_map/reduce_scatter | solution.py:286
  488.9 1.2 copy-start.6
  488.9 310.1 %reduce-scatter.15.cloned.1.call-start = ((), (), s32[]{:S(2)}) async-start(), calls=%async_computation.26 | async-start | bytes 18874368 | tf_op jit(solution)/shard_map/reduce_scatter | solution.py:290
  498.3 1.6 copy-start.11
  498.3 420.5 %reduce-scatter.17.cloned.1.call-start = ((), (), s32[]{:S(2)}) async-start(), calls=%async_computation.27 | async-start | bytes 18874368 | tf_op jit(solution)/shard_map/reduce_scatter | solution.py:291
  510.6 535.1 %all-reduce.18.cloned.1.call-start = ((), (), s32[]{:S(2)}) async-start(), calls=%async_computation.29 | async-start | bytes 6291456 | tf_op jit(solution)/shard_map/psum | solution.py:329
  921.6 0.7 copy-start.30
  921.6 2.6 copy-start.3
  924.1 46.7 %copy-start.8 = (bf16[1,128,2,512]{1,3,2,0:T(8,128)(2,1)S(1)}, bf16[1,128,2,512]{1,3,2,0:T(8,128)(2,1)}, u32[]{:S(2)}) copy-start(bf16[1,128,2,512]{1,3,2,0:T(8,128)(2,1)} %copy-done.7) | copy-start | bytes 786436
  926.8 46.6 %copy-start.2 = (bf16[1024,1024]{1,0:T(8,128)(2,1)S(1)}, bf16[1024,1024]{1,0:T(8,128)(2,1)}, u32[]{:S(2)}) copy-start(bf16[1024,1024]{1,0:T(8,128)(2,1)} %all-gather.24.cloned.1.call-done) | copy-start | bytes 6291460
  1045.7 5.8 copy-start.17
  1045.7 6.6 copy-start.13
  1051.5 2.4 copy-start.12
Sparse Core Ops, SparseCore 0:
  9.9 30.5 all-gather.19
  42.4 29.4 all-gather.23
  73.8 28.7 all-gather.17
  104.5 16.7 all-gather.21
  123.3 16.7 all-gather.25
  141.8 28.5 all-gather.27
  172.3 53.8 all-gather.29
  228.0 54.3 all-gather.31
  374.2 85.4 all-reduce.15
  463.3 51.4 reduce-scatter.12
  518.2 51.2 reduce-scatter.6
  573.1 51.3 reduce-scatter.8
  627.8 51.2 reduce-scatter.10
  683.0 115.9 reduce-scatter.14
  802.8 115.9 reduce-scatter.16
  922.3 123.3 all-reduce.17
where the time goes:
time: 1070 us; the launch traced here: 1060 us
  waiting for transfers between devices  619 us (58%)
  blocking collectives  209 us (20%)
  matrix products  98.4 us (9%)
  other arithmetic  55.4 us (5%)
  local copies, waits for them, and re-layouts  54.5 us (5%)
  between operations  17.2 us (2%)
    reduce_scatter x1, waiting for transfers between devices, per_device(): lax.psum_scatter(grad_in, ('blk', 'head'), scatter_dimension=0, tiled=True)  118 us
    reduce_scatter x1, waiting for transfers between devices, per_device(): lax.psum_scatter(grad_back, ('blk', 'head'), scatter_dimension=0, tiled=T...  117 us
    psum x1, waiting for transfers between devices, per_device(): lax.psum(shard_wq.astype(jnp.bfloat16), 'dp').astype(jnp.float32)  70.7 us
    unnamed x17, waiting for transfers between devices  67.6 us
    reduce_scatter x1, waiting for transfers between devices, per_device(): lax.psum_scatter(inner_dot(tokens, grad_key_tok), ('blk', 'head'), scatte...  53.2 us
    reduce_scatter x1, waiting for transfers between devices, per_device(): lax.psum_scatter(inner_dot(tokens, grad_query_tok), ('blk', 'head'), scat...  52.9 us
    reduce_scatter x1, waiting for transfers between devices, per_device(): lax.psum_scatter(inner_dot(tokens, grad_value_tok), ('blk', 'head'), scat...  52.9 us
    dot_general x12, matrix products, flat_dot(): jnp.dot(left_side.reshape(-1, left_side.shape[-1]), right_side, preferred...  43 us
  transfers between devices with their start and end apart: 18, of which 13 were waited for; matrix products, arithmetic and copies ran while one was open for 10% of the time, Pallas kernels for 0%

commit v1 on v0

--- a/solution.py
+++ b/solution.py
@@ -6,6 +6,152 @@
 from jax.sharding import PartitionSpec as P
 
 HD = 64
+BF = jnp.bfloat16
+F32 = jnp.float32
+GROUP = ("blk", "head")
+
+
+def mm(a, b, dims):
+    return lax.dot_general(a, b, (dims, ((), ())), preferred_element_type=F32)
+
+
+NN = ((1,), (0,))
+NT = ((1,), (1,))
+TN = ((0,), (0,))
+
+
+def norm_parts(v):
+    c = v - jnp.mean(v, -1, keepdims=True)
+    r = lax.rsqrt(jnp.mean(c * c, -1, keepdims=True) + 1e-05)
+    return c * r, r
+
+
+def norm_back(e, n, r):
+    return r * (e - jnp.mean(e, -1, keepdims=True) - n * jnp.mean(e * n, -1, keepdims=True))
+
+
+def sharded_plan(
+    tokens, segment_ids, cotangent,
+    w_query, w_key, w_value, w_out, w_in, w_back,
+    bias_query, bias_value, bias_out, bias_in, bias_back,
+    first_gain, first_shift, second_gain, second_shift,
+):
+    tokens = tokens[0]
+    head_at = lax.axis_index("head")
+    rows_here = tokens.shape[0]
+    ids_own = lax.dynamic_slice(segment_ids[0], (head_at * rows_here,), (rows_here,))
+    vecs = jnp.stack([bias_out, bias_back, first_gain, first_shift, second_gain, second_shift])
+    gather = partial(lax.all_gather, axis_name=GROUP, axis=0, tiled=True)
+    to_cols = partial(lax.all_to_all, axis_name=GROUP, split_axis=1, concat_axis=0, tiled=True)
+    to_rows = partial(lax.all_to_all, axis_name=GROUP, split_axis=0, concat_axis=1, tiled=True)
+    scatter = partial(lax.psum_scatter, axis_name=GROUP, scatter_dimension=0, tiled=True)
+    ids = gather(ids_own)
+    vec_full = lax.all_gather(vecs, GROUP, axis=1, tiled=True).astype(F32)
+    b_out, b_back, g1, s1, g2, s2 = [vec_full[i][None] for i in range(6)]
+    tok_all = gather(tokens)
+    w_qkv = to_cols(jnp.concatenate([w.reshape(rows_here, -1, 128) for w in (w_query, w_key, w_value)], 2).reshape(rows_here, -1))
+    width = w_qkv.shape[1] // 3
+    wq, wk, wv = w_qkv[:, :width], w_qkv[:, width:2 * width], w_qkv[:, 2 * width:]
+    q = ((mm(tok_all, wq, NN) + bias_query.astype(F32)) * 0.125).astype(BF)
+    k = mm(tok_all, wk, NN).astype(BF)
+    v = (mm(tok_all, wv, NN) + bias_value.astype(F32)).astype(BF)
+    allowed = (ids[:, None] == ids[None, :]) & (ids[:, None] >= 0)
+    heads = width // HD
+    probs, ctx = [], []
+    for h in range(heads):
+        sl = slice(h * HD, (h + 1) * HD)
+        s = jnp.where(allowed, mm(k[:, sl], q[:, sl], NT), -1e30)
+        top = jnp.max(s, 0, keepdims=True)
+        ex = jnp.where(allowed, jnp.exp(s - top), 0.0)
+        total = jnp.maximum(jnp.sum(ex, 0, keepdims=True), 1.0)
+        p = ex * (1.0 / total)
+        probs.append(p)
+        ctx.append(mm(p.astype(BF), v[:, sl], TN))
+    ctx = jnp.concatenate(ctx, 1).astype(BF)
+    ctx_tok = to_rows(ctx)
+    out_full = gather(w_out)
+    h1 = tokens.astype(F32) + mm(ctx_tok, out_full, NN) + b_out
+    n1, r1 = norm_parts(h1)
+    y1 = n1 * g1 + s1
+    y1_all = gather(y1.astype(BF))
+    in_cols = to_cols(w_in)
+    z = mm(y1_all, in_cols, NN) + bias_in.astype(F32)
+    gelu = partial(jax.nn.gelu, approximate=False)
+    hidden, gelu_pull = jax.vjp(gelu, z)
+    hidden = hidden.astype(BF)
+    h2 = y1 + scatter(mm(hidden, w_back, NN).astype(BF)).astype(F32) + b_back
+    n2, r2 = norm_parts(h2)
+    output = (n2 * g2 + s2).astype(BF)
+    cot = cotangent[0].astype(F32)
+    dh2 = norm_back(cot * g2, n2, r2)
+    df_all = gather(dh2.astype(BF))
+    d_back = mm(hidden, df_all, TN)
+    dz = gelu_pull(mm(df_all, w_back, NT))[0].astype(BF)
+    d_in = to_rows(mm(y1_all, dz, TN).astype(BF))
+    dy1 = dh2 + scatter(mm(dz, in_cols, NT).astype(BF)).astype(F32)
+    dh1 = norm_back(dy1 * g1, n1, r1)
+    da = dh1.astype(BF)
+    da_all = gather(da)
+    d_out = mm(ctx, da_all, TN)
+    dc = to_cols(mm(da, out_full, NT).astype(BF))
+    dq, dk, dv = [], [], []
+    for h in range(heads):
+        sl = slice(h * HD, (h + 1) * HD)
+        p = probs[h]
+        dp = mm(v[:, sl], dc[:, sl], NT)
+        delta = jnp.sum(p * dp, 0, keepdims=True)
+        ds = (p * (dp - delta)).astype(BF)
+        dq.append(mm(ds, k[:, sl], TN).astype(BF) * 0.125)
+        dk.append(mm(ds, q[:, sl], NN).astype(BF))
+        dv.append(mm(p.astype(BF), dc[:, sl], NN).astype(BF))
+    dq, dk, dv = [jnp.concatenate(x, 1) for x in (dq, dk, dv)]
+    d_qkv = jnp.concatenate([dq, dk, dv], 1)
+    dw_qkv = to_rows(mm(tok_all, d_qkv, TN).astype(BF)).reshape(rows_here, -1, 3, width)
+    input_grad = dh1 + scatter(mm(d_qkv, w_qkv, NT).astype(BF)).astype(F32)
+    me = lax.axis_index("blk") * lax.axis_size("head") + head_at
+
+    def own_cols(x):
+        return lax.dynamic_slice(x, (0, me * rows_here), (x.shape[0], rows_here))
+
+    col = lambda x: jnp.sum(x.astype(F32), 0, keepdims=True)
+    small = jnp.concatenate(
+        [col(cot * n2), col(cot), col(dy1 * n1), col(dy1)], 0
+    )
+    small = lax.psum_scatter(small, GROUP, scatter_dimension=1, tiled=True)
+    small = jnp.concatenate(
+        [small, col(dq), col(dv), col(own_cols(da_all)), col(own_cols(df_all)), col(dz).reshape(-1, rows_here)], 0
+    )
+    small = jnp.concatenate([small, jnp.zeros((-small.shape[0] % 16, rows_here), F32)], 0)
+    wide = w_back.shape[1]
+    packed = jnp.concatenate(
+        [
+            dw_qkv.transpose(0, 2, 1, 3).reshape(-1, wide),
+            d_out.astype(BF),
+            d_in.reshape(-1, wide),
+            d_back.astype(BF),
+            small.astype(BF).reshape(-1, wide),
+        ],
+        0,
+    )
+    total = lax.psum(packed, "dp").astype(F32)
+    at = 3 * rows_here
+    sq = total[:at].reshape(rows_here, 3, wide)
+    t_out = total[at:at + rows_here]
+    at += rows_here
+    t_in = total[at:at + d_in.size // wide].reshape(d_in.shape)
+    at += d_in.size // wide
+    t_back = total[at:at + d_back.shape[0]]
+    at += d_back.shape[0]
+    sv = total[at:].reshape(small.shape)
+    return (
+        output[None], input_grad[None], sq[:, 0], sq[:, 1], sq[:, 2], t_out, t_in, t_back,
+        sv[4], sv[5], sv[6], sv[8:8 + w_back.shape[0] // rows_here].reshape(-1), sv[7], sv[2], sv[3], sv[0], sv[1],
+    )
+
+
+def pick_plan(mesh):
+    group = mesh.shape["blk"] * mesh.shape["head"]
+    return sharded_plan if group == 8 else general_plan
 
 
 def flat_dot(left_side, right_side):
@@ -91,7 +237,7 @@
     return array_in.transpose(0, 2, 1, 3).reshape(array_in.shape[0], array_in.shape[2], -1)
 
 
-def per_device(
+def general_plan(
     tokens,
     segment_ids,
     cotangent,
@@ -403,6 +549,7 @@
         P(("blk", "head")),
         P(("blk", "head")),
     )
+    plan = pick_plan(mesh)
     return jax.shard_map(
-        per_device, mesh=mesh, in_specs=in_specs, out_specs=out_specs, check_vma=False
-    )
+        plan, mesh=mesh, in_specs=in_specs, out_specs=out_specs, check_vma=False
+    )

time: 1070 us -> 536 us (0.50)
  waiting for transfers between devices: 619 us -> 337 us
  blocking collectives: 209 us -> 38 us
  matrix products: 98.4 us -> 58.6 us
  other arithmetic: 55.4 us -> 24.7 us
  local copies, waits for them, and re-layouts: 54.5 us -> 38 us
  starting transfers between devices: 8.21 us -> 23.9 us
    reduce_scatter x6 -> x3, waiting for transfers between devices: 398 us -> 120 us  [the longest x1 41.4 us: sharded_plan(): dy1 = dh2 + scatter(mm(dz, in_cols, NT).astype(BF)).astype(F32)]
    all_gather x10 -> x2, blocking collectives: 117 us -> 38 us  [the longest x1 20.9 us: sharded_plan(): ids = gather(ids_own)]
    unnamed x17 -> x11, waiting for transfers between devices: 67.6 us -> 2.21 us
    all_to_all x6 -> x0, blocking collectives: 53.5 us -> none  [the longest x1 10.5 us: per_device(): lax.all_to_all(key_tok, 'head', split_axis=2, concat_axis=1, tiled=True)]
    psum x1, waiting for transfers between devices: 70.7 us -> 122 us  [sharded_plan(): total = lax.psum(packed, 'dp').astype(F32)]
    all_to_all x2 -> x6, waiting for transfers between devices: 5.65 us -> 47.5 us  [the longest x1 17 us: sharded_plan(): in_cols = to_cols(w_in)]
    dot_general x24 -> x26, matrix products: 98.4 us -> 58.6 us  [mm(): return lax.dot_general(a, b, (dims, ((), ())), preferred_element_type=F32)]
    all_gather x8 -> x5, waiting for transfers between devices: 77 us -> 44.9 us  [the longest x1 28 us: sharded_plan(): df_all = gather(dh2.astype(BF))]
  transfers between devices with their start and end apart: 18 -> 16, of which waited for: 13 -> 12; matrix products, arithmetic and copies ran while one was open for 10% -> 12% of each run, Pallas kernels for 0% -> 0%
where the time goes in v1:
time: 536 us; the launch traced here: 535 us
  waiting for transfers between devices  337 us (63%)
  matrix products  58.6 us (11%)
  local copies, waits for them, and re-layouts  38 us (7%)
  blocking collectives  38 us (7%)
  other arithmetic  24.7 us (5%)
  starting transfers between devices  23.9 us (4%)
  between operations  14.9 us (3%)
    psum x1, waiting for transfers between devices, sharded_plan(): total = lax.psum(packed, 'dp').astype(F32)  122 us
    dot_general x26, matrix products, mm(): return lax.dot_general(a, b, (dims, ((), ())), preferred_element_type=F32)  58.6 us
    reduce_scatter x1, waiting for transfers between devices, sharded_plan(): dy1 = dh2 + scatter(mm(dz, in_cols, NT).astype(BF)).astype(F32)  41.4 us
    reduce_scatter x1, waiting for transfers between devices, sharded_plan(): h2 = y1 + scatter(mm(hidden, w_back, NN).astype(BF)).astype(F32) + b_back  41.3 us
    reduce_scatter x1, waiting for transfers between devices, sharded_plan(): input_grad = dh1 + scatter(mm(d_qkv, w_qkv, NT).astype(BF)).astype(F32)  37.5 us
    all_gather x1, waiting for transfers between devices, sharded_plan(): df_all = gather(dh2.astype(BF))  28 us
    all_gather x1, blocking collectives, sharded_plan(): ids = gather(ids_own)  20.9 us
    unnamed x101, local copies, waits for them, and re-layouts  19 us
  transfers between devices with their start and end apart: 16, of which 12 were waited for; matrix products, arithmetic and copies ran while one was open for 12% of the time, Pallas kernels for 0%

profile of v1, /device:TPU:0, one launch (start us, length us, event | category | flops | bytes accessed | tf_op | source)
XLA Modules:
  0.0 535.1 jit_solution(14101352038774511164)
XLA Ops:
  7.9 1.1 copy.56
  9.1 1.1 copy.57
  10.2 1.1 copy.58
  12.3 5.2 all-to-all-start
  18.3 20.9 %all-gather = s32[1,1024]{1,0:T(1,128)S(1)} all-gather(s32[1,128]{1,0:T(1,128)S(1)} %constant_dynamic-slice_fusion), channel_id=2, replica_groups=mesh['dp'=4,'blk'=4,'head'=2] {'blk','head'}, dimensions={1}, use_global_device_ids=true | all-gather | bytes 4608 | tf_op jit(solution)/shard_map/all_gather | solution.py:48
  39.6 6.3 %all-gather.16.cloned.1.call-done = bf16[1,1024,1024]{2,1,0:T(8,128)(2,1)} async-done(((bf16[1,128,1024]{2,1,0:T(8,128)(2,1)}), bf16[1,1024,1024]{2,1,0:T(8,128)(2,1)}) %all-gather.16.cloned.1.call-update) | async-done | bytes 2097168 | tf_op jit(solution)/shard_map/all_gather | solution.py:51
  45.8 2.6 fusion.49
  50.0 1.3 fusion.2
  51.4 2.7 fusion.104
  58.8 3.4 all-to-all-start.1
  62.4 17.1 %all_gather.24 = bf16[6,1024]{1,0:T(8,128)(2,1)S(1)} all-gather(bf16[6,128]{1,0:T(8,128)(2,1)S(1)} %stack.27), channel_id=1, replica_groups=mesh['dp'=4,'blk'=4,'head'=2] {'blk','head'}, dimensions={1}, use_global_device_ids=true | all-gather | bytes 13824 | tf_op jit(solution)/shard_map/all_gather | solution.py:49
  80.3 2.3 fusion.109
  83.7 1.3 copy.62
  85.1 3.6 all-to-all-start.2
  88.9 17.0 %all-to-all-done.2 = bf16[128,8,512]{0,2,1:T(8,128)(2,1)S(1)} async-done(((bf16[128,8,512]{0,2,1:T(8,128)(2,1)}), bf16[128,8,512]{0,2,1:T(8,128)(2,1)S(1)}, u32[]{:S(2)}, u32[]{:S(2)}) %all-to-all-start.2) | async-done | bytes 1048608 | tf_op jit(solution)/shard_map/all_to_all | solution.py:77
  105.9 1.3 copy.63
  107.2 10.5 %all-gather.10.cloned.1.call-done = bf16[1024,1024]{1,0:T(8,128)(2,1)} async-done(((bf16[128,1024]{1,0:T(8,128)(2,1)}), bf16[1024,1024]{1,0:T(8,128)(2,1)}) %all-gather.10.cloned.1.call-update) | async-done | bytes 2097168 | tf_op jit(solution)/shard_map/all_gather | solution.py:76
  117.7 8.5 %multiply_convert_fusion.4 = (bf16[1024,512]{1,0:T(8,128)(2,1)S(1)}, f32[1024,512]{1,0:T(8,128)}, f32[1024,512]{1,0:T(8,128)}) fusion(f32[512]{0:T(512)S(1)} %convert_element_type.163, bf16[1024,1024]{1,0:T(8,128)(2,1)} %all-gather.10.cloned.1.call-done, bf16[1024,512]{1,0:T(8,128)(2,1)} %bitcast.200), kind=kOutput, calls=%fused_computation.24 | convolution fusion | flops 1108344832 | bytes 8390656 | tf_op jit(solution)/shard_map/dot_general | solution.py:15
  127.2 2.6 convolution_convert_fusion.2
  129.9 41.3 %reduce-scatter.7.cloned.1.call-done = bf16[128,1024]{1,0:T(8,128)(2,1)} async-done(((bf16[1024,1024]{1,0:T(8,128)(2,1)}), bf16[128,1024]{1,0:T(8,128)(2,1)}) %reduce-scatter.7.cloned.1.call-update) | async-done | bytes 262160 | tf_op jit(solution)/shard_map/reduce_scatter | solution.py:82
  171.2 1.2 fusion.102
  173.0 1.1 fusion.100
  174.1 28.0 %all-gather.12.cloned.1.call-done = bf16[1024,1024]{1,0:T(8,128)(2,1)} async-done(((bf16[128,1024]{1,0:T(8,128)(2,1)}), bf16[1024,1024]{1,0:T(8,128)(2,1)}) %all-gather.12.cloned.1.call-update) | async-done | bytes 2097168 | tf_op jit(solution)/shard_map/all_gather | solution.py:87
  202.1 4.9 fusion.98
  208.0 2.6 convolution_convert_fusion.1
  210.6 41.4 %reduce-scatter.9.cloned.1.call-done = bf16[128,1024]{1,0:T(8,128)(2,1)} async-done(((bf16[1024,1024]{1,0:T(8,128)(2,1)}), bf16[128,1024]{1,0:T(8,128)(2,1)}) %reduce-scatter.9.cloned.1.call-update) | async-done | bytes 262160 | tf_op jit(solution)/shard_map/reduce_scatter | solution.py:91
  252.0 1.2 multiply_reduce_fusion.2
  253.3 2.0 fusion.99
  255.2 2.5 fusion.48
  258.5 3.4 all-to-all-start.3
  262.1 1.0 copy.68
  264.1 3.7 all-to-all-done.3
  267.9 5.1 multiply_reduce_fusion
  273.0 2.8 multiply_reduce_fusion.1
  276.5 7.9 %multiply_convert_fusion = (bf16[1024,1024]{1,0:T(8,128)(2,1)}, bf16[1024,1024]{1,0:T(8,128)(2,1)}) fusion(f32[1024,1024]{1,0:T(8,128)} %get-tuple-element.71, f32[1024,1024]{1,0:T(8,128)S(1)} %copy-done.3, f32[1024]{0:T(1024)S(1)} %get-tuple-element.70, f32[1024]{0:T(1024)S(1)} %maximum_divide_fusion, f32[1024,1024]{1,0:T(8,128)} %get-tuple-element.67, ...), kind=kLoop, calls=%fused_computation | loop fusion | flops 8388608 | bytes 20987904 | tf_op jit(solution)/shard_map/convert_element_type | solution.py:103
  284.5 2.2 constant_dynamic-update-slice_fusion.3
  286.7 1.1 constant_dynamic-update-slice_fusion.2
  289.4 1.4 constant_dynamic-update-slice_fusion.1
  290.8 1.5 constant_dynamic-update-slice_fusion
  293.2 2.6 convolution_convert_fusion
  295.9 1.2 copy-done.44
  297.1 2.2 convolution_convert_fusion.4
  299.3 3.7 all-to-all-start.5
  303.0 2.1 fusion.22
  305.1 1.0 copy.86
  306.2 14.1 %all-to-all-done.5 = bf16[8,128,512]{2,1,0:T(8,128)(2,1)S(1)} async-done(((bf16[8,128,512]{2,1,0:T(8,128)(2,1)}), bf16[8,128,512]{2,1,0:T(8,128)(2,1)S(1)}, u32[]{:S(2)}, u32[]{:S(2)}) %all-to-all-start.5) | async-done | bytes 1048608 | tf_op jit(solution)/shard_map/all_to_all | solution.py:90
  320.3 3.5 all-to-all-start.4
  324.2 1.1 dynamic-slice_reduce_fusion
  327.4 1.0 maximum_reduce_fusion.1
  328.4 12.6 %all-to-all-done.4 = bf16[8,128,384]{1,2,0:T(8,128)(2,1)S(1)} async-done(((bf16[8,128,384]{1,2,0:T(8,128)(2,1)}), bf16[8,128,384]{1,2,0:T(8,128)(2,1)S(1)}, u32[]{:S(2)}, u32[]{:S(2)}) %all-to-all-start.4) | async-done | bytes 786464 | tf_op jit(solution)/shard_map/all_to_all | solution.py:109
  341.5 1.0 bitcast_dynamic-update-slice_fusion
  342.6 1.1 dynamic-slice_reduce_fusion.1
  343.8 2.9 fusion.41
  346.7 1.0 constant_dynamic-update-slice_fusion.5
  347.8 2.3 fusion.18
  350.7 37.5 %reduce-scatter.11.cloned.1.call-done = bf16[128,1024]{1,0:T(8,128)(2,1)} async-done(((bf16[1024,1024]{1,0:T(8,128)(2,1)}), bf16[128,1024]{1,0:T(8,128)(2,1)}) %reduce-scatter.11.cloned.1.call-update) | async-done | bytes 262160 | tf_op jit(solution)/shard_map/reduce_scatter | solution.py:110
  388.1 1.8 add_bitcast_fusion
  389.9 122.2 %all-reduce.2.cloned.1.call-done = bf16[1538,1024]{1,0:T(8,128)(2,1)} async-done(((bf16[1538,1024]{1,0:T(8,128)(2,1)}), bf16[1538,1024]{1,0:T(8,128)(2,1)}) %all-reduce.2.cloned.1.call-update) | async-done | bytes 3149840 | tf_op jit(solution)/shard_map/psum | solution.py:136
  514.0 2.5 slice.161
  516.5 2.5 reshape.164
  519.0 1.1 fusion.107
  522.8 1.8 fusion.106
  524.6 1.9 reshape.165
  526.5 1.8 slice.165
  (166 shorter events, 27.0 us)
Async XLA Ops:
  7.2 120.0 %copy-start = (bf16[512,1024]{1,0:T(8,128)(2,1)S(1)}, bf16[512,1024]{1,0:T(8,128)(2,1)}, u32[]{:S(2)}) copy-start(bf16[512,1024]{1,0:T(8,128)(2,1)} %param.26) | copy-start | bytes 3145732
  7.2 38.6 %all-gather.16.cloned.1.call-start = ((), (), s32[]{:S(2)}) async-start(), calls=%async_computation.18 | async-start | bytes 2359296 | tf_op jit(solution)/shard_map/all_gather | solution.py:51
  10.2 8.0 %copy-start.41 = (bf16[128]{0:T(256)(128)(2,1)S(1)}, bf16[128]{0:T(256)(128)(2,1)}, u32[]{:S(2)}) copy-start(bf16[128]{0:T(256)(128)(2,1)} %param.27) | copy-start | bytes 772
  10.2 8.1 %copy-start.42 = (bf16[128]{0:T(256)(128)(2,1)S(1)}, bf16[128]{0:T(256)(128)(2,1)}, u32[]{:S(2)}) copy-start(bf16[128]{0:T(256)(128)(2,1)} %param.28) | copy-start | bytes 772
  10.2 8.1 %copy-start.40 = (s32[1,256]{1,0:T(1,128)S(1)}, s32[1,256]{1,0:T(1,128)}, u32[]{:S(2)}) copy-start(s32[1,256]{1,0:T(1,128)} %param.19) | copy-start | bytes 3076
  12.3 26.9 %all-to-all-start = ((bf16[128,8,384]{0,2,1:T(8,128)(2,1)}), bf16[128,8,384]{0,2,1:T(8,128)(2,1)S(1)}, u32[]{:S(2)}, u32[]{:S(2)}) async-start(bf16[128,8,384]{0,2,1:T(8,128)(2,1)} %pad_maximum_fusion), calls=%async_computation | async-start | bytes 1572864 | tf_op jit(solution)/shard_map/all_to_all | solution.py:52
  17.5 62.1 %all-gather.8.cloned.1.call-start = ((), (), s32[]{:S(2)}) async-start(), calls=%async_computation.10 | async-start | bytes 2359296 | tf_op jit(solution)/shard_map/all_gather | solution.py:72
  39.6 14.6 %copy-start.11 = (bf16[8,128,384]{2,1,0:T(8,128)(2,1)}, bf16[8,128,384]{2,1,0:T(8,128)(2,1)S(1)}, u32[]{:S(2)}) copy-start(bf16[8,128,384]{2,1,0:T(8,128)(2,1)S(1)} %copy.59) | copy-start | bytes 2359300
  45.8 2.6 copy-start.6
  48.4 1.6 copy-start.14
  49.3 0.7 copy-start.16
  54.1 1.9 copy-start.2
  54.1 3.4 copy-start.4
  56.0 6.3 %copy-start.33 = (bf16[128]{0:T(256)(128)(2,1)S(1)}, bf16[128]{0:T(256)(128)(2,1)}, u32[]{:S(2)}) copy-start(bf16[128]{0:T(256)(128)(2,1)} %param.29) | copy-start | bytes 772
  56.0 6.3 %copy-start.34 = (bf16[128]{0:T(256)(128)(2,1)S(1)}, bf16[128]{0:T(256)(128)(2,1)}, u32[]{:S(2)}) copy-start(bf16[128]{0:T(256)(128)(2,1)} %param.31) | copy-start | bytes 772
  56.0 6.3 %copy-start.35 = (bf16[128]{0:T(256)(128)(2,1)S(1)}, bf16[128]{0:T(256)(128)(2,1)}, u32[]{:S(2)}) copy-start(bf16[128]{0:T(256)(128)(2,1)} %param.32) | copy-start | bytes 772
  56.0 6.3 %copy-start.36 = (bf16[128]{0:T(256)(128)(2,1)S(1)}, bf16[128]{0:T(256)(128)(2,1)}, u32[]{:S(2)}) copy-start(bf16[128]{0:T(256)(128)(2,1)} %param.33) | copy-start | bytes 772
  56.0 6.3 %copy-start.37 = (bf16[128]{0:T(256)(128)(2,1)S(1)}, bf16[128]{0:T(256)(128)(2,1)}, u32[]{:S(2)}) copy-start(bf16[128]{0:T(256)(128)(2,1)} %param.34) | copy-start | bytes 772
  56.1 6.3 %copy-start.38 = (bf16[128]{0:T(256)(128)(2,1)S(1)}, bf16[128]{0:T(256)(128)(2,1)}, u32[]{:S(2)}) copy-start(bf16[128]{0:T(256)(128)(2,1)} %param.35) | copy-start | bytes 772
  56.1 24.2 %copy-start.27 = (bf16[1,128,1024]{2,1,0:T(8,128)(2,1)S(1)}, bf16[1,128,1024]{2,1,0:T(8,128)(2,1)}, u32[]{:S(2)}) copy-start(bf16[1,128,1024]{2,1,0:T(8,128)(2,1)} %param.18) | copy-start | bytes 786436
  57.5 0.6 copy-start.21
  58.8 20.8 %all-to-all-start.1 = ((bf16[8,128,128]{1,2,0:T(8,128)(2,1)}), bf16[8,128,128]{1,2,0:T(8,128)(2,1)S(1)}, u32[]{:S(2)}, u32[]{:S(2)}) async-start(bf16[8,128,128]{1,2,0:T(8,128)(2,1)} %pad_maximum_fusion.1), calls=%async_computation.1 | async-start | bytes 524288 | tf_op jit(solution)/shard_map/all_to_all | solution.py:71
  62.2 55.5 %all-gather.10.cloned.1.call-start = ((), (), s32[]{:S(2)}) async-start(), calls=%async_computation.11 | async-start | bytes 2359296 | tf_op jit(solution)/shard_map/all_gather | solution.py:76
  79.6 0.7 copy-start.28
  80.3 3.4 copy-start.23
  83.7 5.1 copy-start.32
  85.1 20.8 %all-to-all-start.2 = ((bf16[128,8,512]{0,2,1:T(8,128)(2,1)}), bf16[128,8,512]{0,2,1:T(8,128)(2,1)S(1)}, u32[]{:S(2)}, u32[]{:S(2)}) async-start(bf16[128,8,512]{0,2,1:T(8,128)(2,1)} %bitcast.191), calls=%async_computation.2 | async-start | bytes 2097152 | tf_op jit(solution)/shard_map/all_to_all | solution.py:77
  88.6 82.6 %reduce-scatter.7.cloned.1.call-start = ((), (), s32[]{:S(2)}) async-start(), calls=%async_computation.12 | async-start | bytes 2359296 | tf_op jit(solution)/shard_map/reduce_scatter | solution.py:82
  126.2 1.0 copy-start.25
  129.8 42.9 %copy-start.19 = (bf16[1,128,1024]{2,1,0:T(8,128)(2,1)S(1)}, bf16[1,128,1024]{2,1,0:T(8,128)(2,1)}, u32[]{:S(2)}) copy-start(bf16[1,128,1024]{2,1,0:T(8,128)(2,1)} %param.20) | copy-start | bytes 786436
  129.8 72.2 %all-gather.12.cloned.1.call-start = ((), (), s32[]{:S(2)}) async-start(), calls=%async_computation.13 | async-start | bytes 2359296 | tf_op jit(solution)/shard_map/all_gather | solution.py:87
  174.1 77.9 %reduce-scatter.9.cloned.1.call-start = ((), (), s32[]{:S(2)}) async-start(), calls=%async_computation.14 | async-start | bytes 2359296 | tf_op jit(solution)/shard_map/reduce_scatter | solution.py:91
  202.1 5.9 %copy-start.24 = (bf16[8,128,512]{2,1,0:T(8,128)(2,1)S(1)}, bf16[8,128,512]{2,1,0:T(8,128)(2,1)}, u32[]{:S(2)}) copy-start(bf16[8,128,512]{2,1,0:T(8,128)(2,1)} %copy.63) | copy-start | bytes 3145732
  207.0 1.0 copy-start.43
  255.2 7.9 %copy-start.18 = (bf16[128,1024]{1,0:T(8,128)(2,1)}, bf16[128,1024]{1,0:T(8,128)(2,1)S(1)}, u32[]{:S(2)}) copy-start(bf16[128,1024]{1,0:T(8,128)(2,1)S(1)} %get-tuple-element.28) | copy-start | bytes 786436
  258.5 9.4 %all-to-all-start.3 = ((bf16[128,8,128]{2,0,1:T(8,128)(2,1)}), bf16[128,8,128]{2,0,1:T(8,128)(2,1)S(1)}, u32[]{:S(2)}, u32[]{:S(2)}) async-start(bf16[128,8,128]{2,0,1:T(8,128)(2,1)} %bitcast.184), calls=%async_computation.5 | async-start | bytes 524288 | tf_op jit(solution)/shard_map/all_to_all | solution.py:96
  261.9 64.4 %reduce-scatter.13.cloned.1.call-start = ((), (), s32[]{:S(2)}) async-start(), calls=%async_computation.19 | async-start | bytes 589824
  263.1 79.5 %all-gather.14.cloned.1.call-start = ((), (), s32[]{:S(2)}) async-start(), calls=%async_computation.16 | async-start | bytes 2359296 | tf_op jit(solution)/shard_map/all_gather | solution.py:94
  263.9 124.2 %reduce-scatter.11.cloned.1.call-start = ((), (), s32[]{:S(2)}) async-start(), calls=%async_computation.15 | async-start | bytes 2359296 | tf_op jit(solution)/shard_map/reduce_scatter | solution.py:110
  267.9 5.1 copy-start.5
  273.0 3.5 copy-start.3
  276.5 7.9 %copy-start.15 = (bf16[1024,128]{0,1:T(8,128)(2,1)S(1)}, bf16[1024,128]{0,1:T(8,128)(2,1)}, u32[]{:S(2)}) copy-start(bf16[1024,128]{0,1:T(8,128)(2,1)} %copy-done.14) | copy-start | bytes 786436
  284.4 2.3 copy-start.8
  284.5 3.4 copy-start.9
  284.5 3.4 copy-start.17
  290.8 2.4 copy-start.12
  292.3 0.9 copy-start.31
  293.2 2.7 copy-start.39
  295.8 1.2 copy-start.44
  299.3 3.7 copy-start.7
  299.3 21.0 %all-to-all-start.5 = ((bf16[8,128,512]{2,1,0:T(8,128)(2,1)}), bf16[8,128,512]{2,1,0:T(8,128)(2,1)S(1)}, u32[]{:S(2)}, u32[]{:S(2)}) async-start(bf16[8,128,512]{2,1,0:T(8,128)(2,1)} %bitcast.202), calls=%async_computation.8 | async-start | bytes 2097152 | tf_op jit(solution)/shard_map/all_to_all | solution.py:90
  320.3 20.7 %all-to-all-start.4 = ((bf16[8,128,384]{1,2,0:T(8,128)(2,1)}), bf16[8,128,384]{1,2,0:T(8,128)(2,1)S(1)}, u32[]{:S(2)}, u32[]{:S(2)}) async-start(bf16[8,128,384]{1,2,0:T(8,128)(2,1)} %bitcast.180), calls=%async_computation.7 | async-start | bytes 1572864 | tf_op jit(solution)/shard_map/all_to_all | solution.py:109
  323.8 188.3 %all-reduce.2.cloned.1.call-start = ((), (), s32[]{:S(2)}) async-start(), calls=%async_computation.17 | async-start | bytes 6324224 | tf_op jit(solution)/shard_map/psum | solution.py:136
  325.3 2.0 copy-start.29
  325.3 2.1 copy-start.30
  326.3 17.5 %copy-start.22 = (bf16[1024,64]{0,1:T(8,128)(2,1)S(1)}, bf16[1024,64]{0,1:T(8,128)(2,1)}, u32[]{:S(2)}) copy-start(bf16[1024,64]{0,1:T(8,128)(2,1)} %copy-done.21) | copy-start | bytes 393220
  343.8 4.0 copy-start.13
  343.8 4.0 copy-start.26
  350.1 38.1 %copy-start.20 = (f32[128,1024]{1,0:T(8,128)S(1)}, f32[128,1024]{1,0:T(8,128)}, u32[]{:S(2)}) copy-start(f32[128,1024]{1,0:T(8,128)} %get-tuple-element.29) | copy-start | bytes 1572868
  519.0 3.8 copy-start.10
  524.6 3.7 copy-start.1
Sparse Core Ops, SparseCore 0:
  9.9 35.8 all-gather.15
  47.7 28.1 all-gather.7
  83.8 33.8 all-gather.9
  130.0 41.1 reduce-scatter.6
  174.2 27.8 all-gather.11
  210.8 41.2 reduce-scatter.8
  266.4 35.5 reduce-scatter.12
  304.1 38.4 all-gather.13
  346.8 41.2 reduce-scatter.10
  390.4 121.7 all-reduce.1

commit v2 on v0

--- a/solution.py
+++ b/solution.py
@@ -1,11 +1,761 @@
 from functools import partial
+from types import SimpleNamespace
 
 import jax
 import jax.numpy as jnp
 from jax import lax
+from jax.experimental import pallas as pl
+from jax.experimental.pallas import tpu as pltpu
 from jax.sharding import PartitionSpec as P
 
 HD = 64
+BF = jnp.bfloat16
+F32 = jnp.float32
+GROUP = ("blk", "head")
+MESH = pl.DeviceIdType.MESH
+NN = ((1,), (0,))
+NT = ((1,), (1,))
+TN = ((0,), (0,))
+
+
+def mm(a, b, dims):
+    return lax.dot_general(a, b, (dims, ((), ())), preferred_element_type=F32)
+
+
+def norm_parts(v):
+    c = v - jnp.mean(v, -1, keepdims=True)
+    r = lax.rsqrt(jnp.mean(c * c, -1, keepdims=True) + 1e-05)
+    return c * r, r
+
+
+def norm_back(e, n, r):
+    return r * (e - jnp.mean(e, -1, keepdims=True) - n * jnp.mean(e * n, -1, keepdims=True))
+
+
+def colsum(x):
+    return jnp.sum(x.astype(F32), 0, keepdims=True)
+
+
+def rows(ref):
+    x = ref[...]
+    return x.reshape(-1, x.shape[-1])
+
+
+def layer_kernel(names, *refs):
+    R = SimpleNamespace(**dict(zip(names, refs, strict=True)))
+    dp, blk, head = [lax.axis_index(a) for a in ("dp", "blk", "head")]
+    core, chip_x = lax.rem(blk, 2), lax.div(blk, 2)
+    T, D = R.tok.shape
+    W = R.q.shape[-1]
+    FW = R.wi.shape[1] // 8
+
+    def dev(p, flip):
+        hh = lax.rem(head + lax.rem(p, 2), 2)
+        bb = lax.rem(chip_x + lax.div(p, 2), 2) * 2 + lax.rem(core + flip, 2)
+        return (dp, bb, hh), bb * 2 + hh
+
+    def c32(i):
+        return jnp.asarray(i, jnp.int32)
+
+    me = blk * 2 + head
+    partner, partner_at = dev(c32(0), 1)
+    z_end = lax.rem(dp, 3) == 0
+    z_other = jnp.where(dp == 0, 1, jnp.where(dp == 3, 2, jnp.where(dp == 1, 0, 3)))
+    z_mid = jnp.where(dp == 1, 2, 1)
+
+    def rcopy(src, dst, ssem, rsem, to):
+        return pltpu.make_async_remote_copy(src, dst, ssem, rsem, device_id=to, device_id_type=MESH)
+
+    def lanes(i, w):
+        return pl.ds(pl.multiple_of(i * w, w), w)
+
+    bar = pltpu.get_barrier_semaphore()
+    for e in range(1, 8):
+        to, _ = dev(c32(e // 2), e % 2)
+        pl.semaphore_signal(bar, 1, device_id=to, device_id_type=MESH)
+    for j in range(1, 4):
+        pl.semaphore_signal(bar, 1, device_id=(lax.rem(dp + j, 4), blk, head), device_id_type=MESH)
+    pl.semaphore_wait(bar, 10)
+
+    half = (pl.ds(0, T // 2), pl.ds(T // 2, T // 2))
+    by_y, by_x, by_both = 1, 2, 3
+
+    def ag_direct(buf, r, p, h):
+        to, _ = dev(c32(p), 0)
+        part = buf.at[me, half[h]]
+        return rcopy(part, part, R.ag_s.at[r, p, h], R.ag_r.at[r, p, h], to)
+
+    def ag_relay(buf, r, h):
+        via, over = (by_x, by_y) if h == 0 else (by_y, by_x)
+        _, at = dev(c32(via), 0)
+        to, _ = dev(c32(over), 0)
+        part = buf.at[at, half[h]]
+        return rcopy(part, part, R.ag_s.at[r, by_both, h], R.ag_r.at[r, by_both, h], to)
+
+    def ag_home(buf, r):
+        return rcopy(buf.at[me], buf.at[me], R.ag_fs.at[r, 0, 0], R.ag_f.at[r, 0, 0], partner)
+
+    def ag_forward(buf, r, p, h):
+        _, at = dev(c32(p), 0)
+        part = buf.at[at, half[h]]
+        return rcopy(part, part, R.ag_fs.at[r, p, h], R.ag_f.at[r, p, h], partner)
+
+    def ag_start(buf, r):
+        ag_direct(buf, r, by_x, 0).start()
+        ag_direct(buf, r, by_y, 1).start()
+        ag_direct(buf, r, by_x, 1).start()
+        ag_direct(buf, r, by_y, 0).start()
+        ag_home(buf, r).start()
+
+    def ag_got(buf, r, p, h):
+        (ag_relay(buf, r, h) if p == by_both else ag_direct(buf, r, p, h)).wait_recv()
+        ag_forward(buf, r, p, h).start()
+
+    def ag_wait(buf, r, p):
+        @pl.when(p == 0)
+        def _():
+            ag_home(buf, r).wait_recv()
+
+        @pl.when(p == by_y)
+        def _():
+            ag_got(buf, r, by_x, 0)
+            ag_relay(buf, r, 0).start()
+            ag_got(buf, r, by_y, 1)
+            ag_relay(buf, r, 1).start()
+            ag_got(buf, r, by_y, 0)
+            for h in (0, 1):
+                ag_forward(buf, r, by_y, h).wait_recv()
+
+        @pl.when(p == by_x)
+        def _():
+            ag_got(buf, r, by_x, 1)
+            for h in (0, 1):
+                ag_forward(buf, r, by_x, h).wait_recv()
+
+        @pl.when(p == by_both)
+        def _():
+            ag_got(buf, r, by_both, 0)
+            ag_got(buf, r, by_both, 1)
+            for h in (0, 1):
+                ag_forward(buf, r, by_both, h).wait_recv()
+
+    def ag_finish(buf, r):
+        ag_home(buf, r).wait_send()
+        for h in (0, 1):
+            ag_direct(buf, r, by_x, h).wait_send()
+            ag_direct(buf, r, by_y, h).wait_send()
+            ag_relay(buf, r, h).wait_send()
+            for p in (by_y, by_x, by_both):
+                ag_forward(buf, r, p, h).wait_send()
+
+    def pair(buf, p):
+        a, b = dev(p, 0)[1], dev(p, 1)[1]
+        return a, b, jnp.concatenate([buf[a], buf[b]], 0)
+
+    def rs_chip(r, p):
+        return rcopy(R.snd_c.at[p], R.rcv_c.at[r, p], R.rs_cs.at[r, p], R.rs_cr.at[r, p], partner)
+
+    def rs_link(r, p, h):
+        over = p if p != by_both else (by_x, by_y)[h]
+        to, _ = dev(c32(over), 0)
+        return rcopy(
+            R.snd_l.at[p, half[h]], R.rcv_l.at[r, p, half[h]], R.rs_ls.at[r, p, h], R.rs_lr.at[r, p, h], to
+        )
+
+    def rs_put(r, p, part):
+        R.snd_c[p] = part[T:].astype(BF)
+        rs_chip(r, p).start()
+        R.keep[p] = part[:T]
+
+    def rs_combine(r, p):
+        rs_chip(r, p).wait_recv()
+        both = R.keep[p] + R.rcv_c[r, p].astype(F32)
+        R.keep[p] = both
+        R.snd_l[p] = both.astype(BF)
+
+        @pl.when(p == by_y)
+        def _():
+            rs_link(r, by_y, 1).start()
+
+        @pl.when(p == by_x)
+        def _():
+            rs_link(r, by_x, 0).start()
+
+        @pl.when(p == by_both)
+        def _():
+            rs_link(r, by_both, 0).start()
+            rs_link(r, by_both, 1).start()
+
+    def rs_relay(r):
+        for p, h in ((by_y, 0), (by_x, 1)):
+            rs_link(r, by_both, h).wait_recv()
+            R.snd_l[p, half[h]] = (R.keep[p, half[h]] + R.rcv_l[r, by_both, half[h]].astype(F32)).astype(BF)
+            rs_link(r, p, h).start()
+
+    def rs_final(r):
+        rs_chip(r, c32(0)).wait_recv()
+        acc = R.keep[0] + R.rcv_c[r, 0].astype(F32)
+        for p in (by_y, by_x):
+            for h in (0, 1):
+                rs_link(r, p, h).wait_recv()
+            acc = acc + R.rcv_l[r, p].astype(F32)
+        for p in range(4):
+            rs_chip(r, c32(p)).wait_send()
+            if p:
+                for h in (0, 1):
+                    rs_link(r, p, h).wait_send()
+        return acc
+
+    zbufs = {
+        "b": [(lambda x, i=i: x.at[i]) for i in range(4)],
+        "i": [(lambda x, i=i: x.at[pl.ds(2 * i, 2)]) for i in range(4)],
+        "o": [lambda x: x],
+        "s": [lambda x: x],
+        "w": [(lambda x, i=i: x.at[i]) for i in range(8)],
+    }
+    chunks = [(k, cut) for k in zbufs for cut in zbufs[k]]
+    Z_IN, Z_OUT, Z_SMALL, Z_QKV, Z_ALL = 4, 8, 9, 10, 18
+
+    def zrefs(c):
+        k, cut = chunks[c]
+        return cut(getattr(R, "zown_" + k)), cut(getattr(R, "zsum_" + k)), cut(getattr(R, "zmid_" + k))
+
+    def z_up(c):
+        own, tot, _ = zrefs(c)
+        return rcopy(own, tot, R.z_s.at[c, 0], R.z_r.at[c, 0], (z_other, blk, head))
+
+    def z_across(c):
+        own, _, mid = zrefs(c)
+        return rcopy(own, mid, R.z_s.at[c, 0], R.z_r.at[c, 1], (z_mid, blk, head))
+
+    def z_down(c):
+        _, tot, _ = zrefs(c)
+        return rcopy(tot, tot, R.z_s.at[c, 1], R.z_r.at[c, 0], (z_other, blk, head))
+
+    def z_produce(c):
+        @pl.when(z_end)
+        def _():
+            z_up(c).start()
+
+    def z_one(c):
+        @pl.when(jnp.logical_not(z_end))
+        def _():
+            own, tot, _ = zrefs(c)
+            z_up(c).wait_recv()
+            own[...] = (own[...].astype(F32) + tot[...].astype(F32)).astype(BF)
+            z_across(c).start()
+
+    def z_two(c):
+        @pl.when(jnp.logical_not(z_end))
+        def _():
+            own, tot, mid = zrefs(c)
+            z_across(c).wait_recv()
+            tot[...] = (own[...].astype(F32) + mid[...].astype(F32)).astype(BF)
+            z_down(c).start()
+
+    def z_finish(c):
+        @pl.when(z_end)
+        def _():
+            z_up(c).wait_send()
+            z_down(c).wait_recv()
+
+        @pl.when(jnp.logical_not(z_end))
+        def _():
+            z_across(c).wait_send()
+            z_down(c).wait_send()
+
+    tok_all, y1_all, df_all, da_all = R.tok_all, R.y1_all, R.df_all, R.da_all
+    local = [
+        pltpu.make_async_copy(R.tok, tok_all.at[me], R.loc.at[0]),
+        pltpu.make_async_copy(R.wb, R.wb_v, R.loc.at[1]),
+        pltpu.make_async_copy(R.wo, R.wo_v, R.loc.at[2]),
+        pltpu.make_async_copy(R.wi.at[:, lanes(me, FW)], R.win.at[me], R.loc.at[3]),
+        pltpu.make_async_copy(R.cot, R.cot_v, R.loc.at[4]),
+    ]
+    for j, w in enumerate((R.wq, R.wk, R.wv)):
+        local.append(pltpu.make_async_copy(w.at[:, lanes(me, W)], R.wqkv.at[me, :, pl.ds(j * W, W)], R.loc.at[5 + j]))
+    for cp in local:
+        cp.start()
+    vecs = [x[...].astype(F32).reshape(1, T) for x in (R.bo, R.bb, R.g1, R.s1, R.g2, R.s2)]
+    vecs.append(R.ids[0:1, lanes(head, T)].astype(F32))
+    R.vec[...] = jnp.concatenate(vecs + [jnp.zeros((1, T), F32)], 0)
+    R.vec_all[me] = R.vec[...]
+
+    def vec_copy(e):
+        to, _ = dev(c32(e // 2), e % 2)
+        return rcopy(R.vec, R.vec_all.at[me], R.vec_s.at[e], R.vec_r.at[e], to)
+
+    def qkv_copy(e, j):
+        to, at = dev(c32(e // 2), e % 2)
+        w = (R.wq, R.wk, R.wv)[j]
+        return rcopy(w.at[:, lanes(at, W)], R.wqkv.at[me, :, pl.ds(j * W, W)], R.qkv_s.at[e, j], R.qkv_r.at[e, j], to)
+
+    def win_copy(e):
+        to, at = dev(c32(e // 2), e % 2)
+        return rcopy(R.wi.at[:, lanes(at, FW)], R.win.at[me], R.win_s.at[e], R.win_r.at[e], to)
+
+    far_first = (6, 7, 2, 3, 4, 5, 1)
+    with jax.named_scope("start_copies"):
+        for e in far_first:
+            vec_copy(e).start()
+        for e in far_first:
+            for j in range(3):
+                qkv_copy(e, j).start()
+        local[0].wait()
+        ag_start(tok_all, 0)
+
+    with jax.named_scope("vectors"):
+        for e in range(1, 8):
+            vec_copy(e).wait_recv()
+        for s in range(8):
+            v = R.vec_all[s]
+            R.vfull[:, s * T:(s + 1) * T] = v
+            ids = jnp.broadcast_to(v[6:7], (T, T)).T
+            R.segk[s] = jnp.where(ids < 0, -2.0, ids)
+
+    with jax.named_scope("wait_qkv_weights"):
+        for e in range(1, 8):
+            for j in range(3):
+                qkv_copy(e, j).wait_recv()
+        for j in range(5, 8):
+            local[j].wait()
+
+    def qkv_step(p, carry):
+        ag_wait(tok_all, 0, p)
+        a, b, x = pair(tok_all, p)
+        y = mm(x, rows(R.wqkv), NN)
+        qq = ((y[:, :W] + R.bq[...].astype(F32).reshape(1, W)) * 0.125).astype(BF)
+        kk = y[:, W:2 * W].astype(BF)
+        vv = (y[:, 2 * W:] + R.bv[...].astype(F32).reshape(1, W)).astype(BF)
+        for at, sl in ((a, slice(0, T)), (b, slice(T, 2 * T))):
+            R.q[at], R.k[at], R.v[at] = qq[sl], kk[sl], vv[sl]
+        return carry
+
+    with jax.named_scope("project_qkv"):
+        lax.fori_loop(0, 4, qkv_step, 0)
+    for e in far_first:
+        win_copy(e).start()
+    for i in (1, 2, 3, 4):
+        local[i].wait()
+
+    def head_mask(h, like):
+        lane = lax.broadcasted_iota(jnp.int32, like.shape, 1)
+        return jnp.where(lax.div(lane, HD) == h, like, jnp.zeros_like(like))
+
+    heads = W // HD
+
+    def ids_of(a, b):
+        return jnp.concatenate([R.vec_all[a, 6:7], R.vec_all[b, 6:7]], 1)
+
+    def attend_step(i, carry):
+        p = 3 - i
+        a, b, qp = pair(R.q, p)
+        segq = ids_of(a, b)
+        segk = rows(R.segk)
+        allowed = jnp.concatenate([segk, segk], 1) == segq
+        kk = rows(R.k)
+        outs = []
+        for h in range(heads):
+            s = jnp.where(allowed, mm(kk, head_mask(h, qp), NT), -1e30)
+            ex = jnp.exp(s - jnp.max(s, 0, keepdims=True))
+            total = jnp.maximum(jnp.sum(ex, 0, keepdims=True), 1.0)
+            pt = (ex * jnp.where(segq >= 0, 1.0 / total, 0.0)).astype(BF)
+            R.pt[h, p] = pt
+            outs.append(mm(R.vt[h * HD:(h + 1) * HD, :], pt, NN))
+        ct = jnp.concatenate(outs, 0).astype(BF)
+        R.ctxt[:, lanes(a, T)] = ct[:, :T]
+        R.ctxt[:, lanes(b, T)] = ct[:, T:]
+        rs_put(0, p, mm(ct, R.wo_v[...], TN))
+
+        @pl.when(p < 3)
+        def _():
+            rs_combine(0, p + 1)
+
+        return carry
+
+    with jax.named_scope("attend"):
+        R.vt[...] = rows(R.v).T
+        lax.fori_loop(0, 4, attend_step, 0)
+
+    with jax.named_scope("first_norm"):
+        rs_relay(0)
+        rs = rs_final(0)
+        h1 = tok_all[me].astype(F32) + rs + R.vfull[0:1]
+        n1, r1 = norm_parts(h1)
+        y1 = n1 * R.vfull[2:3] + R.vfull[3:4]
+        R.n1[...], R.y1[...] = n1, y1
+        R.r1[...] = jnp.broadcast_to(r1, R.r1.shape)
+        y1_all[me] = y1.astype(BF)
+        ag_start(y1_all, 1)
+    R.kt[...] = rows(R.k).T
+
+    with jax.named_scope("wait_hidden_weights"):
+        for e in range(1, 8):
+            win_copy(e).wait_recv()
+
+    def hidden_step(p, carry):
+        ag_wait(y1_all, 1, p)
+        a, b, x = pair(y1_all, p)
+        z = hidden_in(x)
+        cdf = 0.5 * (1.0 + lax.erf(z * 0.7071067811865476))
+        low = (z * cdf).astype(BF)
+        slope = cdf + z * (jnp.exp(-0.5 * z * z) * 0.3989422804014327)
+        R.hid[a], R.hid[b] = low[:T], low[T:]
+        R.slope[a], R.slope[b] = slope[:T], slope[T:]
+        rs_put(1, p, mm(low, R.wb_v[...], NN))
+
+        @pl.when(p > 1)
+        def _():
+            rs_combine(1, p - 1)
+
+        return carry
+
+    def hidden_in(x):
+        return mm(x, rows(R.win), NN) + R.bi[...].astype(F32).reshape(1, FW)
+
+    with jax.named_scope("hidden"):
+        lax.fori_loop(0, 4, hidden_step, 0)
+        rs_combine(1, c32(3))
+
+    with jax.named_scope("second_norm"):
+        rs_relay(1)
+        rs = rs_final(1)
+        h2 = R.y1[...] + rs + R.vfull[1:2]
+        n2, r2 = norm_parts(h2)
+        gain = R.vfull[4:5]
+        R.out[...] = (n2 * gain + R.vfull[5:6]).astype(BF)
+        cot = R.cot_v[...].astype(F32)
+        dh2 = norm_back(cot * gain, n2, r2)
+        R.dh2[...] = dh2
+        df_all[me] = dh2.astype(BF)
+        ag_start(df_all, 2)
+        R.sv[0:1, :] = colsum(cot * n2)
+        R.sv[1:2, :] = colsum(cot)
+
+    def hidden_back_step(p, carry):
+        ag_wait(df_all, 2, p)
+        a, b, x = pair(df_all, p)
+        slope = jnp.concatenate([R.slope[a], R.slope[b]], 0)
+        dz = (mm(x, R.wb_v[...], NT) * slope).astype(BF)
+        R.dz[a], R.dz[b] = dz[:T], dz[T:]
+        rs_put(2, p, mm(dz, rows(R.win), NT))
+
+        @pl.when(p > 1)
+        def _():
+            rs_combine(2, p - 1)
+
+        return carry
+
+    with jax.named_scope("hidden_back"):
+        lax.fori_loop(0, 4, hidden_back_step, 0)
+        rs_combine(2, c32(3))
+
+    with jax.named_scope("grad_back"):
+        for i in range(4):
+            g = mm(R.hid[:, :, i * T:(i + 1) * T].reshape(8 * T, T), rows(df_all), TN)
+            R.zown_b[i] = g.astype(BF)
+            z_produce(i)
+        rs_relay(2)
+
+    def din_copy(p, flip):
+        to, at = dev(p, flip)
+        return rcopy(R.din_snd.at[at], R.zown_i.at[me], R.din_s.at[p, flip], R.din_r.at[p, flip], to)
+
+    def din_step(p, carry):
+        a, b = dev(p, 0)[1], dev(p, 1)[1]
+        x = jnp.concatenate([y1_all[:, :, lanes(a, T)], y1_all[:, :, lanes(b, T)]], 2).reshape(8 * T, 2 * T)
+        g = mm(x, rows(R.dz), TN).astype(BF)
+        R.din_snd[b] = g[T:]
+        din_copy(p, 1).start()
+
+        @pl.when(p == 0)
+        def _():
+            R.zown_i[me] = g[:T]
+
+        @pl.when(p > 0)
+        def _():
+            R.din_snd[a] = g[:T]
+            din_copy(p, 0).start()
+
+        return carry
+
+    with jax.named_scope("grad_in"):
+        lax.fori_loop(0, 4, din_step, 0)
+    z_one(0)
+
+    with jax.named_scope("first_norm_back"):
+        rs = rs_final(2)
+        dy1 = R.dh2[...] + rs
+        n1 = R.n1[...]
+        dh1 = norm_back(dy1 * R.vfull[2:3], n1, R.r1[:, 0:1])
+        R.dh1[...] = dh1
+        da_all[me] = dh1.astype(BF)
+        ag_start(da_all, 3)
+        R.sv[2:3, :] = colsum(dy1 * n1)
+        R.sv[3:4, :] = colsum(dy1)
+
+    def sv_copy(e):
+        to, at = dev(c32(e // 2), e % 2)
+        return rcopy(R.sv.at[:, lanes(at, T)], R.sv_rcv.at[me], R.sv_s.at[e], R.sv_r.at[e], to)
+
+    for e in far_first:
+        sv_copy(e).start()
+    R.sv_rcv[me] = R.sv[:, lanes(me, T)]
+    z_one(1)
+    z_two(0)
+
+    def z_service(p):
+        @pl.when(p == 1)
+        def _():
+            z_one(2)
+            z_two(1)
+
+        @pl.when(p == 3)
+        def _():
+            z_one(3)
+            z_two(2)
+
+    R.dk[...] = jnp.zeros_like(R.dk)
+    R.dv[...] = jnp.zeros_like(R.dv)
+
+    def attend_back_step(p, carry):
+        ag_wait(da_all, 3, p)
+        a, b, x = pair(da_all, p)
+        qp = jnp.concatenate([R.q[a], R.q[b]], 0)
+        dc = mm(x, R.wo_v[...], NT).astype(BF)
+        vv = rows(R.v)
+        outs = []
+        for h in range(heads):
+            dcm, qm = head_mask(h, dc), head_mask(h, qp)
+            low = R.pt[h, p]
+            pt = low.astype(F32)
+            dpt = mm(vv, dcm, NT)
+            ds = (pt * (dpt - jnp.sum(pt * dpt, 0, keepdims=True))).astype(BF)
+            outs.append(mm(R.kt[h * HD:(h + 1) * HD, :], ds, NN))
+            R.dk[...] += mm(ds, qm, NN)
+            R.dv[...] += mm(low, dcm, NN)
+        dq = jnp.concatenate(outs, 0).T.astype(BF) * 0.125
+        R.dqkv[a, :, 0:W] = dq[:T]
+        R.dqkv[b, :, 0:W] = dq[T:]
+        z_service(p)
+        return carry
+
+    with jax.named_scope("attend_back"):
+        lax.fori_loop(0, 4, attend_back_step, 0)
+        R.dqkv[:, :, W:2 * W] = R.dk[...].astype(BF).reshape(8, T, W)
+        R.dqkv[:, :, 2 * W:] = R.dv[...].astype(BF).reshape(8, T, W)
+
+    def dqkv_copy(p, flip):
+        to, at = dev(p, flip)
+        return rcopy(R.dqkv_snd.at[at], R.zown_w.at[me], R.dqkv_s.at[p, flip], R.dqkv_r.at[p, flip], to)
+
+    def dqkv_step(p, carry):
+        a, b = dev(p, 0)[1], dev(p, 1)[1]
+        x = jnp.concatenate([tok_all[:, :, lanes(a, T)], tok_all[:, :, lanes(b, T)]], 2).reshape(8 * T, 2 * T)
+        g = mm(x, rows(R.dqkv), TN).astype(BF)
+        R.dqkv_snd[b] = g[T:]
+        dqkv_copy(p, 1).start()
+
+        @pl.when(p == 0)
+        def _():
+            R.zown_w[me] = g[:T]
+
+        @pl.when(p > 0)
+        def _():
+            R.dqkv_snd[a] = g[:T]
+            dqkv_copy(p, 0).start()
+
+        return carry
+
+    with jax.named_scope("grad_qkv"):
+        lax.fori_loop(0, 4, dqkv_step, 0)
+
+    with jax.named_scope("grad_out"):
+        for p in range(4):
+            for flip in (0, 1):
+                if (p, flip) != (0, 0):
+                    din_copy(c32(p), flip).wait_recv()
+        for c in range(Z_IN, Z_OUT):
+            z_produce(c)
+        R.zown_o[...] = mm(R.ctxt[...], rows(da_all), NN).astype(BF)
+        z_produce(Z_OUT)
+        z_one(4)
+        z_two(3)
+
+    def input_step(p, carry):
+        a, b, x = pair(R.dqkv, p)
+        rs_put(3, p, mm(x, rows(R.wqkv), NT))
+
+        @pl.when(p > 1)
+        def _():
+            rs_combine(3, p - 1)
+
+        return carry
+
+    with jax.named_scope("input_back"):
+        lax.fori_loop(0, 4, input_step, 0)
+        rs_combine(3, c32(3))
+        z_one(5)
+        z_two(4)
+
+    with jax.named_scope("small_grads"):
+        for e in range(1, 8):
+            sv_copy(e).wait_recv()
+        acc = R.sv_rcv[0]
+        for s in range(1, 8):
+            acc = acc + R.sv_rcv[s]
+        own = lanes(me, T)
+        parts = [
+            acc[0:4],
+            colsum(rows(R.dqkv)[:, 0:W]),
+            colsum(rows(R.dqkv)[:, 2 * W:]),
+            colsum(da_all[:, :, own].reshape(8 * T, T)),
+            colsum(df_all[:, :, own].reshape(8 * T, T)),
+        ]
+        dbi = colsum(rows(R.dz))
+        parts += [dbi[:, i * T:(i + 1) * T] for i in range(FW // T)]
+        parts.append(jnp.zeros((16 - 8 - FW // T, T), F32))
+        R.zown_s[...] = jnp.concatenate(parts, 0).astype(BF)
+        z_produce(Z_SMALL)
+        rs_relay(3)
+
+    with jax.named_scope("z_rest"):
+        z_one(6)
+        z_two(5)
+        for p in range(4):
+            for flip in (0, 1):
+                if (p, flip) != (0, 0):
+                    dqkv_copy(c32(p), flip).wait_recv()
+        for c in range(Z_QKV, Z_ALL):
+            z_produce(c)
+    with jax.named_scope("input_grad"):
+        R.igrad[...] = R.dh1[...] + rs_final(3)
+    with jax.named_scope("z_last"):
+        for c in range(7, Z_ALL):
+            z_one(c)
+            z_two(c - 1)
+        z_two(Z_ALL - 1)
+
+    with jax.named_scope("finish"):
+        for c in range(Z_ALL):
+            z_finish(c)
+        for buf, r in ((tok_all, 0), (y1_all, 1), (df_all, 2), (da_all, 3)):
+            ag_finish(buf, r)
+        for e in range(1, 8):
+            vec_copy(e).wait_send()
+            win_copy(e).wait_send()
+            sv_copy(e).wait_send()
+            for j in range(3):
+                qkv_copy(e, j).wait_send()
+            din_copy(c32(e // 2), e % 2).wait_send()
+            dqkv_copy(c32(e // 2), e % 2).wait_send()
+
+
+def sharded_plan(
+    tokens, segment_ids, cotangent,
+    w_query, w_key, w_value, w_out, w_in, w_back,
+    bias_query, bias_value, bias_out, bias_in, bias_back,
+    first_gain, first_shift, second_gain, second_shift,
+):
+    tokens, cotangent = tokens[0], cotangent[0]
+    T, D = tokens.shape
+    W, FW = D // 8, w_in.shape[1] // 8
+    ins = dict(
+        tok=tokens, cot=cotangent, wq=w_query, wk=w_key, wv=w_value, wo=w_out, wi=w_in, wb=w_back, ids=segment_ids,
+        bo=bias_out, bb=bias_back, g1=first_gain, s1=first_shift, g2=second_gain, s2=second_shift,
+        bq=bias_query, bv=bias_value, bi=bias_in,
+    )
+    in_hbm = 8
+    outs = dict(
+        out=((T, D), BF), igrad=((T, D), F32), zsum_b=((4, T, D), BF), zsum_i=((8, T, FW), BF),
+        zsum_o=((T, D), BF), zsum_w=((8, T, 3 * W), BF), zsum_s=((16, T), BF),
+    )
+    blocks = {k: ((8, T, D), BF) for k in ("tok_all", "y1_all", "df_all", "da_all")}
+    scr = dict(
+        **blocks,
+        wqkv=((8, T, 3 * W), BF), win=((8, T, FW), BF), wb_v=(w_back.shape, BF), wo_v=(w_out.shape, BF),
+        cot_v=((T, D), BF), vec=((8, T), F32), vec_all=((8, 8, T), F32), vfull=((8, D), F32), segk=((8, T, T), F32),
+        q=((8, T, W), BF), k=((8, T, W), BF), v=((8, T, W), BF), vt=((W, 8 * T), BF), kt=((W, 8 * T), BF),
+        pt=((W // HD, 4, 8 * T, 2 * T), BF), ctxt=((W, 8 * T), BF),
+        hid=((8, T, FW), BF), slope=((8, T, FW), F32), dz=((8, T, FW), BF),
+        n1=((T, D), F32), r1=((T, 128), F32), y1=((T, D), F32), dh2=((T, D), F32), dh1=((T, D), F32),
+        sv=((8, D), F32), sv_rcv=((8, 8, T), F32),
+        keep=((4, T, D), F32), snd_c=((4, T, D), BF), snd_l=((4, T, D), BF),
+        rcv_c=((4, 4, T, D), BF), rcv_l=((4, 4, T, D), BF),
+        dk=((8 * T, W), F32), dv=((8 * T, W), F32), dqkv=((8, T, 3 * W), BF),
+        din_snd=((8, T, FW), BF), dqkv_snd=((8, T, 3 * W), BF),
+        **{z + k[4:]: s for z in ("zown", "zmid") for k, s in outs.items() if k.startswith("zsum")},
+    )
+    sems = dict(
+        ag_s=(4, 4, 2), ag_r=(4, 4, 2), ag_fs=(4, 4, 2), ag_f=(4, 4, 2),
+        rs_cs=(4, 4), rs_cr=(4, 4), rs_ls=(4, 4, 2), rs_lr=(4, 4, 2),
+        z_s=(18, 2), z_r=(18, 2), loc=(8,), vec_s=(8,), vec_r=(8,), qkv_s=(8, 3), qkv_r=(8, 3), win_s=(8,), win_r=(8,),
+        sv_s=(8,), sv_r=(8,), din_s=(4, 2), din_r=(4, 2), dqkv_s=(4, 2), dqkv_r=(4, 2),
+    )
+    names = list(ins) + list(outs) + list(scr) + list(sems)
+    res = pl.pallas_call(
+        partial(layer_kernel, names),
+        out_shape=[jax.ShapeDtypeStruct(*s) for s in outs.values()],
+        in_specs=[pl.BlockSpec(memory_space=pl.ANY if i < in_hbm else pltpu.VMEM) for i in range(len(ins))],
+        out_specs=[pl.BlockSpec(memory_space=pltpu.VMEM) for _ in outs],
+        scratch_shapes=[pltpu.VMEM(*s) for s in scr.values()] + [pltpu.SemaphoreType.DMA(s) for s in sems.values()],
+        compiler_params=pltpu.CompilerParams(collective_id=0, has_side_effects=True, vmem_limit_bytes=60 << 20),
+        name="layer",
+    )(*ins.values())
+    grid = 4
+    wide = pl.BlockSpec((T // grid, D), lambda i: (i, 0))
+
+    def whole(n):
+        return pl.BlockSpec((n,), lambda i: (0,))
+
+    firsts = [(T, D), (T, D), (T, D), (T, D), (T, D), (T, D), w_in.shape, w_back.shape]
+    types = [BF] + [F32] * 7
+    return_specs = [wide, wide] + [pl.BlockSpec((T, 2 * T), lambda i: (0, i))] * 3 + [
+        wide, pl.BlockSpec((T, 2 * FW), lambda i: (0, i)), pl.BlockSpec((T, D), lambda i: (i, 0)),
+    ]
+    sizes = [T, T, T, FW, T, T, T, T, T]
+    final = pl.pallas_call(
+        finish_kernel,
+        grid=(grid,),
+        out_shape=[jax.ShapeDtypeStruct(s, t) for s, t in zip(firsts, types)]
+        + [jax.ShapeDtypeStruct((n,), F32) for n in sizes],
+        in_specs=[
+            wide, wide, pl.BlockSpec((1, T, D), lambda i: (i, 0, 0)), pl.BlockSpec((2, T, FW), lambda i: (i, 0, 0)),
+            wide, pl.BlockSpec((2, T, 3 * W), lambda i: (i, 0, 0)), pl.BlockSpec((16, T), lambda i: (0, 0)),
+        ],
+        out_specs=return_specs + [whole(n) for n in sizes],
+        name="finish",
+    )(*res)
+    return (final[0][None], final[1][None], *final[2:])
+
+
+def finish_kernel(out, igrad, tb, ti, to, tw, ts, o_out, o_igrad, o_q, o_k, o_v, o_o, o_i, o_b, *o_small):
+    o_out[...] = out[...]
+    o_igrad[...] = igrad[...]
+    o_b[...] = tb[0].astype(F32)
+    o_o[...] = to[...].astype(F32)
+    width = ti.shape[2]
+    for j in range(2):
+        o_i[:, j * width:(j + 1) * width] = ti[j].astype(F32)
+    W = tw.shape[2] // 3
+    for j, o in enumerate((o_q, o_k, o_v)):
+        for s in range(2):
+            o[:, s * W:(s + 1) * W] = tw[s, :, j * W:(j + 1) * W].astype(F32)
+
+    @pl.when(pl.program_id(0) == 0)
+    def _():
+        v = ts[...].astype(F32)
+        bq, bv, bo, bi, bb, g1, s1, g2, s2 = o_small
+        for o, i in ((bq, 4), (bv, 5), (bo, 6), (bb, 7), (g1, 2), (s1, 3), (g2, 0), (s2, 1)):
+            o[...] = v[i]
+        n = v.shape[1]
+        for i in range(bi.shape[0] // n):
+            bi[i * n:(i + 1) * n] = v[8 + i]
+
+
+def pick_plan(mesh):
+    group = mesh.shape["blk"] * mesh.shape["head"]
+    return sharded_plan if (mesh.shape["dp"], group) == (4, 8) else general_plan
 
 
 def flat_dot(left_side, right_side):
@@ -91,7 +841,7 @@
     return array_in.transpose(0, 2, 1, 3).reshape(array_in.shape[0], array_in.shape[2], -1)
 
 
-def per_device(
+def general_plan(
     tokens,
     segment_ids,
     cotangent,
@@ -128,21 +878,21 @@
         gain_two,
         shift_two,
     ) = (
-        lax.all_gather(w_query, ("blk", "head"), axis=0, tiled=True),
-        lax.all_gather(w_key, ("blk", "head"), axis=0, tiled=True),
-        lax.all_gather(w_value, ("blk", "head"), axis=0, tiled=True),
-        lax.all_gather(w_out, ("blk", "head"), axis=0, tiled=True),
-        lax.all_gather(w_in, ("blk", "head"), axis=0, tiled=True),
-        lax.all_gather(w_back, ("blk", "head"), axis=0, tiled=True),
-        lax.all_gather(bias_query, ("blk", "head"), axis=0, tiled=True),
-        lax.all_gather(bias_value, ("blk", "head"), axis=0, tiled=True),
-        lax.all_gather(bias_out, ("blk", "head"), axis=0, tiled=True),
-        lax.all_gather(bias_in, ("blk", "head"), axis=0, tiled=True),
-        lax.all_gather(bias_back, ("blk", "head"), axis=0, tiled=True),
-        lax.all_gather(first_gain, ("blk", "head"), axis=0, tiled=True),
-        lax.all_gather(first_shift, ("blk", "head"), axis=0, tiled=True),
-        lax.all_gather(second_gain, ("blk", "head"), axis=0, tiled=True),
-        lax.all_gather(second_shift, ("blk", "head"), axis=0, tiled=True),
+        lax.all_gather(w_query, GROUP, axis=0, tiled=True),
+        lax.all_gather(w_key, GROUP, axis=0, tiled=True),
+        lax.all_gather(w_value, GROUP, axis=0, tiled=True),
+        lax.all_gather(w_out, GROUP, axis=0, tiled=True),
+        lax.all_gather(w_in, GROUP, axis=0, tiled=True),
+        lax.all_gather(w_back, GROUP, axis=0, tiled=True),
+        lax.all_gather(bias_query, GROUP, axis=0, tiled=True),
+        lax.all_gather(bias_value, GROUP, axis=0, tiled=True),
+        lax.all_gather(bias_out, GROUP, axis=0, tiled=True),
+        lax.all_gather(bias_in, GROUP, axis=0, tiled=True),
+        lax.all_gather(bias_back, GROUP, axis=0, tiled=True),
+        lax.all_gather(first_gain, GROUP, axis=0, tiled=True),
+        lax.all_gather(first_shift, GROUP, axis=0, tiled=True),
+        lax.all_gather(second_gain, GROUP, axis=0, tiled=True),
+        lax.all_gather(second_shift, GROUP, axis=0, tiled=True),
     )
     query_bias = query_bias.astype(jnp.float32)
     value_bias = value_bias.astype(jnp.float32)
@@ -278,36 +1028,36 @@
         shard_s2,
     ) = (
         lax.psum_scatter(
-            inner_dot(tokens, grad_query_tok), ("blk", "head"), scatter_dimension=0, tiled=True
+            inner_dot(tokens, grad_query_tok), GROUP, scatter_dimension=0, tiled=True
         ),
         lax.psum_scatter(
-            inner_dot(tokens, grad_key_tok), ("blk", "head"), scatter_dimension=0, tiled=True
+            inner_dot(tokens, grad_key_tok), GROUP, scatter_dimension=0, tiled=True
         ),
         lax.psum_scatter(
-            inner_dot(tokens, grad_value_tok), ("blk", "head"), scatter_dimension=0, tiled=True
+            inner_dot(tokens, grad_value_tok), GROUP, scatter_dimension=0, tiled=True
         ),
-        lax.psum_scatter(grad_out, ("blk", "head"), scatter_dimension=0, tiled=True),
-        lax.psum_scatter(grad_in, ("blk", "head"), scatter_dimension=0, tiled=True),
-        lax.psum_scatter(grad_back, ("blk", "head"), scatter_dimension=0, tiled=True),
+        lax.psum_scatter(grad_out, GROUP, scatter_dimension=0, tiled=True),
+        lax.psum_scatter(grad_in, GROUP, scatter_dimension=0, tiled=True),
+        lax.psum_scatter(grad_back, GROUP, scatter_dimension=0, tiled=True),
         lax.psum_scatter(
             jnp.sum(grad_query_tok.astype(jnp.float32), (0, 1)),
-            ("blk", "head"),
+            GROUP,
             scatter_dimension=0,
             tiled=True,
         ),
         lax.psum_scatter(
             jnp.sum(grad_value_tok.astype(jnp.float32), (0, 1)),
-            ("blk", "head"),
+            GROUP,
             scatter_dimension=0,
             tiled=True,
         ),
-        lax.psum_scatter(grad_out_bias, ("blk", "head"), scatter_dimension=0, tiled=True),
-        lax.psum_scatter(grad_in_bias, ("blk", "head"), scatter_dimension=0, tiled=True),
-        lax.psum_scatter(grad_back_bias, ("blk", "head"), scatter_dimension=0, tiled=True),
-        lax.psum_scatter(grad_gain_one, ("blk", "head"), scatter_dimension=0, tiled=True),
-        lax.psum_scatter(grad_shift_one, ("blk", "head"), scatter_dimension=0, tiled=True),
-        lax.psum_scatter(grad_gain_two, ("blk", "head"), scatter_dimension=0, tiled=True),
-        lax.psum_scatter(grad_shift_two, ("blk", "head"), scatter_dimension=0, tiled=True),
+        lax.psum_scatter(grad_out_bias, GROUP, scatter_dimension=0, tiled=True),
+        lax.psum_scatter(grad_in_bias, GROUP, scatter_dimension=0, tiled=True),
+        lax.psum_scatter(grad_back_bias, GROUP, scatter_dimension=0, tiled=True),
+        lax.psum_scatter(grad_gain_one, GROUP, scatter_dimension=0, tiled=True),
+        lax.psum_scatter(grad_shift_one, GROUP, scatter_dimension=0, tiled=True),
+        lax.psum_scatter(grad_gain_two, GROUP, scatter_dimension=0, tiled=True),
+        lax.psum_scatter(grad_shift_two, GROUP, scatter_dimension=0, tiled=True),
     )
     (
         total_wq,
@@ -365,44 +1115,45 @@
 
 def solution(mesh):
     in_specs = (
-        P("dp", ("blk", "head"), None),
+        P("dp", GROUP, None),
         P("dp", "blk"),
-        P("dp", ("blk", "head"), None),
-        P(("blk", "head"), None),
-        P(("blk", "head"), None),
-        P(("blk", "head"), None),
-        P(("blk", "head"), None),
-        P(("blk", "head"), None),
-        P(("blk", "head"), None),
-        P(("blk", "head")),
-        P(("blk", "head")),
-        P(("blk", "head")),
-        P(("blk", "head")),
-        P(("blk", "head")),
-        P(("blk", "head")),
-        P(("blk", "head")),
-        P(("blk", "head")),
-        P(("blk", "head")),
+        P("dp", GROUP, None),
+        P(GROUP, None),
+        P(GROUP, None),
+        P(GROUP, None),
+        P(GROUP, None),
+        P(GROUP, None),
+        P(GROUP, None),
+        P(GROUP),
+        P(GROUP),
+        P(GROUP),
+        P(GROUP),
+        P(GROUP),
+        P(GROUP),
+        P(GROUP),
+        P(GROUP),
+        P(GROUP),
     )
     out_specs = (
-        P("dp", ("blk", "head"), None),
-        P("dp", ("blk", "head"), None),
-        P(("blk", "head"), None),
-        P(("blk", "head"), None),
-        P(("blk", "head"), None),
-        P(("blk", "head"), None),
-        P(("blk", "head"), None),
-        P(("blk", "head"), None),
-        P(("blk", "head")),
-        P(("blk", "head")),
-        P(("blk", "head")),
-        P(("blk", "head")),
-        P(("blk", "head")),
-        P(("blk", "head")),
-        P(("blk", "head")),
-        P(("blk", "head")),
-        P(("blk", "head")),
-    )
+        P("dp", GROUP, None),
+        P("dp", GROUP, None),
+        P(GROUP, None),
+        P(GROUP, None),
+        P(GROUP, None),
+        P(GROUP, None),
+        P(GROUP, None),
+        P(GROUP, None),
+        P(GROUP),
+        P(GROUP),
+        P(GROUP),
+        P(GROUP),
+        P(GROUP),
+        P(GROUP),
+        P(GROUP),
+        P(GROUP),
+        P(GROUP),
+    )
+    plan = pick_plan(mesh)
     return jax.shard_map(
-        per_device, mesh=mesh, in_specs=in_specs, out_specs=out_specs, check_vma=False
-    )
+        plan, mesh=mesh, in_specs=in_specs, out_specs=out_specs, check_vma=False
+    )

time: 1070 us -> 209 us (0.20)
  waiting for transfers between devices: 619 us -> 0 us
  blocking collectives: 209 us -> 0 us
  Pallas kernels: 0 us -> 207 us
  matrix products: 98.4 us -> 0 us
  other arithmetic: 55.4 us -> 0 us
  local copies, waits for them, and re-layouts: 54.5 us -> 0 us
  between operations: 17.2 us -> 0.83 us
    reduce_scatter x6 -> x0, waiting for transfers between devices: 398 us -> none  [the longest x1 118 us: per_device(): lax.psum_scatter(grad_in, ('blk', 'head'), scatter_dimension=0, tiled=True)]
    pallas_call x0 -> x2, Pallas kernels: none -> 207 us  [the longest x1 202 us: sharded_plan(): pl.pallas_call(partial(layer_kernel, names), out_shape=[jax.ShapeDtypeStr...]
    all_gather x10 -> x0, blocking collectives: 117 us -> none  [the longest x1 15.2 us: per_device(): lax.all_gather(bias_in, ('blk', 'head'), axis=0, tiled=True)]
    dot_general x24 -> x0, matrix products: 98.4 us -> none  [the longest x12 43 us: flat_dot(): jnp.dot(left_side.reshape(-1, left_side.shape[-1]), right_side, preferred...]
    all_gather x8 -> x0, waiting for transfers between devices: 77 us -> none  [the longest x1 31.1 us: per_device(): lax.all_gather(w_key, ('blk', 'head'), axis=0, tiled=True)]
    psum x1 -> x0, waiting for transfers between devices: 70.7 us -> none  [per_device(): lax.psum(shard_wq.astype(jnp.bfloat16), 'dp').astype(jnp.float32)]
    unnamed x17 -> x0, waiting for transfers between devices: 67.6 us -> none
    all_to_all x6 -> x0, blocking collectives: 53.5 us -> none  [the longest x1 10.5 us: per_device(): lax.all_to_all(key_tok, 'head', split_axis=2, concat_axis=1, tiled=True)]
  transfers between devices with their start and end apart: 18 -> 0, of which waited for: 13 -> 0; matrix products, arithmetic and copies ran while one was open for 10% -> 0% of each run, Pallas kernels for 0% -> 0%
where the time goes in v2:
time: 209 us; the launch traced here: 208 us
  Pallas kernels  207 us (99%)
    pallas_call x1, Pallas kernels, sharded_plan(): pl.pallas_call(partial(layer_kernel, names), out_shape=[jax.ShapeDtypeStr...  202 us
    pallas_call x1, Pallas kernels, sharded_plan(): pl.pallas_call(finish_kernel, grid=(grid,), out_shape=[jax.ShapeDtypeStru...  5.5 us

profile of v2, /device:TPU:0, one launch (start us, length us, event | category | flops | bytes accessed | tf_op | source)
XLA Modules:
  0.0 208.3 jit_solution(4275330888403326491)
XLA Ops:
  0.7 202.0 %layer.1 = (bf16[128,1024]{1,0:T(8,128)(2,1)}, f32[128,1024]{1,0:T(8,128)}, bf16[4,128,1024]{2,1,0:T(8,128)(2,1)}, bf16[8,128,512]{2,1,0:T(8,128)(2,1)}, bf16[12...) custom-call(bf16[128,1024]{1,0:T(8,128)(2,1)} %bitcast.4, bf16[128,1024]{1,0:T(8,128)(2,1)} %bitcast.5, ...), custom_call_target="tpu_custom_call" | custom-call | tf_op jit(solution)/shard_map/layer/pallas_call | solution.py:696
  202.7 5.5 %finish.1 = (bf16[128,1024]{1,0:T(8,128)(2,1)}, f32[128,1024]{1,0:T(8,128)}, f32[128,1024]{1,0:T(8,128)}, f32[128,1024]{1,0:T(8,128)}, f32[128,1024]{1,0:T(8,128...) custom-call(bf16[128,1024]{1,0:T(8,128)(2,1)} %get-tuple-element.41., ...), custom_call_target="tpu_custom_call" | custom-call | tf_op jit(solution)/shard_map/finish/pallas_call | solution.py:717

commit v3 on v2

--- a/solution.py
+++ b/solution.py
@@ -36,6 +36,12 @@
     return jnp.sum(x.astype(F32), 0, keepdims=True)
 
 
+def when(cond):
+    if isinstance(cond, bool):
+        return (lambda body: body()) if cond else (lambda body: None)
+    return pl.when(cond)
+
+
 def rows(ref):
     x = ref[...]
     return x.reshape(-1, x.shape[-1])
@@ -111,31 +117,32 @@
         (ag_relay(buf, r, h) if p == by_both else ag_direct(buf, r, p, h)).wait_recv()
         ag_forward(buf, r, p, h).start()
 
-    def ag_wait(buf, r, p):
-        @pl.when(p == 0)
+    def ag_wait(buf, r, p, relayed=lambda: None):
+        @when(p == 0)
         def _():
             ag_home(buf, r).wait_recv()
 
-        @pl.when(p == by_y)
+        @when(p == by_y)
         def _():
             ag_got(buf, r, by_x, 0)
             ag_relay(buf, r, 0).start()
             ag_got(buf, r, by_y, 1)
             ag_relay(buf, r, 1).start()
+            relayed()
             ag_got(buf, r, by_y, 0)
+            ag_got(buf, r, by_x, 1)
             for h in (0, 1):
                 ag_forward(buf, r, by_y, h).wait_recv()
 
-        @pl.when(p == by_x)
-        def _():
-            ag_got(buf, r, by_x, 1)
+        @when(p == by_x)
+        def _():
+            ag_got(buf, r, by_both, 0)
+            ag_got(buf, r, by_both, 1)
             for h in (0, 1):
                 ag_forward(buf, r, by_x, h).wait_recv()
 
-        @pl.when(p == by_both)
-        def _():
-            ag_got(buf, r, by_both, 0)
-            ag_got(buf, r, by_both, 1)
+        @when(p == by_both)
+        def _():
             for h in (0, 1):
                 ag_forward(buf, r, by_both, h).wait_recv()
 
@@ -173,15 +180,15 @@
         R.keep[p] = both
         R.snd_l[p] = both.astype(BF)
 
-        @pl.when(p == by_y)
+        @when(p == by_y)
         def _():
             rs_link(r, by_y, 1).start()
 
-        @pl.when(p == by_x)
+        @when(p == by_x)
         def _():
             rs_link(r, by_x, 0).start()
 
-        @pl.when(p == by_both)
+        @when(p == by_both)
         def _():
             rs_link(r, by_both, 0).start()
             rs_link(r, by_both, 1).start()
@@ -206,18 +213,17 @@
                     rs_link(r, p, h).wait_send()
         return acc
 
-    zbufs = {
-        "b": [(lambda x, i=i: x.at[i]) for i in range(4)],
-        "i": [(lambda x, i=i: x.at[pl.ds(2 * i, 2)]) for i in range(4)],
-        "o": [lambda x: x],
-        "s": [lambda x: x],
-        "w": [(lambda x, i=i: x.at[i]) for i in range(8)],
-    }
-    chunks = [(k, cut) for k in zbufs for cut in zbufs[k]]
-    Z_IN, Z_OUT, Z_SMALL, Z_QKV, Z_ALL = 4, 8, 9, 10, 18
+    quarter = (pl.ds(0, T // 4), pl.ds(T // 4, T // 4))
+    chunks = [("b", lambda x, q=q: x.at[0, q], T // 4) for q in quarter] + [("b", lambda x: x.at[0, half[1]], T // 2)]
+    chunks += [("b", lambda x, i=i, h=h: x.at[i, h], T // 2) for i in range(1, 4) for h in half]
+    chunks += [("i", lambda x, t=t: x.at[t], T // 2) for t in range(8)]
+    chunks += [("o", lambda x, h=h: x.at[h], T // 2) for h in half] + [("s", lambda x: x, 1)]
+    chunks += [("w", lambda x, t=t: x.at[t], 3 * T // 8) for t in range(7)]
+    chunks += [("w", lambda x, h=h: x.at[7, h], 3 * T // 16) for h in half]
+    Z_IN, Z_OUT, Z_SMALL, Z_QKV, Z_ALL = 9, 17, 19, 20, len(chunks)
 
     def zrefs(c):
-        k, cut = chunks[c]
+        k, cut, _ = chunks[c]
         return cut(getattr(R, "zown_" + k)), cut(getattr(R, "zsum_" + k)), cut(getattr(R, "zmid_" + k))
 
     def z_up(c):
@@ -232,7 +238,22 @@
         _, tot, _ = zrefs(c)
         return rcopy(tot, tot, R.z_s.at[c, 1], R.z_r.at[c, 0], (z_other, blk, head))
 
+    row_us, hop_us = 0.0432, 2.0
+    steps, sent = [], 0.0
+    for c, (_, _, n) in enumerate(chunks):
+        sent += n * row_us
+        steps += [(sent + hop_us, c, 0), (sent + n * row_us + 2.2 * hop_us, c, 1)]
+    steps.sort()
+    made = set()
+
+    def z_until(us):
+        while steps and steps[0][0] <= us and steps[0][1] in made:
+            _, c, second = steps.pop(0)
+            (z_two if second else z_one)(c)
+
     def z_produce(c):
+        made.add(c)
+
         @pl.when(z_end)
         def _():
             z_up(c).start()
@@ -257,7 +278,8 @@
         @pl.when(z_end)
         def _():
             z_up(c).wait_send()
-            z_down(c).wait_recv()
+            if not Z_IN <= c < Z_OUT:
+                z_down(c).wait_recv()
 
         @pl.when(jnp.logical_not(z_end))
         def _():
@@ -322,6 +344,12 @@
 
     def qkv_step(p, carry):
         ag_wait(tok_all, 0, p)
+
+        @when(p == by_y)
+        def _():
+            for e in far_first:
+                win_copy(e).start()
+
         a, b, x = pair(tok_all, p)
         y = mm(x, rows(R.wqkv), NN)
         qq = ((y[:, :W] + R.bq[...].astype(F32).reshape(1, W)) * 0.125).astype(BF)
@@ -333,8 +361,6 @@
 
     with jax.named_scope("project_qkv"):
         lax.fori_loop(0, 4, qkv_step, 0)
-    for e in far_first:
-        win_copy(e).start()
     for i in (1, 2, 3, 4):
         local[i].wait()
 
@@ -355,22 +381,23 @@
         allowed = jnp.concatenate([segk, segk], 1) == segq
         kk = rows(R.k)
         outs = []
+        scores = [mm(kk, head_mask(h, qp), NT) for h in range(heads)]
         for h in range(heads):
-            s = jnp.where(allowed, mm(kk, head_mask(h, qp), NT), -1e30)
+            s = jnp.where(allowed, scores[h], -1e30)
             ex = jnp.exp(s - jnp.max(s, 0, keepdims=True))
             total = jnp.maximum(jnp.sum(ex, 0, keepdims=True), 1.0)
             pt = (ex * jnp.where(segq >= 0, 1.0 / total, 0.0)).astype(BF)
             R.pt[h, p] = pt
             outs.append(mm(R.vt[h * HD:(h + 1) * HD, :], pt, NN))
+            if h == 0:
+                @pl.when(p < 3)
+                def _():
+                    rs_combine(0, p + 1)
+
         ct = jnp.concatenate(outs, 0).astype(BF)
         R.ctxt[:, lanes(a, T)] = ct[:, :T]
         R.ctxt[:, lanes(b, T)] = ct[:, T:]
         rs_put(0, p, mm(ct, R.wo_v[...], TN))
-
-        @pl.when(p < 3)
-        def _():
-            rs_combine(0, p + 1)
-
         return carry
 
     with jax.named_scope("attend"):
@@ -395,6 +422,10 @@
 
     def hidden_step(p, carry):
         ag_wait(y1_all, 1, p)
+
+        @pl.when(p > 1)
+        def _():
+            rs_combine(1, p - 1)
         a, b, x = pair(y1_all, p)
         z = hidden_in(x)
         cdf = 0.5 * (1.0 + lax.erf(z * 0.7071067811865476))
@@ -403,10 +434,6 @@
         R.hid[a], R.hid[b] = low[:T], low[T:]
         R.slope[a], R.slope[b] = slope[:T], slope[T:]
         rs_put(1, p, mm(low, R.wb_v[...], NN))
-
-        @pl.when(p > 1)
-        def _():
-            rs_combine(1, p - 1)
 
         return carry
 
@@ -432,18 +459,29 @@
         R.sv[0:1, :] = colsum(cot * n2)
         R.sv[1:2, :] = colsum(cot)
 
+    def grad_back(i):
+        x = R.hid[:, :, i * T:(i + 1) * T].reshape(8 * T, T)
+        R.zown_b[i] = mm(x, rows(df_all), TN).astype(BF)
+        for c in range(3) if i == 0 else (2 * i + 1, 2 * i + 2):
+            z_produce(c)
+
     def hidden_back_step(p, carry):
         ag_wait(df_all, 2, p)
+
+        @pl.when(p > 1)
+        def _():
+            rs_combine(2, p - 1)
+
+        @when(p == by_both)
+        def _():
+            grad_back(0)
+
         a, b, x = pair(df_all, p)
         slope = jnp.concatenate([R.slope[a], R.slope[b]], 0)
         dz = (mm(x, R.wb_v[...], NT) * slope).astype(BF)
         R.dz[a], R.dz[b] = dz[:T], dz[T:]
         rs_put(2, p, mm(dz, rows(R.win), NT))
 
-        @pl.when(p > 1)
-        def _():
-            rs_combine(2, p - 1)
-
         return carry
 
     with jax.named_scope("hidden_back"):
@@ -451,37 +489,40 @@
         rs_combine(2, c32(3))
 
     with jax.named_scope("grad_back"):
+        for i in range(1, 4):
+            grad_back(i)
+        z_until(6.0)
+        rs_relay(2)
+        z_until(7.5)
+
+    def grad_in(i):
+        x = y1_all[:, :, 2 * i * T:(2 * i + 2) * T].reshape(8 * T, 2 * T)
+        g = mm(x, rows(R.dz), TN).astype(BF)
+        R.zown_i[2 * i], R.zown_i[2 * i + 1] = g[:T], g[T:]
+        z_produce(Z_IN + 2 * i)
+        z_produce(Z_IN + 2 * i + 1)
+
+    def din_copy(t, s):
+        return rcopy(R.zsum_i.at[t], R.grad_i.at[s], R.din_s.at[t], R.din_r.at[s], (dp, t // 2, t % 2))
+
+    def z_deliver(t):
+        @pl.when(z_end)
+        def _():
+            z_down(Z_IN + t).wait_recv()
+
+        @pl.when(me != t)
+        def _():
+            din_copy(t, me).start()
+
+        @pl.when(me == t)
+        def _():
+            R.grad_i[me] = R.zsum_i[t]
+
+    with jax.named_scope("grad_in"):
         for i in range(4):
-            g = mm(R.hid[:, :, i * T:(i + 1) * T].reshape(8 * T, T), rows(df_all), TN)
-            R.zown_b[i] = g.astype(BF)
-            z_produce(i)
-        rs_relay(2)
-
-    def din_copy(p, flip):
-        to, at = dev(p, flip)
-        return rcopy(R.din_snd.at[at], R.zown_i.at[me], R.din_s.at[p, flip], R.din_r.at[p, flip], to)
-
-    def din_step(p, carry):
-        a, b = dev(p, 0)[1], dev(p, 1)[1]
-        x = jnp.concatenate([y1_all[:, :, lanes(a, T)], y1_all[:, :, lanes(b, T)]], 2).reshape(8 * T, 2 * T)
-        g = mm(x, rows(R.dz), TN).astype(BF)
-        R.din_snd[b] = g[T:]
-        din_copy(p, 1).start()
-
-        @pl.when(p == 0)
-        def _():
-            R.zown_i[me] = g[:T]
-
-        @pl.when(p > 0)
-        def _():
-            R.din_snd[a] = g[:T]
-            din_copy(p, 0).start()
-
-        return carry
-
-    with jax.named_scope("grad_in"):
-        lax.fori_loop(0, 4, din_step, 0)
-    z_one(0)
+            grad_in(i)
+            if i % 2:
+                z_until(8.0 + i)
 
     with jax.named_scope("first_norm_back"):
         rs = rs_final(2)
@@ -501,26 +542,16 @@
     for e in far_first:
         sv_copy(e).start()
     R.sv_rcv[me] = R.sv[:, lanes(me, T)]
-    z_one(1)
-    z_two(0)
-
-    def z_service(p):
-        @pl.when(p == 1)
-        def _():
-            z_one(2)
-            z_two(1)
-
-        @pl.when(p == 3)
-        def _():
-            z_one(3)
-            z_two(2)
+
+    z_until(12.0)
 
     R.dk[...] = jnp.zeros_like(R.dk)
     R.dv[...] = jnp.zeros_like(R.dv)
 
-    def attend_back_step(p, carry):
-        ag_wait(da_all, 3, p)
-        a, b, x = pair(da_all, p)
+    def attend_back_step(p):
+        ag_wait(da_all, 3, p, lambda: z_until(17.0))
+        z_until((13.8, 20.0, 23.0, 25.8)[p])
+        a, b, x = pair(da_all, c32(p))
         qp = jnp.concatenate([R.q[a], R.q[b]], 0)
         dc = mm(x, R.wo_v[...], NT).astype(BF)
         vv = rows(R.v)
@@ -534,14 +565,14 @@
             outs.append(mm(R.kt[h * HD:(h + 1) * HD, :], ds, NN))
             R.dk[...] += mm(ds, qm, NN)
             R.dv[...] += mm(low, dcm, NN)
+            z_until((14.8, 21.0, 24.0, 26.8)[p] + h)
         dq = jnp.concatenate(outs, 0).T.astype(BF) * 0.125
         R.dqkv[a, :, 0:W] = dq[:T]
         R.dqkv[b, :, 0:W] = dq[T:]
-        z_service(p)
-        return carry
 
     with jax.named_scope("attend_back"):
-        lax.fori_loop(0, 4, attend_back_step, 0)
+        for p in range(4):
+            attend_back_step(p)
         R.dqkv[:, :, W:2 * W] = R.dk[...].astype(BF).reshape(8, T, W)
         R.dqkv[:, :, 2 * W:] = R.dv[...].astype(BF).reshape(8, T, W)
 
@@ -549,54 +580,41 @@
         to, at = dev(p, flip)
         return rcopy(R.dqkv_snd.at[at], R.zown_w.at[me], R.dqkv_s.at[p, flip], R.dqkv_r.at[p, flip], to)
 
-    def dqkv_step(p, carry):
-        a, b = dev(p, 0)[1], dev(p, 1)[1]
+    def dqkv_step(p):
+        a, b = dev(c32(p), 0)[1], dev(c32(p), 1)[1]
         x = jnp.concatenate([tok_all[:, :, lanes(a, T)], tok_all[:, :, lanes(b, T)]], 2).reshape(8 * T, 2 * T)
         g = mm(x, rows(R.dqkv), TN).astype(BF)
         R.dqkv_snd[b] = g[T:]
-        dqkv_copy(p, 1).start()
-
-        @pl.when(p == 0)
-        def _():
+        dqkv_copy(c32(p), 1).start()
+        if p == 0:
             R.zown_w[me] = g[:T]
-
-        @pl.when(p > 0)
-        def _():
+        else:
             R.dqkv_snd[a] = g[:T]
-            dqkv_copy(p, 0).start()
-
-        return carry
+            dqkv_copy(c32(p), 0).start()
+        z_until(28.3 + 0.5 * p)
 
     with jax.named_scope("grad_qkv"):
-        lax.fori_loop(0, 4, dqkv_step, 0)
+        for p in range(4):
+            dqkv_step(p)
 
     with jax.named_scope("grad_out"):
-        for p in range(4):
-            for flip in (0, 1):
-                if (p, flip) != (0, 0):
-                    din_copy(c32(p), flip).wait_recv()
-        for c in range(Z_IN, Z_OUT):
-            z_produce(c)
         R.zown_o[...] = mm(R.ctxt[...], rows(da_all), NN).astype(BF)
         z_produce(Z_OUT)
-        z_one(4)
-        z_two(3)
-
-    def input_step(p, carry):
-        a, b, x = pair(R.dqkv, p)
+        z_produce(Z_OUT + 1)
+        z_until(31.0)
+
+    def input_step(p):
+        if p > 1:
+            rs_combine(3, p - 1)
+        a, b, x = pair(R.dqkv, c32(p))
         rs_put(3, p, mm(x, rows(R.wqkv), NT))
-
-        @pl.when(p > 1)
-        def _():
-            rs_combine(3, p - 1)
-
-        return carry
+        z_until((30.8, 31.4, 32.8, 34.4)[p])
 
     with jax.named_scope("input_back"):
-        lax.fori_loop(0, 4, input_step, 0)
+        for p in range(4):
+            input_step(p)
         rs_combine(3, c32(3))
-        z_one(5)
-        z_two(4)
+        z_until(36.5)
 
     with jax.named_scope("small_grads"):
         for e in range(1, 8):
@@ -617,28 +635,33 @@
         parts.append(jnp.zeros((16 - 8 - FW // T, T), F32))
         R.zown_s[...] = jnp.concatenate(parts, 0).astype(BF)
         z_produce(Z_SMALL)
-        rs_relay(3)
+        z_until(39.0)
 
     with jax.named_scope("z_rest"):
-        z_one(6)
-        z_two(5)
         for p in range(4):
             for flip in (0, 1):
                 if (p, flip) != (0, 0):
                     dqkv_copy(c32(p), flip).wait_recv()
         for c in range(Z_QKV, Z_ALL):
             z_produce(c)
+        z_until(42.0)
+        rs_relay(3)
+        z_until(46.0)
     with jax.named_scope("input_grad"):
         R.igrad[...] = R.dh1[...] + rs_final(3)
     with jax.named_scope("z_last"):
-        for c in range(7, Z_ALL):
-            z_one(c)
-            z_two(c - 1)
-        z_two(Z_ALL - 1)
+        for t in range(8):
+            z_until(49.0 + 2 * t)
+            z_deliver(t)
+        z_until(1000.0)
 
     with jax.named_scope("finish"):
         for c in range(Z_ALL):
             z_finish(c)
+        for t in range(8):
+            @pl.when(me != t)
+            def _():
+                din_copy(t, t).wait()
         for buf, r in ((tok_all, 0), (y1_all, 1), (df_all, 2), (da_all, 3)):
             ag_finish(buf, r)
         for e in range(1, 8):
@@ -647,7 +670,6 @@
             sv_copy(e).wait_send()
             for j in range(3):
                 qkv_copy(e, j).wait_send()
-            din_copy(c32(e // 2), e % 2).wait_send()
             dqkv_copy(c32(e // 2), e % 2).wait_send()
 
 
@@ -667,8 +689,8 @@
     )
     in_hbm = 8
     outs = dict(
-        out=((T, D), BF), igrad=((T, D), F32), zsum_b=((4, T, D), BF), zsum_i=((8, T, FW), BF),
-        zsum_o=((T, D), BF), zsum_w=((8, T, 3 * W), BF), zsum_s=((16, T), BF),
+        out=((T, D), BF), igrad=((T, D), F32), zsum_b=((4, T, D), BF),
+        grad_i=((8, T, FW), BF), zsum_o=((T, D), BF), zsum_w=((8, T, 3 * W), BF), zsum_s=((16, T), BF),
     )
     blocks = {k: ((8, T, D), BF) for k in ("tok_all", "y1_all", "df_all", "da_all")}
     scr = dict(
@@ -683,14 +705,15 @@
         keep=((4, T, D), F32), snd_c=((4, T, D), BF), snd_l=((4, T, D), BF),
         rcv_c=((4, 4, T, D), BF), rcv_l=((4, 4, T, D), BF),
         dk=((8 * T, W), F32), dv=((8 * T, W), F32), dqkv=((8, T, 3 * W), BF),
-        din_snd=((8, T, FW), BF), dqkv_snd=((8, T, 3 * W), BF),
+        dqkv_snd=((8, T, 3 * W), BF),
         **{z + k[4:]: s for z in ("zown", "zmid") for k, s in outs.items() if k.startswith("zsum")},
+        **{k: ((8, T, FW), BF) for k in ("zown_i", "zmid_i", "zsum_i")},
     )
     sems = dict(
         ag_s=(4, 4, 2), ag_r=(4, 4, 2), ag_fs=(4, 4, 2), ag_f=(4, 4, 2),
         rs_cs=(4, 4), rs_cr=(4, 4), rs_ls=(4, 4, 2), rs_lr=(4, 4, 2),
-        z_s=(18, 2), z_r=(18, 2), loc=(8,), vec_s=(8,), vec_r=(8,), qkv_s=(8, 3), qkv_r=(8, 3), win_s=(8,), win_r=(8,),
-        sv_s=(8,), sv_r=(8,), din_s=(4, 2), din_r=(4, 2), dqkv_s=(4, 2), dqkv_r=(4, 2),
+        z_s=(29, 2), z_r=(29, 2), loc=(8,), vec_s=(8,), vec_r=(8,), qkv_s=(8, 3), qkv_r=(8, 3), win_s=(8,), win_r=(8,),
+        sv_s=(8,), sv_r=(8,), din_s=(8,), din_r=(8,), dqkv_s=(4, 2), dqkv_r=(4, 2),
     )
     names = list(ins) + list(outs) + list(scr) + list(sems)
     res = pl.pallas_call(

time: 209 us -> 181 us (0.87)
  Pallas kernels: 207 us -> 180 us
    pallas_call x1, Pallas kernels: 202 us -> 174 us  [sharded_plan(): pl.pallas_call(partial(layer_kernel, names), out_shape=[jax.ShapeDtypeStr...]
where the time goes in v3:
time: 181 us
  Pallas kernels  180 us (99%)
    pallas_call x1, Pallas kernels, sharded_plan(): pl.pallas_call(partial(layer_kernel, names), out_shape=[jax.ShapeDtypeStr...  174 us
    pallas_call x1, Pallas kernels, sharded_plan(): pl.pallas_call(finish_kernel, grid=(grid,), out_shape=[jax.ShapeDtypeStru...  5.5 us

profile of v3, /device:TPU:0, one launch (start us, length us, event | category | flops | bytes accessed | tf_op | source)
XLA Modules:
  0.0 180.6 jit_solution(12404609991897689393)
XLA Ops:
  0.7 174.3 %layer.1 = (bf16[128,1024]{1,0:T(8,128)(2,1)}, f32[128,1024]{1,0:T(8,128)}, bf16[4,128,1024]{2,1,0:T(8,128)(2,1)}, bf16[8,128,512]{2,1,0:T(8,128)(2,1)}, bf16[12...) custom-call(bf16[128,1024]{1,0:T(8,128)(2,1)} %bitcast.4, bf16[128,1024]{1,0:T(8,128)(2,1)} %bitcast.5, ...), custom_call_target="tpu_custom_call" | custom-call | tf_op jit(solution)/shard_map/layer/pallas_call | solution.py:719
  175.0 5.5 %finish.1 = (bf16[128,1024]{1,0:T(8,128)(2,1)}, f32[128,1024]{1,0:T(8,128)}, f32[128,1024]{1,0:T(8,128)}, f32[128,1024]{1,0:T(8,128)}, f32[128,1024]{1,0:T(8,128...) custom-call(bf16[128,1024]{1,0:T(8,128)(2,1)} %get-tuple-element.41., ...), custom_call_target="tpu_custom_call" | custom-call | tf_op jit(solution)/shard_map/finish/pallas_call | solution.py:740

commit v4 on v3

--- a/solution.py
+++ b/solution.py
@@ -72,8 +72,32 @@
     def rcopy(src, dst, ssem, rsem, to):
         return pltpu.make_async_remote_copy(src, dst, ssem, rsem, device_id=to, device_id_type=MESH)
 
+    def all_of(ref, ssem, rsem):
+        return rcopy(ref, ref, ssem, rsem, partner)
+
+    seven = pl.ds(0, 7)
+
     def lanes(i, w):
         return pl.ds(pl.multiple_of(i * w, w), w)
+
+    tok_all, y1_all, df_all, da_all = R.tok_all, R.y1_all, R.df_all, R.da_all
+    small_in = (R.ids, R.bo, R.bb, R.g1, R.s1, R.g2, R.s2, R.bq, R.bv, R.bi)
+    small_v = (R.ids_v, R.bo_v, R.bb_v, R.g1_v, R.s1_v, R.g2_v, R.s2_v, R.bq_v, R.bv_v, R.bi_v)
+    local = [
+        pltpu.make_async_copy(R.tok, tok_all.at[me], R.loc.at[0]),
+        pltpu.make_async_copy(R.wb, R.wb_v, R.loc.at[1]),
+        pltpu.make_async_copy(R.wo, R.wo_v, R.loc.at[2]),
+        pltpu.make_async_copy(R.wi.at[:, lanes(me, FW)], R.win.at[me], R.loc.at[3]),
+        pltpu.make_async_copy(R.cot, R.cot_v, R.loc.at[4]),
+    ]
+    for j, w in enumerate((R.wq, R.wk, R.wv)):
+        local.append(pltpu.make_async_copy(w.at[:, lanes(me, W)], R.wqkv.at[me, :, pl.ds(j * W, W)], R.loc.at[5]))
+    small = [
+        pltpu.make_async_copy(x, y, R.small_s.at[i])
+        for i, (x, y) in enumerate(zip(small_in, small_v, strict=True))
+    ]
+    for cp in local + small:
+        cp.start()
 
     bar = pltpu.get_barrier_semaphore()
     for e in range(1, 8):
@@ -83,28 +107,31 @@
         pl.semaphore_signal(bar, 1, device_id=(lax.rem(dp + j, 4), blk, head), device_id_type=MESH)
     pl.semaphore_wait(bar, 10)
 
+    put_out = pltpu.make_async_copy(R.out_v, R.out, R.put_s.at[0])
+    put_igrad = pltpu.make_async_copy(R.igrad_v, R.igrad, R.put_s.at[1])
+
     half = (pl.ds(0, T // 2), pl.ds(T // 2, T // 2))
     by_y, by_x, by_both = 1, 2, 3
 
     def ag_direct(buf, r, p, h):
         to, _ = dev(c32(p), 0)
         part = buf.at[me, half[h]]
-        return rcopy(part, part, R.ag_s.at[r, p, h], R.ag_r.at[r, p, h], to)
+        return rcopy(part, part, R.ag_s.at[r], R.ag_r.at[p, h], to)
 
     def ag_relay(buf, r, h):
         via, over = (by_x, by_y) if h == 0 else (by_y, by_x)
         _, at = dev(c32(via), 0)
         to, _ = dev(c32(over), 0)
         part = buf.at[at, half[h]]
-        return rcopy(part, part, R.ag_s.at[r, by_both, h], R.ag_r.at[r, by_both, h], to)
+        return rcopy(part, part, R.ag_s.at[r], R.ag_r.at[by_both, h], to)
 
     def ag_home(buf, r):
-        return rcopy(buf.at[me], buf.at[me], R.ag_fs.at[r, 0, 0], R.ag_f.at[r, 0, 0], partner)
+        return rcopy(buf.at[me], buf.at[me], R.ag_s.at[r], R.ag_f.at[0, 0], partner)
 
     def ag_forward(buf, r, p, h):
         _, at = dev(c32(p), 0)
         part = buf.at[at, half[h]]
-        return rcopy(part, part, R.ag_fs.at[r, p, h], R.ag_f.at[r, p, h], partner)
+        return rcopy(part, part, R.ag_s.at[r], R.ag_f.at[p, h], partner)
 
     def ag_start(buf, r):
         ag_direct(buf, r, by_x, 0).start()
@@ -147,26 +174,20 @@
                 ag_forward(buf, r, by_both, h).wait_recv()
 
     def ag_finish(buf, r):
-        ag_home(buf, r).wait_send()
-        for h in (0, 1):
-            ag_direct(buf, r, by_x, h).wait_send()
-            ag_direct(buf, r, by_y, h).wait_send()
-            ag_relay(buf, r, h).wait_send()
-            for p in (by_y, by_x, by_both):
-                ag_forward(buf, r, p, h).wait_send()
+        all_of(buf.at[seven], R.ag_s.at[r], R.ag_r.at[0, 0]).wait_send()
 
     def pair(buf, p):
         a, b = dev(p, 0)[1], dev(p, 1)[1]
         return a, b, jnp.concatenate([buf[a], buf[b]], 0)
 
     def rs_chip(r, p):
-        return rcopy(R.snd_c.at[p], R.rcv_c.at[r, p], R.rs_cs.at[r, p], R.rs_cr.at[r, p], partner)
+        return rcopy(R.snd_c.at[p], R.rcv_c.at[r, p], R.rs_s.at[0], R.rs_cr.at[p], partner)
 
     def rs_link(r, p, h):
         over = p if p != by_both else (by_x, by_y)[h]
         to, _ = dev(c32(over), 0)
         return rcopy(
-            R.snd_l.at[p, half[h]], R.rcv_l.at[r, p, half[h]], R.rs_ls.at[r, p, h], R.rs_lr.at[r, p, h], to
+            R.snd_l.at[p, half[h]], R.rcv_l.at[r, p, half[h]], R.rs_s.at[1], R.rs_lr.at[p, h], to
         )
 
     def rs_put(r, p, part):
@@ -206,11 +227,8 @@
             for h in (0, 1):
                 rs_link(r, p, h).wait_recv()
             acc = acc + R.rcv_l[r, p].astype(F32)
-        for p in range(4):
-            rs_chip(r, c32(p)).wait_send()
-            if p:
-                for h in (0, 1):
-                    rs_link(r, p, h).wait_send()
+        all_of(R.snd_c, R.rs_s.at[0], R.rs_cr.at[0]).wait_send()
+        all_of(R.snd_l.at[pl.ds(1, 3)], R.rs_s.at[1], R.rs_cr.at[0]).wait_send()
         return acc
 
     quarter = (pl.ds(0, T // 4), pl.ds(T // 4, T // 4))
@@ -226,17 +244,22 @@
         k, cut, _ = chunks[c]
         return cut(getattr(R, "zown_" + k)), cut(getattr(R, "zsum_" + k)), cut(getattr(R, "zmid_" + k))
 
+    kinds = "biosw"
+
+    def z_sem(c, way):
+        return R.z_s.at[kinds.index(chunks[c][0]), way]
+
     def z_up(c):
         own, tot, _ = zrefs(c)
-        return rcopy(own, tot, R.z_s.at[c, 0], R.z_r.at[c, 0], (z_other, blk, head))
+        return rcopy(own, tot, z_sem(c, 0), R.z_r.at[c, 0], (z_other, blk, head))
 
     def z_across(c):
         own, _, mid = zrefs(c)
-        return rcopy(own, mid, R.z_s.at[c, 0], R.z_r.at[c, 1], (z_mid, blk, head))
+        return rcopy(own, mid, z_sem(c, 0), R.z_r.at[c, 1], (z_mid, blk, head))
 
     def z_down(c):
         _, tot, _ = zrefs(c)
-        return rcopy(tot, tot, R.z_s.at[c, 1], R.z_r.at[c, 0], (z_other, blk, head))
+        return rcopy(tot, tot, z_sem(c, 1), R.z_r.at[c, 0], (z_other, blk, head))
 
     row_us, hop_us = 0.0432, 2.0
     steps, sent = [], 0.0
@@ -277,90 +300,79 @@
     def z_finish(c):
         @pl.when(z_end)
         def _():
-            z_up(c).wait_send()
             if not Z_IN <= c < Z_OUT:
                 z_down(c).wait_recv()
 
-        @pl.when(jnp.logical_not(z_end))
-        def _():
-            z_across(c).wait_send()
-            z_down(c).wait_send()
-
-    tok_all, y1_all, df_all, da_all = R.tok_all, R.y1_all, R.df_all, R.da_all
-    local = [
-        pltpu.make_async_copy(R.tok, tok_all.at[me], R.loc.at[0]),
-        pltpu.make_async_copy(R.wb, R.wb_v, R.loc.at[1]),
-        pltpu.make_async_copy(R.wo, R.wo_v, R.loc.at[2]),
-        pltpu.make_async_copy(R.wi.at[:, lanes(me, FW)], R.win.at[me], R.loc.at[3]),
-        pltpu.make_async_copy(R.cot, R.cot_v, R.loc.at[4]),
-    ]
-    for j, w in enumerate((R.wq, R.wk, R.wv)):
-        local.append(pltpu.make_async_copy(w.at[:, lanes(me, W)], R.wqkv.at[me, :, pl.ds(j * W, W)], R.loc.at[5 + j]))
-    for cp in local:
-        cp.start()
-    vecs = [x[...].astype(F32).reshape(1, T) for x in (R.bo, R.bb, R.g1, R.s1, R.g2, R.s2)]
-    vecs.append(R.ids[0:1, lanes(head, T)].astype(F32))
-    R.vec[...] = jnp.concatenate(vecs + [jnp.zeros((1, T), F32)], 0)
-    R.vec_all[me] = R.vec[...]
+    def z_sent():
+        for i, k in enumerate(kinds):
+            own, tot = getattr(R, "zown_" + k), getattr(R, "zsum_" + k)
+            all_of(own, R.z_s.at[i, 0], R.z_r.at[0, 0]).wait_send()
+
+            @pl.when(jnp.logical_not(z_end))
+            def _():
+                all_of(tot, R.z_s.at[i, 1], R.z_r.at[0, 0]).wait_send()
 
     def vec_copy(e):
         to, _ = dev(c32(e // 2), e % 2)
-        return rcopy(R.vec, R.vec_all.at[me], R.vec_s.at[e], R.vec_r.at[e], to)
+        return rcopy(R.vec, R.vec_all.at[me], R.vec_s.at[0], R.vec_s.at[1], to)
 
     def qkv_copy(e, j):
         to, at = dev(c32(e // 2), e % 2)
         w = (R.wq, R.wk, R.wv)[j]
-        return rcopy(w.at[:, lanes(at, W)], R.wqkv.at[me, :, pl.ds(j * W, W)], R.qkv_s.at[e, j], R.qkv_r.at[e, j], to)
+        return rcopy(w.at[:, lanes(at, W)], R.wqkv.at[me, :, pl.ds(j * W, W)], R.qkv_s.at[0], R.qkv_s.at[1], to)
 
     def win_copy(e):
         to, at = dev(c32(e // 2), e % 2)
-        return rcopy(R.wi.at[:, lanes(at, FW)], R.win.at[me], R.win_s.at[e], R.win_r.at[e], to)
+        return rcopy(R.wi.at[:, lanes(at, FW)], R.win.at[me], R.win_s.at[0], R.win_s.at[1], to)
 
     far_first = (6, 7, 2, 3, 4, 5, 1)
     with jax.named_scope("start_copies"):
-        for e in far_first:
-            vec_copy(e).start()
         for e in far_first:
             for j in range(3):
                 qkv_copy(e, j).start()
         local[0].wait()
         ag_start(tok_all, 0)
+        for cp in small:
+            cp.wait()
+        vecs = [x[...].astype(F32).reshape(1, T) for x in small_v[1:7]]
+        vecs.append(R.ids_v[0:1, lanes(head, T)].astype(F32))
+        R.vec[...] = jnp.concatenate(vecs + [jnp.zeros((1, T), F32)], 0)
+        R.vec_all[me] = R.vec[...]
+        for e in far_first:
+            vec_copy(e).start()
+
+    with jax.named_scope("wait_qkv_weights"):
+        all_of(R.wqkv.at[seven], R.qkv_s.at[0], R.qkv_s.at[1]).wait_recv()
+        pltpu.make_async_copy(R.wqkv.at[me], R.wqkv.at[me], R.loc.at[5]).wait()
+
+    def qkv_step(p, carry):
+        ag_wait(tok_all, 0, p)
+
+        @when(p == by_y)
+        def _():
+            for e in far_first:
+                win_copy(e).start()
+
+        a, b, x = pair(tok_all, p)
+        y = mm(x, rows(R.wqkv), NN)
+        qq = ((y[:, :W] + R.bq_v[...].astype(F32).reshape(1, W)) * 0.125).astype(BF)
+        kk = y[:, W:2 * W].astype(BF)
+        vv = (y[:, 2 * W:] + R.bv_v[...].astype(F32).reshape(1, W)).astype(BF)
+        for at, sl in ((a, slice(0, T)), (b, slice(T, 2 * T))):
+            R.q[at], R.k[at], R.v[at] = qq[sl], kk[sl], vv[sl]
+        return carry
+
+    with jax.named_scope("project_qkv"):
+        lax.fori_loop(0, 4, qkv_step, 0)
 
     with jax.named_scope("vectors"):
-        for e in range(1, 8):
-            vec_copy(e).wait_recv()
+        all_of(R.vec_all.at[seven], R.vec_s.at[0], R.vec_s.at[1]).wait_recv()
         for s in range(8):
             v = R.vec_all[s]
             R.vfull[:, s * T:(s + 1) * T] = v
             ids = jnp.broadcast_to(v[6:7], (T, T)).T
             R.segk[s] = jnp.where(ids < 0, -2.0, ids)
 
-    with jax.named_scope("wait_qkv_weights"):
-        for e in range(1, 8):
-            for j in range(3):
-                qkv_copy(e, j).wait_recv()
-        for j in range(5, 8):
-            local[j].wait()
-
-    def qkv_step(p, carry):
-        ag_wait(tok_all, 0, p)
-
-        @when(p == by_y)
-        def _():
-            for e in far_first:
-                win_copy(e).start()
-
-        a, b, x = pair(tok_all, p)
-        y = mm(x, rows(R.wqkv), NN)
-        qq = ((y[:, :W] + R.bq[...].astype(F32).reshape(1, W)) * 0.125).astype(BF)
-        kk = y[:, W:2 * W].astype(BF)
-        vv = (y[:, 2 * W:] + R.bv[...].astype(F32).reshape(1, W)).astype(BF)
-        for at, sl in ((a, slice(0, T)), (b, slice(T, 2 * T))):
-            R.q[at], R.k[at], R.v[at] = qq[sl], kk[sl], vv[sl]
-        return carry
-
-    with jax.named_scope("project_qkv"):
-        lax.fori_loop(0, 4, qkv_step, 0)
     for i in (1, 2, 3, 4):
         local[i].wait()
 
@@ -417,15 +429,10 @@
     R.kt[...] = rows(R.k).T
 
     with jax.named_scope("wait_hidden_weights"):
-        for e in range(1, 8):
-            win_copy(e).wait_recv()
+        all_of(R.win.at[seven], R.win_s.at[0], R.win_s.at[1]).wait_recv()
 
     def hidden_step(p, carry):
         ag_wait(y1_all, 1, p)
-
-        @pl.when(p > 1)
-        def _():
-            rs_combine(1, p - 1)
         a, b, x = pair(y1_all, p)
         z = hidden_in(x)
         cdf = 0.5 * (1.0 + lax.erf(z * 0.7071067811865476))
@@ -433,12 +440,17 @@
         slope = cdf + z * (jnp.exp(-0.5 * z * z) * 0.3989422804014327)
         R.hid[a], R.hid[b] = low[:T], low[T:]
         R.slope[a], R.slope[b] = slope[:T], slope[T:]
+
+        @pl.when(p > 1)
+        def _():
+            rs_combine(1, p - 1)
+
         rs_put(1, p, mm(low, R.wb_v[...], NN))
 
         return carry
 
     def hidden_in(x):
-        return mm(x, rows(R.win), NN) + R.bi[...].astype(F32).reshape(1, FW)
+        return mm(x, rows(R.win), NN) + R.bi_v[...].astype(F32).reshape(1, FW)
 
     with jax.named_scope("hidden"):
         lax.fori_loop(0, 4, hidden_step, 0)
@@ -450,7 +462,8 @@
         h2 = R.y1[...] + rs + R.vfull[1:2]
         n2, r2 = norm_parts(h2)
         gain = R.vfull[4:5]
-        R.out[...] = (n2 * gain + R.vfull[5:6]).astype(BF)
+        R.out_v[...] = (n2 * gain + R.vfull[5:6]).astype(BF)
+        put_out.start()
         cot = R.cot_v[...].astype(F32)
         dh2 = norm_back(cot * gain, n2, r2)
         R.dh2[...] = dh2
@@ -468,10 +481,6 @@
     def hidden_back_step(p, carry):
         ag_wait(df_all, 2, p)
 
-        @pl.when(p > 1)
-        def _():
-            rs_combine(2, p - 1)
-
         @when(p == by_both)
         def _():
             grad_back(0)
@@ -480,6 +489,11 @@
         slope = jnp.concatenate([R.slope[a], R.slope[b]], 0)
         dz = (mm(x, R.wb_v[...], NT) * slope).astype(BF)
         R.dz[a], R.dz[b] = dz[:T], dz[T:]
+
+        @pl.when(p > 1)
+        def _():
+            rs_combine(2, p - 1)
+
         rs_put(2, p, mm(dz, rows(R.win), NT))
 
         return carry
@@ -503,7 +517,7 @@
         z_produce(Z_IN + 2 * i + 1)
 
     def din_copy(t, s):
-        return rcopy(R.zsum_i.at[t], R.grad_i.at[s], R.din_s.at[t], R.din_r.at[s], (dp, t // 2, t % 2))
+        return rcopy(R.zsum_i.at[t], R.grad_i.at[s], R.din_s.at[0], R.din_s.at[1], (dp, t // 2, t % 2))
 
     def z_deliver(t):
         @pl.when(z_end)
@@ -537,7 +551,7 @@
 
     def sv_copy(e):
         to, at = dev(c32(e // 2), e % 2)
-        return rcopy(R.sv.at[:, lanes(at, T)], R.sv_rcv.at[me], R.sv_s.at[e], R.sv_r.at[e], to)
+        return rcopy(R.sv.at[:, lanes(at, T)], R.sv_rcv.at[me], R.sv_s.at[0], R.sv_s.at[1], to)
 
     for e in far_first:
         sv_copy(e).start()
@@ -578,7 +592,7 @@
 
     def dqkv_copy(p, flip):
         to, at = dev(p, flip)
-        return rcopy(R.dqkv_snd.at[at], R.zown_w.at[me], R.dqkv_s.at[p, flip], R.dqkv_r.at[p, flip], to)
+        return rcopy(R.dqkv_snd.at[at], R.zown_w.at[me], R.dqkv_s.at[0], R.dqkv_s.at[1], to)
 
     def dqkv_step(p):
         a, b = dev(c32(p), 0)[1], dev(c32(p), 1)[1]
@@ -617,8 +631,7 @@
         z_until(36.5)
 
     with jax.named_scope("small_grads"):
-        for e in range(1, 8):
-            sv_copy(e).wait_recv()
+        all_of(R.sv_rcv.at[seven], R.sv_s.at[0], R.sv_s.at[1]).wait_recv()
         acc = R.sv_rcv[0]
         for s in range(1, 8):
             acc = acc + R.sv_rcv[s]
@@ -638,17 +651,15 @@
         z_until(39.0)
 
     with jax.named_scope("z_rest"):
-        for p in range(4):
-            for flip in (0, 1):
-                if (p, flip) != (0, 0):
-                    dqkv_copy(c32(p), flip).wait_recv()
+        all_of(R.zown_w.at[seven], R.dqkv_s.at[0], R.dqkv_s.at[1]).wait_recv()
         for c in range(Z_QKV, Z_ALL):
             z_produce(c)
         z_until(42.0)
         rs_relay(3)
         z_until(46.0)
     with jax.named_scope("input_grad"):
-        R.igrad[...] = R.dh1[...] + rs_final(3)
+        R.igrad_v[...] = R.dh1[...] + rs_final(3)
+        put_igrad.start()
     with jax.named_scope("z_last"):
         for t in range(8):
             z_until(49.0 + 2 * t)
@@ -656,21 +667,34 @@
         z_until(1000.0)
 
     with jax.named_scope("finish"):
+        puts = [put_out, put_igrad]
+
+        def put(i, src, dst):
+            puts.append(pltpu.make_async_copy(src, dst, R.put_s.at[i]))
+            puts[-1].start()
+
         for c in range(Z_ALL):
             z_finish(c)
-        for t in range(8):
-            @pl.when(me != t)
-            def _():
-                din_copy(t, t).wait()
+            if c == Z_IN - 1:
+                put(2, R.zsum_b, R.gb)
+            if c == Z_OUT - 1:
+                all_of(R.grad_i.at[seven], R.din_s.at[0], R.din_s.at[1]).wait()
+                put(3, R.grad_i, R.gi)
+            if c == Z_SMALL:
+                put(4, R.zsum_o, R.go)
+                put(5, R.zsum_s, R.gs)
+            if c >= Z_QKV and c - Z_QKV < 7:
+                put(6 + c - Z_QKV, R.zsum_w.at[c - Z_QKV], R.gw.at[c - Z_QKV])
+        put(13, R.zsum_w.at[7], R.gw.at[7])
+        z_sent()
         for buf, r in ((tok_all, 0), (y1_all, 1), (df_all, 2), (da_all, 3)):
             ag_finish(buf, r)
-        for e in range(1, 8):
-            vec_copy(e).wait_send()
-            win_copy(e).wait_send()
-            sv_copy(e).wait_send()
-            for j in range(3):
-                qkv_copy(e, j).wait_send()
-            dqkv_copy(c32(e // 2), e % 2).wait_send()
+        for ref, sem in (
+            (R.vec_all, R.vec_s), (R.win, R.win_s), (R.sv_rcv, R.sv_s), (R.wqkv, R.qkv_s), (R.zown_w, R.dqkv_s),
+        ):
+            all_of(ref.at[seven], sem.at[0], sem.at[1]).wait_send()
+        for cp in puts:
+            cp.wait()
 
 
 def sharded_plan(
@@ -689,9 +713,10 @@
     )
     in_hbm = 8
     outs = dict(
-        out=((T, D), BF), igrad=((T, D), F32), zsum_b=((4, T, D), BF),
-        grad_i=((8, T, FW), BF), zsum_o=((T, D), BF), zsum_w=((8, T, 3 * W), BF), zsum_s=((16, T), BF),
-    )
+        out=((T, D), BF), igrad=((T, D), F32), gb=((4, T, D), BF), gi=((8, T, FW), BF), go=((T, D), BF),
+        gw=((8, T, 3 * W), BF), gs=((16, T), BF),
+    )
+    sums = dict(b=outs["gb"], i=outs["gi"], o=outs["go"], w=outs["gw"], s=outs["gs"])
     blocks = {k: ((8, T, D), BF) for k in ("tok_all", "y1_all", "df_all", "da_all")}
     scr = dict(
         **blocks,
@@ -706,74 +731,93 @@
         rcv_c=((4, 4, T, D), BF), rcv_l=((4, 4, T, D), BF),
         dk=((8 * T, W), F32), dv=((8 * T, W), F32), dqkv=((8, T, 3 * W), BF),
         dqkv_snd=((8, T, 3 * W), BF),
-        **{z + k[4:]: s for z in ("zown", "zmid") for k, s in outs.items() if k.startswith("zsum")},
-        **{k: ((8, T, FW), BF) for k in ("zown_i", "zmid_i", "zsum_i")},
+        **{z + k: v for z in ("zown_", "zsum_", "zmid_") for k, v in sums.items()}, grad_i=outs["gi"],
+        out_v=outs["out"], igrad_v=outs["igrad"],
+        **{k + "_v": (v.shape, v.dtype) for k, v in list(ins.items())[in_hbm:]},
     )
     sems = dict(
-        ag_s=(4, 4, 2), ag_r=(4, 4, 2), ag_fs=(4, 4, 2), ag_f=(4, 4, 2),
-        rs_cs=(4, 4), rs_cr=(4, 4), rs_ls=(4, 4, 2), rs_lr=(4, 4, 2),
-        z_s=(29, 2), z_r=(29, 2), loc=(8,), vec_s=(8,), vec_r=(8,), qkv_s=(8, 3), qkv_r=(8, 3), win_s=(8,), win_r=(8,),
-        sv_s=(8,), sv_r=(8,), din_s=(8,), din_r=(8,), dqkv_s=(4, 2), dqkv_r=(4, 2),
+        ag_s=(4,), ag_r=(4, 2), ag_f=(4, 2), rs_s=(2,), rs_cr=(4,), rs_lr=(4, 2),
+
+        z_s=(5, 2), z_r=(29, 2), loc=(6,), small_s=(10,), put_s=(14,), vec_s=(2,), qkv_s=(2,), win_s=(2,), sv_s=(2,), din_s=(2,), dqkv_s=(2,),
     )
     names = list(ins) + list(outs) + list(scr) + list(sems)
     res = pl.pallas_call(
         partial(layer_kernel, names),
         out_shape=[jax.ShapeDtypeStruct(*s) for s in outs.values()],
-        in_specs=[pl.BlockSpec(memory_space=pl.ANY if i < in_hbm else pltpu.VMEM) for i in range(len(ins))],
-        out_specs=[pl.BlockSpec(memory_space=pltpu.VMEM) for _ in outs],
+        in_specs=[pl.BlockSpec(memory_space=pltpu.HBM)] * len(ins),
+        out_specs=[pl.BlockSpec(memory_space=pltpu.HBM)] * len(outs),
         scratch_shapes=[pltpu.VMEM(*s) for s in scr.values()] + [pltpu.SemaphoreType.DMA(s) for s in sems.values()],
         compiler_params=pltpu.CompilerParams(collective_id=0, has_side_effects=True, vmem_limit_bytes=60 << 20),
         name="layer",
     )(*ins.values())
-    grid = 4
-    wide = pl.BlockSpec((T // grid, D), lambda i: (i, 0))
-
-    def whole(n):
-        return pl.BlockSpec((n,), lambda i: (0,))
-
-    firsts = [(T, D), (T, D), (T, D), (T, D), (T, D), (T, D), w_in.shape, w_back.shape]
-    types = [BF] + [F32] * 7
-    return_specs = [wide, wide] + [pl.BlockSpec((T, 2 * T), lambda i: (0, i))] * 3 + [
-        wide, pl.BlockSpec((T, 2 * FW), lambda i: (0, i)), pl.BlockSpec((T, D), lambda i: (i, 0)),
-    ]
+    firsts = [(T, D)] * 6 + [w_in.shape, w_back.shape]
     sizes = [T, T, T, FW, T, T, T, T, T]
+    shapes = [(n, t) for n, t in zip(firsts, [BF] + [F32] * 7)] + [((n,), F32) for n in sizes]
+    loaded = list(outs.values())
+    stored = [((3, T, D), F32), ((T, D), F32), (w_in.shape, F32), (w_back.shape, F32)] + shapes[8:]
     final = pl.pallas_call(
         finish_kernel,
-        grid=(grid,),
-        out_shape=[jax.ShapeDtypeStruct(s, t) for s, t in zip(firsts, types)]
-        + [jax.ShapeDtypeStruct((n,), F32) for n in sizes],
-        in_specs=[
-            wide, wide, pl.BlockSpec((1, T, D), lambda i: (i, 0, 0)), pl.BlockSpec((2, T, FW), lambda i: (i, 0, 0)),
-            wide, pl.BlockSpec((2, T, 3 * W), lambda i: (i, 0, 0)), pl.BlockSpec((16, T), lambda i: (0, 0)),
-        ],
-        out_specs=return_specs + [whole(n) for n in sizes],
+        out_shape=[jax.ShapeDtypeStruct(*s) for s in shapes],
+        in_specs=[pl.BlockSpec(memory_space=pltpu.HBM)] * len(loaded),
+        out_specs=[pl.BlockSpec(memory_space=pltpu.HBM)] * len(shapes),
+        scratch_shapes=[pltpu.VMEM(*s) for s in loaded + stored]
+        + [pltpu.SemaphoreType.DMA((len(loaded) + 4,)), pltpu.SemaphoreType.DMA((len(shapes) + 6,))],
+        compiler_params=pltpu.CompilerParams(vmem_limit_bytes=60 << 20),
         name="finish",
     )(*res)
     return (final[0][None], final[1][None], *final[2:])
 
 
-def finish_kernel(out, igrad, tb, ti, to, tw, ts, o_out, o_igrad, o_q, o_k, o_v, o_o, o_i, o_b, *o_small):
-    o_out[...] = out[...]
-    o_igrad[...] = igrad[...]
-    o_b[...] = tb[0].astype(F32)
-    o_o[...] = to[...].astype(F32)
-    width = ti.shape[2]
-    for j in range(2):
-        o_i[:, j * width:(j + 1) * width] = ti[j].astype(F32)
-    W = tw.shape[2] // 3
-    for j, o in enumerate((o_q, o_k, o_v)):
-        for s in range(2):
-            o[:, s * W:(s + 1) * W] = tw[s, :, j * W:(j + 1) * W].astype(F32)
-
-    @pl.when(pl.program_id(0) == 0)
-    def _():
-        v = ts[...].astype(F32)
-        bq, bv, bo, bi, bb, g1, s1, g2, s2 = o_small
-        for o, i in ((bq, 4), (bv, 5), (bo, 6), (bb, 7), (g1, 2), (s1, 3), (g2, 0), (s2, 1)):
-            o[...] = v[i]
-        n = v.shape[1]
-        for i in range(bi.shape[0] // n):
-            bi[i * n:(i + 1) * n] = v[8 + i]
+def finish_kernel(*refs):
+    ins, outs, rest = refs[:7], refs[7:24], refs[24:]
+    loaded, stored, (load_s, store_s) = rest[:7], rest[7:20], rest[20:]
+    out, igrad, gb, gi, go, gw, gs = loaded
+    qkv, o_o, o_i, o_b, *o_small = stored
+    order = (3, 2, 5, 4, 1, 0, 6)
+    loads = {i: pltpu.make_async_copy(ins[i], loaded[i], load_s.at[i]) for i in order}
+    for i in order:
+        loads[i].start()
+    stores = []
+
+    def store(src, dst):
+        stores.append(pltpu.make_async_copy(src, dst, store_s.at[len(stores)]))
+        stores[-1].start()
+
+    width = gi.shape[2]
+    loads[3].wait()
+    for j in range(8):
+        o_i[:, j * width:(j + 1) * width] = gi[j].astype(F32)
+    store(o_i, outs[6])
+    loads[2].wait()
+    T = gb.shape[1]
+    for j in range(4):
+        o_b[j * T:(j + 1) * T, :] = gb[j].astype(F32)
+    store(o_b, outs[7])
+    loads[5].wait()
+    W = gw.shape[2] // 3
+    for j in range(3):
+        for s in range(8):
+            qkv[j, :, s * W:(s + 1) * W] = gw[s, :, j * W:(j + 1) * W].astype(F32)
+        store(qkv.at[j], outs[2 + j])
+    loads[4].wait()
+    o_o[...] = go[...].astype(F32)
+    store(o_o, outs[5])
+    loads[1].wait()
+    store(igrad, outs[1])
+    loads[0].wait()
+    store(out, outs[0])
+    loads[6].wait()
+    v = gs[...].astype(F32)
+    bq, bv, bo, bi, bb, g1, s1, g2, s2 = o_small
+    for o, i in ((bq, 4), (bv, 5), (bo, 6), (bb, 7), (g1, 2), (s1, 3), (g2, 0), (s2, 1)):
+        o[...] = v[i]
+    n = v.shape[1]
+    for i in range(bi.shape[0] // n):
+        bi[i * n:(i + 1) * n] = v[8 + i]
+    for i, o in enumerate(o_small):
+        store(o, outs[8 + i])
+    for cp in stores:
+        cp.wait()
 
 
 def pick_plan(mesh):

time: 181 us -> 177 us (0.978)
  Pallas kernels: 180 us -> 176 us
    pallas_call x1, Pallas kernels: 174 us -> 171 us  [sharded_plan(): pl.pallas_call(partial(layer_kernel, names), out_shape=[jax.ShapeDtypeStr...]
where the time goes in v4:
time: 177 us
  Pallas kernels  176 us (99%)
    pallas_call x1, Pallas kernels, sharded_plan(): pl.pallas_call(partial(layer_kernel, names), out_shape=[jax.ShapeDtypeStr...  171 us
    pallas_call x1, Pallas kernels, sharded_plan(): pl.pallas_call(finish_kernel, out_shape=[jax.ShapeDtypeStruct(*s) for s i...  4.56 us

profile of v4, /device:TPU:0, one launch (start us, length us, event | category | flops | bytes accessed | tf_op | source)
XLA Modules:
  0.0 176.5 jit_solution(3935161554825625127)
XLA Ops:
  0.7 171.1 %layer.1 = (bf16[128,1024]{1,0:T(8,128)(2,1)}, f32[128,1024]{1,0:T(8,128)}, bf16[4,128,1024]{2,1,0:T(8,128)(2,1)}, bf16[8,128,512]{2,1,0:T(8,128)(2,1)}, bf16[12...) custom-call(bf16[128,1024]{1,0:T(8,128)(2,1)} %bitcast.4, bf16[128,1024]{1,0:T(8,128)(2,1)} %bitcast.5, ...), custom_call_target="tpu_custom_call" | custom-call | tf_op jit(solution)/shard_map/layer/pallas_call | solution.py:744
  171.8 4.6 %finish.1 = (bf16[128,1024]{1,0:T(8,128)(2,1)}, f32[128,1024]{1,0:T(8,128)}, f32[128,1024]{1,0:T(8,128)}, f32[128,1024]{1,0:T(8,128)}, f32[128,1024]{1,0:T(8,128...) custom-call(bf16[128,1024]{1,0:T(8,128)(2,1)} %get-tuple-element.41., ...), custom_call_target="tpu_custom_call" | custom-call | tf_op jit(solution)/shard_map/finish/pallas_call | solution.py:758

commit v5 on v4

--- a/solution.py
+++ b/solution.py
@@ -113,123 +113,136 @@
     half = (pl.ds(0, T // 2), pl.ds(T // 2, T // 2))
     by_y, by_x, by_both = 1, 2, 3
 
-    def ag_direct(buf, r, p, h):
+    def piece(st, q):
+        return pl.ds((2 * st + q) * (T // 4), T // 4)
+
+    def ag_direct(buf, r, st, p, q):
         to, _ = dev(c32(p), 0)
-        part = buf.at[me, half[h]]
-        return rcopy(part, part, R.ag_s.at[r], R.ag_r.at[p, h], to)
-
-    def ag_relay(buf, r, h):
-        via, over = (by_x, by_y) if h == 0 else (by_y, by_x)
+        part = buf.at[me, piece(st, q)]
+        return rcopy(part, part, R.ag_s.at[r], R.ag_r.at[st, p, q], to)
+
+    def ag_relay(buf, r, st, q):
+        via, over = (by_x, by_y) if q == 0 else (by_y, by_x)
         _, at = dev(c32(via), 0)
         to, _ = dev(c32(over), 0)
-        part = buf.at[at, half[h]]
-        return rcopy(part, part, R.ag_s.at[r], R.ag_r.at[by_both, h], to)
-
-    def ag_home(buf, r):
-        return rcopy(buf.at[me], buf.at[me], R.ag_s.at[r], R.ag_f.at[0, 0], partner)
-
-    def ag_forward(buf, r, p, h):
+        part = buf.at[at, piece(st, q)]
+        return rcopy(part, part, R.ag_s.at[r], R.ag_r.at[st, by_both, q], to)
+
+    def ag_home(buf, r, st):
+        part = buf.at[me, half[st]]
+        return rcopy(part, part, R.ag_s.at[r], R.ag_f.at[st, 0, 0], partner)
+
+    def ag_forward(buf, r, st, p, q):
         _, at = dev(c32(p), 0)
-        part = buf.at[at, half[h]]
-        return rcopy(part, part, R.ag_s.at[r], R.ag_f.at[p, h], partner)
-
-    def ag_start(buf, r):
-        ag_direct(buf, r, by_x, 0).start()
-        ag_direct(buf, r, by_y, 1).start()
-        ag_direct(buf, r, by_x, 1).start()
-        ag_direct(buf, r, by_y, 0).start()
-        ag_home(buf, r).start()
-
-    def ag_got(buf, r, p, h):
-        (ag_relay(buf, r, h) if p == by_both else ag_direct(buf, r, p, h)).wait_recv()
-        ag_forward(buf, r, p, h).start()
-
-    def ag_wait(buf, r, p, relayed=lambda: None):
-        @when(p == 0)
-        def _():
-            ag_home(buf, r).wait_recv()
-
-        @when(p == by_y)
-        def _():
-            ag_got(buf, r, by_x, 0)
-            ag_relay(buf, r, 0).start()
-            ag_got(buf, r, by_y, 1)
-            ag_relay(buf, r, 1).start()
-            relayed()
-            ag_got(buf, r, by_y, 0)
-            ag_got(buf, r, by_x, 1)
-            for h in (0, 1):
-                ag_forward(buf, r, by_y, h).wait_recv()
-
-        @when(p == by_x)
-        def _():
-            ag_got(buf, r, by_both, 0)
-            ag_got(buf, r, by_both, 1)
-            for h in (0, 1):
-                ag_forward(buf, r, by_x, h).wait_recv()
-
-        @when(p == by_both)
-        def _():
-            for h in (0, 1):
-                ag_forward(buf, r, by_both, h).wait_recv()
+        part = buf.at[at, piece(st, q)]
+        return rcopy(part, part, R.ag_s.at[r], R.ag_f.at[st, p, q], partner)
+
+    def ag_start(buf, r, st):
+        for p, q in ((by_x, 0), (by_y, 1), (by_x, 1), (by_y, 0)):
+            ag_direct(buf, r, st, p, q).start()
+        ag_home(buf, r, st).start()
+
+    def ag_got(buf, r, st, p, q):
+        (ag_relay(buf, r, st, q) if p == by_both else ag_direct(buf, r, st, p, q)).wait_recv()
+        ag_forward(buf, r, st, p, q).start()
+
+    def ag_near(buf, r, st):
+        for p, q in ((by_x, 0), (by_y, 1)):
+            ag_got(buf, r, st, p, q)
+            ag_relay(buf, r, st, q).start()
+        for p, q in ((by_y, 0), (by_x, 1)):
+            ag_got(buf, r, st, p, q)
+
+    def ag_far(buf, r, st):
+        for q in (0, 1):
+            ag_got(buf, r, st, by_both, q)
+
+    def ag_have(buf, r, st, p):
+        if p == 0:
+            ag_home(buf, r, st).wait_recv()
+        else:
+            for q in (0, 1):
+                ag_forward(buf, r, st, p, q).wait_recv()
+
+    def ag_wait(buf, r, p, between=lambda: None):
+        for st in (0, 1):
+            if p == by_y:
+                ag_near(buf, r, st)
+                between()
+            if p == by_x:
+                ag_far(buf, r, st)
+        for st in (0, 1):
+            ag_have(buf, r, st, p)
 
     def ag_finish(buf, r):
-        all_of(buf.at[seven], R.ag_s.at[r], R.ag_r.at[0, 0]).wait_send()
+        all_of(buf.at[seven], R.ag_s.at[r], R.ag_r.at[0, 0, 0]).wait_send()
 
     def pair(buf, p):
         a, b = dev(p, 0)[1], dev(p, 1)[1]
         return a, b, jnp.concatenate([buf[a], buf[b]], 0)
 
-    def rs_chip(r, p):
-        return rcopy(R.snd_c.at[p], R.rcv_c.at[r, p], R.rs_s.at[0], R.rs_cr.at[p], partner)
-
-    def rs_link(r, p, h):
-        over = p if p != by_both else (by_x, by_y)[h]
+    def half_pair(buf, p, st):
+        a, b = dev(p, 0)[1], dev(p, 1)[1]
+        return a, b, jnp.concatenate([buf[a, half[st]], buf[b, half[st]]], 0)
+
+    def rs_chip(r, st, p):
+        return rcopy(
+            R.snd_c.at[p, half[st]], R.rcv_c.at[r, p, half[st]], R.rs_s.at[0], R.rs_cr.at[st, p], partner
+        )
+
+    def rs_link(r, st, p, q):
+        over = p if p != by_both else (by_x, by_y)[q]
         to, _ = dev(c32(over), 0)
         return rcopy(
-            R.snd_l.at[p, half[h]], R.rcv_l.at[r, p, half[h]], R.rs_s.at[1], R.rs_lr.at[p, h], to
+            R.snd_l.at[p, piece(st, q)], R.rcv_l.at[r, p, piece(st, q)], R.rs_s.at[1], R.rs_lr.at[st, p, q], to
         )
 
-    def rs_put(r, p, part):
-        R.snd_c[p] = part[T:].astype(BF)
-        rs_chip(r, p).start()
-        R.keep[p] = part[:T]
-
-    def rs_combine(r, p):
-        rs_chip(r, p).wait_recv()
-        both = R.keep[p] + R.rcv_c[r, p].astype(F32)
-        R.keep[p] = both
-        R.snd_l[p] = both.astype(BF)
-
-        @when(p == by_y)
-        def _():
-            rs_link(r, by_y, 1).start()
-
-        @when(p == by_x)
-        def _():
-            rs_link(r, by_x, 0).start()
-
-        @when(p == by_both)
-        def _():
-            rs_link(r, by_both, 0).start()
-            rs_link(r, by_both, 1).start()
-
-    def rs_relay(r):
-        for p, h in ((by_y, 0), (by_x, 1)):
-            rs_link(r, by_both, h).wait_recv()
-            R.snd_l[p, half[h]] = (R.keep[p, half[h]] + R.rcv_l[r, by_both, half[h]].astype(F32)).astype(BF)
-            rs_link(r, p, h).start()
-
-    def rs_final(r):
-        rs_chip(r, c32(0)).wait_recv()
-        acc = R.keep[0] + R.rcv_c[r, 0].astype(F32)
+    def rs_put(r, st, p, same, other):
+        R.snd_c[p, half[st]] = other.astype(BF)
+        rs_chip(r, st, p).start()
+        R.keep[p, half[st]] = same
+
+    def rs_put_pair(r, p, part):
+        for st in (0, 1):
+            at = st * (T // 2)
+            rs_put(r, st, p, part[at:at + T // 2], part[T + at:T + at + T // 2])
+
+    def rs_combine(r, st, p):
+        rs_chip(r, st, p).wait_recv()
+        both = R.keep[p, half[st]] + R.rcv_c[r, p, half[st]].astype(F32)
+        R.keep[p, half[st]] = both
+        R.snd_l[p, half[st]] = both.astype(BF)
+        for target, parts in ((by_y, (1,)), (by_x, (0,)), (by_both, (0, 1))):
+            @when(p == target)
+            def _():
+                for q in parts:
+                    rs_link(r, st, target, q).start()
+
+    def rs_combine_pair(r, p):
+        rs_combine(r, 0, p)
+        rs_combine(r, 1, p)
+
+    def rs_relay(r, st):
+        for p, q in ((by_y, 0), (by_x, 1)):
+            rs_link(r, st, by_both, q).wait_recv()
+            rows_q = piece(st, q)
+            R.snd_l[p, rows_q] = (R.keep[p, rows_q] + R.rcv_l[r, by_both, rows_q].astype(F32)).astype(BF)
+            rs_link(r, st, p, q).start()
+
+    def rs_final(r, st):
+        rs_chip(r, st, c32(0)).wait_recv()
+        acc = R.keep[0, half[st]] + R.rcv_c[r, 0, half[st]].astype(F32)
         for p in (by_y, by_x):
-            for h in (0, 1):
-                rs_link(r, p, h).wait_recv()
-            acc = acc + R.rcv_l[r, p].astype(F32)
-        all_of(R.snd_c, R.rs_s.at[0], R.rs_cr.at[0]).wait_send()
-        all_of(R.snd_l.at[pl.ds(1, 3)], R.rs_s.at[1], R.rs_cr.at[0]).wait_send()
+            for q in (0, 1):
+                rs_link(r, st, p, q).wait_recv()
+            acc = acc + R.rcv_l[r, p, half[st]].astype(F32)
+        if st == 1:
+            all_of(R.snd_c, R.rs_s.at[0], R.rs_cr.at[0, 0]).wait_send()
+            all_of(R.snd_l.at[pl.ds(1, 3)], R.rs_s.at[1], R.rs_cr.at[0, 0]).wait_send()
         return acc
+
+    def rs_whole(r):
+        return jnp.concatenate([rs_final(r, 0), rs_final(r, 1)], 0)
 
     quarter = (pl.ds(0, T // 4), pl.ds(T // 4, T // 4))
     chunks = [("b", lambda x, q=q: x.at[0, q], T // 4) for q in quarter] + [("b", lambda x: x.at[0, half[1]], T // 2)]
@@ -331,7 +344,8 @@
             for j in range(3):
                 qkv_copy(e, j).start()
         local[0].wait()
-        ag_start(tok_all, 0)
+        for st in (0, 1):
+            ag_start(tok_all, 0, st)
         for cp in small:
             cp.wait()
         vecs = [x[...].astype(F32).reshape(1, T) for x in small_v[1:7]]
@@ -345,25 +359,23 @@
         all_of(R.wqkv.at[seven], R.qkv_s.at[0], R.qkv_s.at[1]).wait_recv()
         pltpu.make_async_copy(R.wqkv.at[me], R.wqkv.at[me], R.loc.at[5]).wait()
 
-    def qkv_step(p, carry):
+    def qkv_step(p):
         ag_wait(tok_all, 0, p)
 
-        @when(p == by_y)
-        def _():
+        if p == by_y:
             for e in far_first:
                 win_copy(e).start()
-
-        a, b, x = pair(tok_all, p)
+        a, b, x = pair(tok_all, c32(p))
         y = mm(x, rows(R.wqkv), NN)
         qq = ((y[:, :W] + R.bq_v[...].astype(F32).reshape(1, W)) * 0.125).astype(BF)
         kk = y[:, W:2 * W].astype(BF)
         vv = (y[:, 2 * W:] + R.bv_v[...].astype(F32).reshape(1, W)).astype(BF)
         for at, sl in ((a, slice(0, T)), (b, slice(T, 2 * T))):
             R.q[at], R.k[at], R.v[at] = qq[sl], kk[sl], vv[sl]
-        return carry
 
     with jax.named_scope("project_qkv"):
-        lax.fori_loop(0, 4, qkv_step, 0)
+        for p in range(4):
+            qkv_step(p)
 
     with jax.named_scope("vectors"):
         all_of(R.vec_all.at[seven], R.vec_s.at[0], R.vec_s.at[1]).wait_recv()
@@ -404,12 +416,12 @@
             if h == 0:
                 @pl.when(p < 3)
                 def _():
-                    rs_combine(0, p + 1)
+                    rs_combine_pair(0, p + 1)
 
         ct = jnp.concatenate(outs, 0).astype(BF)
         R.ctxt[:, lanes(a, T)] = ct[:, :T]
         R.ctxt[:, lanes(b, T)] = ct[:, T:]
-        rs_put(0, p, mm(ct, R.wo_v[...], TN))
+        rs_put_pair(0, p, mm(ct, R.wo_v[...], TN))
         return carry
 
     with jax.named_scope("attend"):
@@ -417,60 +429,69 @@
         lax.fori_loop(0, 4, attend_step, 0)
 
     with jax.named_scope("first_norm"):
-        rs_relay(0)
-        rs = rs_final(0)
-        h1 = tok_all[me].astype(F32) + rs + R.vfull[0:1]
-        n1, r1 = norm_parts(h1)
-        y1 = n1 * R.vfull[2:3] + R.vfull[3:4]
-        R.n1[...], R.y1[...] = n1, y1
-        R.r1[...] = jnp.broadcast_to(r1, R.r1.shape)
-        y1_all[me] = y1.astype(BF)
-        ag_start(y1_all, 1)
+        rs_relay(0, 0)
+        rs_relay(0, 1)
+        for st in (0, 1):
+            rs = rs_final(0, st)
+            h1 = tok_all[me, half[st]].astype(F32) + rs + R.vfull[0:1]
+            n1, r1 = norm_parts(h1)
+            y1 = n1 * R.vfull[2:3] + R.vfull[3:4]
+            R.n1[half[st]], R.y1[half[st]] = n1, y1
+            R.r1[half[st]] = jnp.broadcast_to(r1, (T // 2, 128))
+            y1_all[me, half[st]] = y1.astype(BF)
+            ag_start(y1_all, 1, st)
     R.kt[...] = rows(R.k).T
 
     with jax.named_scope("wait_hidden_weights"):
         all_of(R.win.at[seven], R.win_s.at[0], R.win_s.at[1]).wait_recv()
 
-    def hidden_step(p, carry):
-        ag_wait(y1_all, 1, p)
-        a, b, x = pair(y1_all, p)
-        z = hidden_in(x)
+    def hidden_step(st, p):
+        ag_have(y1_all, 1, st, p)
+        a, b, x = half_pair(y1_all, c32(p), st)
+        z = mm(x, rows(R.win), NN) + R.bi_v[...].astype(F32).reshape(1, FW)
         cdf = 0.5 * (1.0 + lax.erf(z * 0.7071067811865476))
         low = (z * cdf).astype(BF)
         slope = cdf + z * (jnp.exp(-0.5 * z * z) * 0.3989422804014327)
-        R.hid[a], R.hid[b] = low[:T], low[T:]
-        R.slope[a], R.slope[b] = slope[:T], slope[T:]
-
-        @pl.when(p > 1)
-        def _():
-            rs_combine(1, p - 1)
-
-        rs_put(1, p, mm(low, R.wb_v[...], NN))
-
-        return carry
-
-    def hidden_in(x):
-        return mm(x, rows(R.win), NN) + R.bi_v[...].astype(F32).reshape(1, FW)
+        R.hid[a, half[st]], R.hid[b, half[st]] = low[:T // 2], low[T // 2:]
+        R.slope[a, half[st]], R.slope[b, half[st]] = slope[:T // 2], slope[T // 2:]
+        if p > 1:
+            rs_combine(1, st, p - 1)
+        part = mm(low, R.wb_v[...], NN)
+        rs_put(1, st, p, part[:T // 2], part[T // 2:])
 
     with jax.named_scope("hidden"):
-        lax.fori_loop(0, 4, hidden_step, 0)
-        rs_combine(1, c32(3))
+        hidden_step(0, 0)
+        ag_near(y1_all, 1, 0)
+        hidden_step(0, 1)
+        hidden_step(1, 0)
+        ag_near(y1_all, 1, 1)
+        hidden_step(0, 2)
+        ag_far(y1_all, 1, 0)
+        hidden_step(1, 1)
+        hidden_step(0, 3)
+        ag_far(y1_all, 1, 1)
+        hidden_step(1, 2)
+        rs_combine(1, 0, 3)
+        hidden_step(1, 3)
+        rs_combine(1, 1, 3)
 
     with jax.named_scope("second_norm"):
-        rs_relay(1)
-        rs = rs_final(1)
-        h2 = R.y1[...] + rs + R.vfull[1:2]
-        n2, r2 = norm_parts(h2)
-        gain = R.vfull[4:5]
-        R.out_v[...] = (n2 * gain + R.vfull[5:6]).astype(BF)
+        rs_relay(1, 0)
+        rs_relay(1, 1)
+        for st in (0, 1):
+            rs = rs_final(1, st)
+            h2 = R.y1[half[st]] + rs + R.vfull[1:2]
+            n2, r2 = norm_parts(h2)
+            gain = R.vfull[4:5]
+            R.out_v[half[st]] = (n2 * gain + R.vfull[5:6]).astype(BF)
+            cot = R.cot_v[half[st]].astype(F32)
+            dh2 = norm_back(cot * gain, n2, r2)
+            R.dh2[half[st]] = dh2
+            df_all[me, half[st]] = dh2.astype(BF)
+            ag_start(df_all, 2, st)
+            sums = jnp.concatenate([colsum(cot * n2), colsum(cot)], 0)
+            R.sv[0:2, :] = sums if st == 0 else R.sv[0:2, :] + sums
         put_out.start()
-        cot = R.cot_v[...].astype(F32)
-        dh2 = norm_back(cot * gain, n2, r2)
-        R.dh2[...] = dh2
-        df_all[me] = dh2.astype(BF)
-        ag_start(df_all, 2)
-        R.sv[0:1, :] = colsum(cot * n2)
-        R.sv[1:2, :] = colsum(cot)
 
     def grad_back(i):
         x = R.hid[:, :, i * T:(i + 1) * T].reshape(8 * T, T)
@@ -478,35 +499,29 @@
         for c in range(3) if i == 0 else (2 * i + 1, 2 * i + 2):
             z_produce(c)
 
-    def hidden_back_step(p, carry):
+    def hidden_back_step(p):
         ag_wait(df_all, 2, p)
-
-        @when(p == by_both)
-        def _():
+        if p == by_both:
             grad_back(0)
-
-        a, b, x = pair(df_all, p)
+        a, b, x = pair(df_all, c32(p))
         slope = jnp.concatenate([R.slope[a], R.slope[b]], 0)
         dz = (mm(x, R.wb_v[...], NT) * slope).astype(BF)
         R.dz[a], R.dz[b] = dz[:T], dz[T:]
-
-        @pl.when(p > 1)
-        def _():
-            rs_combine(2, p - 1)
-
-        rs_put(2, p, mm(dz, rows(R.win), NT))
-
-        return carry
+        if p > 1:
+            rs_combine_pair(2, p - 1)
+        rs_put_pair(2, p, mm(dz, rows(R.win), NT))
 
     with jax.named_scope("hidden_back"):
-        lax.fori_loop(0, 4, hidden_back_step, 0)
-        rs_combine(2, c32(3))
+        for p in range(4):
+            hidden_back_step(p)
+        rs_combine_pair(2, 3)
 
     with jax.named_scope("grad_back"):
         for i in range(1, 4):
             grad_back(i)
         z_until(6.0)
-        rs_relay(2)
+        rs_relay(2, 0)
+        rs_relay(2, 1)
         z_until(7.5)
 
     def grad_in(i):
@@ -539,13 +554,14 @@
                 z_until(8.0 + i)
 
     with jax.named_scope("first_norm_back"):
-        rs = rs_final(2)
+        rs = rs_whole(2)
         dy1 = R.dh2[...] + rs
         n1 = R.n1[...]
         dh1 = norm_back(dy1 * R.vfull[2:3], n1, R.r1[:, 0:1])
         R.dh1[...] = dh1
         da_all[me] = dh1.astype(BF)
-        ag_start(da_all, 3)
+        for st in (0, 1):
+            ag_start(da_all, 3, st)
         R.sv[2:3, :] = colsum(dy1 * n1)
         R.sv[3:4, :] = colsum(dy1)
 
@@ -619,15 +635,15 @@
 
     def input_step(p):
         if p > 1:
-            rs_combine(3, p - 1)
+            rs_combine_pair(3, p - 1)
         a, b, x = pair(R.dqkv, c32(p))
-        rs_put(3, p, mm(x, rows(R.wqkv), NT))
+        rs_put_pair(3, p, mm(x, rows(R.wqkv), NT))
         z_until((30.8, 31.4, 32.8, 34.4)[p])
 
     with jax.named_scope("input_back"):
         for p in range(4):
             input_step(p)
-        rs_combine(3, c32(3))
+        rs_combine_pair(3, 3)
         z_until(36.5)
 
     with jax.named_scope("small_grads"):
@@ -655,10 +671,11 @@
         for c in range(Z_QKV, Z_ALL):
             z_produce(c)
         z_until(42.0)
-        rs_relay(3)
+        rs_relay(3, 0)
+        rs_relay(3, 1)
         z_until(46.0)
     with jax.named_scope("input_grad"):
-        R.igrad_v[...] = R.dh1[...] + rs_final(3)
+        R.igrad_v[...] = R.dh1[...] + rs_whole(3)
         put_igrad.start()
     with jax.named_scope("z_last"):
         for t in range(8):
@@ -736,8 +753,7 @@
         **{k + "_v": (v.shape, v.dtype) for k, v in list(ins.items())[in_hbm:]},
     )
     sems = dict(
-        ag_s=(4,), ag_r=(4, 2), ag_f=(4, 2), rs_s=(2,), rs_cr=(4,), rs_lr=(4, 2),
-
+        ag_s=(4,), ag_r=(2, 4, 2), ag_f=(2, 4, 2), rs_s=(2,), rs_cr=(2, 4), rs_lr=(2, 4, 2),
         z_s=(5, 2), z_r=(29, 2), loc=(6,), small_s=(10,), put_s=(14,), vec_s=(2,), qkv_s=(2,), win_s=(2,), sv_s=(2,), din_s=(2,), dqkv_s=(2,),
     )
     names = list(ins) + list(outs) + list(scr) + list(sems)

time: 177 us -> 167 us (0.944)
  Pallas kernels: 176 us -> 166 us
    pallas_call x1, Pallas kernels: 171 us -> 161 us  [sharded_plan(): pl.pallas_call(partial(layer_kernel, names), out_shape=[jax.ShapeDtypeStr...]
where the time goes in v5:
time: 167 us
  Pallas kernels  166 us (99%)
    pallas_call x1, Pallas kernels, sharded_plan(): pl.pallas_call(partial(layer_kernel, names), out_shape=[jax.ShapeDtypeStr...  161 us
    pallas_call x1, Pallas kernels, sharded_plan(): pl.pallas_call(finish_kernel, out_shape=[jax.ShapeDtypeStruct(*s) for s i...  4.56 us

profile of v5, /device:TPU:0, one launch (start us, length us, event | category | flops | bytes accessed | tf_op | source)
XLA Modules:
  0.0 166.8 jit_solution(1004079340611897955)
XLA Ops:
  0.7 161.3 %layer.1 = (bf16[128,1024]{1,0:T(8,128)(2,1)}, f32[128,1024]{1,0:T(8,128)}, bf16[4,128,1024]{2,1,0:T(8,128)(2,1)}, bf16[8,128,512]{2,1,0:T(8,128)(2,1)}, bf16[12...) custom-call(bf16[128,1024]{1,0:T(8,128)(2,1)} %bitcast.4, bf16[128,1024]{1,0:T(8,128)(2,1)} %bitcast.5, ...), custom_call_target="tpu_custom_call" | custom-call | tf_op jit(solution)/shard_map/layer/pallas_call | solution.py:760
  162.0 4.6 %finish.1 = (bf16[128,1024]{1,0:T(8,128)(2,1)}, f32[128,1024]{1,0:T(8,128)}, f32[128,1024]{1,0:T(8,128)}, f32[128,1024]{1,0:T(8,128)}, f32[128,1024]{1,0:T(8,128...) custom-call(bf16[128,1024]{1,0:T(8,128)(2,1)} %get-tuple-element.41., ...), custom_call_target="tpu_custom_call" | custom-call | tf_op jit(solution)/shard_map/finish/pallas_call | solution.py:774

commit v6 on v5

--- a/solution.py
+++ b/solution.py
@@ -81,17 +81,27 @@
         return pl.ds(pl.multiple_of(i * w, w), w)
 
     tok_all, y1_all, df_all, da_all = R.tok_all, R.y1_all, R.df_all, R.da_all
+    half = (pl.ds(0, T // 2), pl.ds(T // 2, T // 2))
+
+    def share(z):
+        return pl.ds(pl.multiple_of(T // 2 + z * (T // 8), T // 8), T // 8)
+
     small_in = (R.ids, R.bo, R.bb, R.g1, R.s1, R.g2, R.s2, R.bq, R.bv, R.bi)
     small_v = (R.ids_v, R.bo_v, R.bb_v, R.g1_v, R.s1_v, R.g2_v, R.s2_v, R.bq_v, R.bv_v, R.bi_v)
     local = [
         pltpu.make_async_copy(R.tok, tok_all.at[me], R.loc.at[0]),
         pltpu.make_async_copy(R.wb, R.wb_v, R.loc.at[1]),
         pltpu.make_async_copy(R.wo, R.wo_v, R.loc.at[2]),
-        pltpu.make_async_copy(R.wi.at[:, lanes(me, FW)], R.win.at[me], R.loc.at[3]),
+        pltpu.make_async_copy(R.wi.at[half[0], lanes(me, FW)], R.win.at[me, half[0]], R.loc.at[3]),
         pltpu.make_async_copy(R.cot, R.cot_v, R.loc.at[4]),
     ]
+    local_share = pltpu.make_async_copy(R.wi.at[share(dp), lanes(me, FW)], R.win.at[me, share(dp)], R.loc.at[6])
+    local_share.start()
     for j, w in enumerate((R.wq, R.wk, R.wv)):
-        local.append(pltpu.make_async_copy(w.at[:, lanes(me, W)], R.wqkv.at[me, :, pl.ds(j * W, W)], R.loc.at[5]))
+        for part, at in ((half[0], 5), (share(dp), 7)):
+            local.append(
+                pltpu.make_async_copy(w.at[part, lanes(me, W)], R.wqkv.at[me, part, pl.ds(j * W, W)], R.loc.at[at])
+            )
     small = [
         pltpu.make_async_copy(x, y, R.small_s.at[i])
         for i, (x, y) in enumerate(zip(small_in, small_v, strict=True))
@@ -110,7 +120,6 @@
     put_out = pltpu.make_async_copy(R.out_v, R.out, R.put_s.at[0])
     put_igrad = pltpu.make_async_copy(R.igrad_v, R.igrad, R.put_s.at[1])
 
-    half = (pl.ds(0, T // 2), pl.ds(T // 2, T // 2))
     by_y, by_x, by_both = 1, 2, 3
 
     def piece(st, q):
@@ -164,11 +173,11 @@
             for q in (0, 1):
                 ag_forward(buf, r, st, p, q).wait_recv()
 
-    def ag_wait(buf, r, p, between=lambda: None):
+    def ag_wait(buf, r, p, between=lambda st: None):
         for st in (0, 1):
             if p == by_y:
                 ag_near(buf, r, st)
-                between()
+                between(st)
             if p == by_x:
                 ag_far(buf, r, st)
         for st in (0, 1):
@@ -329,20 +338,47 @@
         to, _ = dev(c32(e // 2), e % 2)
         return rcopy(R.vec, R.vec_all.at[me], R.vec_s.at[0], R.vec_s.at[1], to)
 
-    def qkv_copy(e, j):
+    def qkv_copy(e, j, part, sems):
         to, at = dev(c32(e // 2), e % 2)
         w = (R.wq, R.wk, R.wv)[j]
-        return rcopy(w.at[:, lanes(at, W)], R.wqkv.at[me, :, pl.ds(j * W, W)], R.qkv_s.at[0], R.qkv_s.at[1], to)
-
-    def win_copy(e):
+        return rcopy(w.at[part, lanes(at, W)], R.wqkv.at[me, part, pl.ds(j * W, W)], sems.at[0], sems.at[1], to)
+
+    def win_copy(e, part, sems):
         to, at = dev(c32(e // 2), e % 2)
-        return rcopy(R.wi.at[:, lanes(at, FW)], R.win.at[me], R.win_s.at[0], R.win_s.at[1], to)
+        return rcopy(R.wi.at[part, lanes(at, FW)], R.win.at[me, part], sems.at[0], sems.at[1], to)
+
+    def along(i, k, way):
+        sign = 1 if way == 0 else -1
+        q, to = dp - sign * k, dp + sign
+        part = (R.wqkv, R.win)[i].at[:, share(q)]
+        return rcopy(part, part, R.along_s.at[i, way, k], R.along_r.at[i, way, k], (to, blk, head))
+
+    def along_do(i, k, act):
+        for way, sends, gets in (
+            (0, (dp <= 2) & (dp >= k), dp >= k + 1),
+            (1, (dp >= 1) & (dp + k <= 3), dp + k <= 2),
+        ):
+            @pl.when(gets if act == 1 else sends)
+            def _():
+                step = along(i, k, way)
+                (step.start, step.wait_recv, step.wait_send)[act]()
+
+    def along_send(i, k):
+        along_do(i, k, 0)
+
+    def along_got(i, k):
+        along_do(i, k, 1)
+
+    def along_sent(i):
+        for k in range(3):
+            along_do(i, k, 2)
 
     far_first = (6, 7, 2, 3, 4, 5, 1)
     with jax.named_scope("start_copies"):
-        for e in far_first:
-            for j in range(3):
-                qkv_copy(e, j).start()
+        for part, sems in ((share(dp), R.qshare_s), (half[0], R.qkv_s)):
+            for e in far_first:
+                for j in range(3):
+                    qkv_copy(e, j, part, sems).start()
         local[0].wait()
         for st in (0, 1):
             ag_start(tok_all, 0, st)
@@ -356,15 +392,32 @@
             vec_copy(e).start()
 
     with jax.named_scope("wait_qkv_weights"):
-        all_of(R.wqkv.at[seven], R.qkv_s.at[0], R.qkv_s.at[1]).wait_recv()
-        pltpu.make_async_copy(R.wqkv.at[me], R.wqkv.at[me], R.loc.at[5]).wait()
+        own = R.wqkv.at[me, pl.ds(0, T // 8)]
+        pltpu.make_async_copy(own, own, R.loc.at[7]).wait()
+        all_of(R.wqkv.at[seven, pl.ds(0, T // 8)], R.qshare_s.at[0], R.qshare_s.at[1]).wait()
+        along_send(0, 0)
+        along_got(0, 0)
+        along_send(0, 1)
+        ag_near(tok_all, 0, 0)
+        along_got(0, 1)
+        along_send(0, 2)
+        ag_near(tok_all, 0, 1)
+        ag_far(tok_all, 0, 0)
+        for e in far_first:
+            win_copy(e, share(dp), R.share_s).start()
+        own = R.wqkv.at[me, half[0]]
+        pltpu.make_async_copy(own, own, R.loc.at[5]).wait()
+        all_of(R.wqkv.at[seven, half[0]], R.qkv_s.at[0], R.qkv_s.at[1]).wait()
+        along_got(0, 2)
+        along_sent(0)
 
     def qkv_step(p):
-        ag_wait(tok_all, 0, p)
-
-        if p == by_y:
+        if p == by_x:
+            ag_far(tok_all, 0, 1)
             for e in far_first:
-                win_copy(e).start()
+                win_copy(e, half[0], R.win_s).start()
+        for st in (0, 1):
+            ag_have(tok_all, 0, st, p)
         a, b, x = pair(tok_all, c32(p))
         y = mm(x, rows(R.wqkv), NN)
         qq = ((y[:, :W] + R.bq_v[...].astype(F32).reshape(1, W)) * 0.125).astype(BF)
@@ -418,6 +471,17 @@
                 def _():
                     rs_combine_pair(0, p + 1)
 
+                @pl.when(p == 3)
+                def _():
+                    local_share.wait()
+                    all_of(R.win.at[seven, pl.ds(0, T // 8)], R.share_s.at[0], R.share_s.at[1]).wait()
+                    along_send(1, 0)
+
+                @pl.when(p == 1)
+                def _():
+                    along_got(1, 0)
+                    along_send(1, 1)
+
         ct = jnp.concatenate(outs, 0).astype(BF)
         R.ctxt[:, lanes(a, T)] = ct[:, :T]
         R.ctxt[:, lanes(b, T)] = ct[:, T:]
@@ -431,6 +495,8 @@
     with jax.named_scope("first_norm"):
         rs_relay(0, 0)
         rs_relay(0, 1)
+        along_got(1, 1)
+        along_send(1, 2)
         for st in (0, 1):
             rs = rs_final(0, st)
             h1 = tok_all[me, half[st]].astype(F32) + rs + R.vfull[0:1]
@@ -443,37 +509,46 @@
     R.kt[...] = rows(R.k).T
 
     with jax.named_scope("wait_hidden_weights"):
-        all_of(R.win.at[seven], R.win_s.at[0], R.win_s.at[1]).wait_recv()
-
-    def hidden_step(st, p):
-        ag_have(y1_all, 1, st, p)
-        a, b, x = half_pair(y1_all, c32(p), st)
-        z = mm(x, rows(R.win), NN) + R.bi_v[...].astype(F32).reshape(1, FW)
+        all_of(R.win.at[seven, half[0]], R.win_s.at[0], R.win_s.at[1]).wait()
+        along_got(1, 2)
+        along_sent(1)
+
+    def hidden_step(*items):
+        found = [half_pair(y1_all, c32(p), st) for st, p in items]
+        z = mm(jnp.concatenate([x for _, _, x in found], 0), rows(R.win), NN) + R.bi_v[...].astype(F32).reshape(1, FW)
         cdf = 0.5 * (1.0 + lax.erf(z * 0.7071067811865476))
         low = (z * cdf).astype(BF)
         slope = cdf + z * (jnp.exp(-0.5 * z * z) * 0.3989422804014327)
-        R.hid[a, half[st]], R.hid[b, half[st]] = low[:T // 2], low[T // 2:]
-        R.slope[a, half[st]], R.slope[b, half[st]] = slope[:T // 2], slope[T // 2:]
-        if p > 1:
-            rs_combine(1, st, p - 1)
         part = mm(low, R.wb_v[...], NN)
-        rs_put(1, st, p, part[:T // 2], part[T // 2:])
+        for i, ((st, p), (a, b, _)) in enumerate(zip(items, found, strict=True)):
+            same, other = slice(i * T, i * T + T // 2), slice(i * T + T // 2, (i + 1) * T)
+            rs_put(1, st, p, part[same], part[other])
+            R.hid[a, half[st]], R.hid[b, half[st]] = low[same], low[other]
+            R.slope[a, half[st]], R.slope[b, half[st]] = slope[same], slope[other]
 
     with jax.named_scope("hidden"):
-        hidden_step(0, 0)
+        for st in (0, 1):
+            ag_have(y1_all, 1, st, 0)
+        hidden_step((0, 0), (1, 0))
         ag_near(y1_all, 1, 0)
-        hidden_step(0, 1)
-        hidden_step(1, 0)
+        for p in (by_y, by_x):
+            ag_have(y1_all, 1, 0, p)
+        hidden_step((0, by_y), (0, by_x))
         ag_near(y1_all, 1, 1)
-        hidden_step(0, 2)
         ag_far(y1_all, 1, 0)
-        hidden_step(1, 1)
-        hidden_step(0, 3)
+        for p in (by_y, by_x):
+            ag_have(y1_all, 1, 1, p)
+            rs_combine(1, 0, p)
+        hidden_step((1, by_y), (1, by_x))
         ag_far(y1_all, 1, 1)
-        hidden_step(1, 2)
-        rs_combine(1, 0, 3)
-        hidden_step(1, 3)
-        rs_combine(1, 1, 3)
+        ag_have(y1_all, 1, 0, by_both)
+        hidden_step((0, by_both))
+        for p in (by_y, by_x):
+            rs_combine(1, 1, p)
+        ag_have(y1_all, 1, 1, by_both)
+        hidden_step((1, by_both))
+        rs_combine(1, 0, by_both)
+        rs_combine(1, 1, by_both)
 
     with jax.named_scope("second_norm"):
         rs_relay(1, 0)
@@ -519,10 +594,11 @@
     with jax.named_scope("grad_back"):
         for i in range(1, 4):
             grad_back(i)
-        z_until(6.0)
+        z_until(7.5)
         rs_relay(2, 0)
+        z_until(8.6)
         rs_relay(2, 1)
-        z_until(7.5)
+        z_until(9.8)
 
     def grad_in(i):
         x = y1_all[:, :, 2 * i * T:(2 * i + 2) * T].reshape(8 * T, 2 * T)
@@ -551,7 +627,7 @@
         for i in range(4):
             grad_in(i)
             if i % 2:
-                z_until(8.0 + i)
+                z_until(10.0 + i)
 
     with jax.named_scope("first_norm_back"):
         rs = rs_whole(2)
@@ -573,14 +649,14 @@
         sv_copy(e).start()
     R.sv_rcv[me] = R.sv[:, lanes(me, T)]
 
-    z_until(12.0)
+    z_until(13.8)
 
     R.dk[...] = jnp.zeros_like(R.dk)
     R.dv[...] = jnp.zeros_like(R.dv)
 
     def attend_back_step(p):
-        ag_wait(da_all, 3, p, lambda: z_until(17.0))
-        z_until((13.8, 20.0, 23.0, 25.8)[p])
+        ag_wait(da_all, 3, p, lambda st: z_until(18.0 + 2.5 * st))
+        z_until((14.6, 21.5, 25.0, 27.8)[p])
         a, b, x = pair(da_all, c32(p))
         qp = jnp.concatenate([R.q[a], R.q[b]], 0)
         dc = mm(x, R.wo_v[...], NT).astype(BF)
@@ -595,7 +671,7 @@
             outs.append(mm(R.kt[h * HD:(h + 1) * HD, :], ds, NN))
             R.dk[...] += mm(ds, qm, NN)
             R.dv[...] += mm(low, dcm, NN)
-            z_until((14.8, 21.0, 24.0, 26.8)[p] + h)
+            z_until((16.0, 22.8, 26.2, 28.8)[p] + 1.2 * h)
         dq = jnp.concatenate(outs, 0).T.astype(BF) * 0.125
         R.dqkv[a, :, 0:W] = dq[:T]
         R.dqkv[b, :, 0:W] = dq[T:]
@@ -621,7 +697,7 @@
         else:
             R.dqkv_snd[a] = g[:T]
             dqkv_copy(c32(p), 0).start()
-        z_until(28.3 + 0.5 * p)
+        z_until(30.5 + 0.5 * p)
 
     with jax.named_scope("grad_qkv"):
         for p in range(4):
@@ -631,20 +707,20 @@
         R.zown_o[...] = mm(R.ctxt[...], rows(da_all), NN).astype(BF)
         z_produce(Z_OUT)
         z_produce(Z_OUT + 1)
-        z_until(31.0)
+        z_until(33.0)
 
     def input_step(p):
         if p > 1:
             rs_combine_pair(3, p - 1)
         a, b, x = pair(R.dqkv, c32(p))
         rs_put_pair(3, p, mm(x, rows(R.wqkv), NT))
-        z_until((30.8, 31.4, 32.8, 34.4)[p])
+        z_until((33.5, 34.0, 35.5, 37.0)[p])
 
     with jax.named_scope("input_back"):
         for p in range(4):
             input_step(p)
         rs_combine_pair(3, 3)
-        z_until(36.5)
+        z_until(39.0)
 
     with jax.named_scope("small_grads"):
         all_of(R.sv_rcv.at[seven], R.sv_s.at[0], R.sv_s.at[1]).wait_recv()
@@ -664,22 +740,23 @@
         parts.append(jnp.zeros((16 - 8 - FW // T, T), F32))
         R.zown_s[...] = jnp.concatenate(parts, 0).astype(BF)
         z_produce(Z_SMALL)
-        z_until(39.0)
+        z_until(41.0)
 
     with jax.named_scope("z_rest"):
         all_of(R.zown_w.at[seven], R.dqkv_s.at[0], R.dqkv_s.at[1]).wait_recv()
         for c in range(Z_QKV, Z_ALL):
             z_produce(c)
-        z_until(42.0)
+        z_until(44.5)
         rs_relay(3, 0)
+        z_until(47.0)
         rs_relay(3, 1)
-        z_until(46.0)
+        z_until(50.0)
     with jax.named_scope("input_grad"):
         R.igrad_v[...] = R.dh1[...] + rs_whole(3)
         put_igrad.start()
     with jax.named_scope("z_last"):
         for t in range(8):
-            z_until(49.0 + 2 * t)
+            z_until(51.0 + 2 * t)
             z_deliver(t)
         z_until(1000.0)
 
@@ -707,7 +784,7 @@
         for buf, r in ((tok_all, 0), (y1_all, 1), (df_all, 2), (da_all, 3)):
             ag_finish(buf, r)
         for ref, sem in (
-            (R.vec_all, R.vec_s), (R.win, R.win_s), (R.sv_rcv, R.sv_s), (R.wqkv, R.qkv_s), (R.zown_w, R.dqkv_s),
+            (R.vec_all, R.vec_s), (R.sv_rcv, R.sv_s), (R.zown_w, R.dqkv_s),
         ):
             all_of(ref.at[seven], sem.at[0], sem.at[1]).wait_send()
         for cp in puts:
@@ -754,7 +831,7 @@
     )
     sems = dict(
         ag_s=(4,), ag_r=(2, 4, 2), ag_f=(2, 4, 2), rs_s=(2,), rs_cr=(2, 4), rs_lr=(2, 4, 2),
-        z_s=(5, 2), z_r=(29, 2), loc=(6,), small_s=(10,), put_s=(14,), vec_s=(2,), qkv_s=(2,), win_s=(2,), sv_s=(2,), din_s=(2,), dqkv_s=(2,),
+        z_s=(5, 2), z_r=(29, 2), loc=(8,), small_s=(10,), put_s=(14,), vec_s=(2,), qkv_s=(2,), win_s=(2,), share_s=(2,), qshare_s=(2,), along_s=(2, 2, 3), along_r=(2, 2, 3), sv_s=(2,), din_s=(2,), dqkv_s=(2,),
     )
     names = list(ins) + list(outs) + list(scr) + list(sems)
     res = pl.pallas_call(

time: 167 us -> 161 us (0.964)
  Pallas kernels: 166 us -> 160 us
    pallas_call x1, Pallas kernels: 161 us -> 155 us  [sharded_plan(): pl.pallas_call(partial(layer_kernel, names), out_shape=[jax.ShapeDtypeStr...]
where the time goes in v6:
time: 161 us
  Pallas kernels  160 us (99%)
    pallas_call x1, Pallas kernels, sharded_plan(): pl.pallas_call(partial(layer_kernel, names), out_shape=[jax.ShapeDtypeStr...  155 us
    pallas_call x1, Pallas kernels, sharded_plan(): pl.pallas_call(finish_kernel, out_shape=[jax.ShapeDtypeStruct(*s) for s i...  4.56 us

profile of v6, /device:TPU:0, one launch (start us, length us, event | category | flops | bytes accessed | tf_op | source)
XLA Modules:
  0.0 160.8 jit_solution(17338503493532580270)
XLA Ops:
  0.7 155.4 %layer.1 = (bf16[128,1024]{1,0:T(8,128)(2,1)}, f32[128,1024]{1,0:T(8,128)}, bf16[4,128,1024]{2,1,0:T(8,128)(2,1)}, bf16[8,128,512]{2,1,0:T(8,128)(2,1)}, bf16[12...) custom-call(bf16[128,1024]{1,0:T(8,128)(2,1)} %bitcast.4, bf16[128,1024]{1,0:T(8,128)(2,1)} %bitcast.5, ...), custom_call_target="tpu_custom_call" | custom-call | tf_op jit(solution)/shard_map/layer/pallas_call | solution.py:837
  156.1 4.6 %finish.1 = (bf16[128,1024]{1,0:T(8,128)(2,1)}, f32[128,1024]{1,0:T(8,128)}, f32[128,1024]{1,0:T(8,128)}, f32[128,1024]{1,0:T(8,128)}, f32[128,1024]{1,0:T(8,128...) custom-call(bf16[128,1024]{1,0:T(8,128)(2,1)} %get-tuple-element.41., ...), custom_call_target="tpu_custom_call" | custom-call | tf_op jit(solution)/shard_map/finish/pallas_call | solution.py:851

commit v7 on v6

--- a/solution.py
+++ b/solution.py
@@ -253,14 +253,14 @@
     def rs_whole(r):
         return jnp.concatenate([rs_final(r, 0), rs_final(r, 1)], 0)
 
-    quarter = (pl.ds(0, T // 4), pl.ds(T // 4, T // 4))
-    chunks = [("b", lambda x, q=q: x.at[0, q], T // 4) for q in quarter] + [("b", lambda x: x.at[0, half[1]], T // 2)]
+    first = ((0, T // 8), (T // 8, T // 8), (T // 4, T // 4), (T // 2, T // 2))
+    chunks = [("b", lambda x, i=i, n=n: x.at[0, pl.ds(i, n)], n) for i, n in first]
     chunks += [("b", lambda x, i=i, h=h: x.at[i, h], T // 2) for i in range(1, 4) for h in half]
     chunks += [("i", lambda x, t=t: x.at[t], T // 2) for t in range(8)]
     chunks += [("o", lambda x, h=h: x.at[h], T // 2) for h in half] + [("s", lambda x: x, 1)]
     chunks += [("w", lambda x, t=t: x.at[t], 3 * T // 8) for t in range(7)]
     chunks += [("w", lambda x, h=h: x.at[7, h], 3 * T // 16) for h in half]
-    Z_IN, Z_OUT, Z_SMALL, Z_QKV, Z_ALL = 9, 17, 19, 20, len(chunks)
+    Z_IN, Z_OUT, Z_SMALL, Z_QKV, Z_ALL = 10, 18, 20, 21, len(chunks)
 
     def zrefs(c):
         k, cut, _ = chunks[c]
@@ -447,13 +447,36 @@
 
     heads = W // HD
 
-    def ids_of(a, b):
-        return jnp.concatenate([R.vec_all[a, 6:7], R.vec_all[b, 6:7]], 1)
-
-    def attend_step(i, carry):
-        p = 3 - i
-        a, b, qp = pair(R.q, p)
-        segq = ids_of(a, b)
+    far, near_a, near_b, here = [
+        [(0, by_both), (1, by_both)], [(0, by_y), (0, by_x)], [(1, by_y), (1, by_x)], [(0, 0), (1, 0)],
+    ]
+
+    def rows_of(buf, items):
+        found = [half_pair(buf, c32(p), st) for st, p in items]
+        return [(a, b) for a, b, _ in found], jnp.concatenate([x for _, _, x in found], 0)
+
+    def put_rows(buf, items, places, value, lane=slice(None)):
+        for i, ((st, _), (a, b)) in enumerate(zip(items, places, strict=True)):
+            buf[a, half[st], lane] = value[i * T:i * T + T // 2]
+            buf[b, half[st], lane] = value[i * T + T // 2:(i + 1) * T]
+
+    def put_parts(r, items, part):
+        for i, (st, p) in enumerate(items):
+            rs_put(r, st, p, part[i * T:i * T + T // 2], part[i * T + T // 2:(i + 1) * T])
+
+    def ids_of(items, places):
+        return jnp.concatenate(
+            [
+                R.vec_all[at, 6:7, st * (T // 2):(st + 1) * (T // 2)]
+                for (st, _), both in zip(items, places, strict=True)
+                for at in both
+            ],
+            1,
+        )
+
+    def attend_step(slot, items, between):
+        places, qp = rows_of(R.q, items)
+        segq = ids_of(items, places)
         segk = rows(R.segk)
         allowed = jnp.concatenate([segk, segk], 1) == segq
         kk = rows(R.k)
@@ -464,39 +487,44 @@
             ex = jnp.exp(s - jnp.max(s, 0, keepdims=True))
             total = jnp.maximum(jnp.sum(ex, 0, keepdims=True), 1.0)
             pt = (ex * jnp.where(segq >= 0, 1.0 / total, 0.0)).astype(BF)
-            R.pt[h, p] = pt
+            R.pt[h, slot] = pt
             outs.append(mm(R.vt[h * HD:(h + 1) * HD, :], pt, NN))
             if h == 0:
-                @pl.when(p < 3)
-                def _():
-                    rs_combine_pair(0, p + 1)
-
-                @pl.when(p == 3)
-                def _():
-                    local_share.wait()
-                    all_of(R.win.at[seven, pl.ds(0, T // 8)], R.share_s.at[0], R.share_s.at[1]).wait()
-                    along_send(1, 0)
-
-                @pl.when(p == 1)
-                def _():
-                    along_got(1, 0)
-                    along_send(1, 1)
-
-        ct = jnp.concatenate(outs, 0).astype(BF)
-        R.ctxt[:, lanes(a, T)] = ct[:, :T]
-        R.ctxt[:, lanes(b, T)] = ct[:, T:]
-        rs_put_pair(0, p, mm(ct, R.wo_v[...], TN))
-        return carry
+                between()
+        ct = jnp.concatenate(outs, 0).T.astype(BF)
+        put_rows(R.ctx, items, places, ct)
+        put_parts(0, items, mm(ct, R.wo_v[...], NN))
+
+    def after_far():
+        local_share.wait()
+        all_of(R.win.at[seven, pl.ds(0, T // 8)], R.share_s.at[0], R.share_s.at[1]).wait()
+        along_send(1, 0)
+
+    def after_near_a():
+        rs_combine_pair(0, by_both)
+
+    def after_near_b():
+        rs_combine(0, 0, by_y)
+        rs_combine(0, 0, by_x)
+        along_got(1, 0)
+        along_send(1, 1)
+
+    def after_here():
+        rs_combine(0, 1, by_y)
+        rs_combine(0, 1, by_x)
+        rs_relay(0, 1)
 
     with jax.named_scope("attend"):
         R.vt[...] = rows(R.v).T
-        lax.fori_loop(0, 4, attend_step, 0)
-
-    with jax.named_scope("first_norm"):
+        attend_step(0, far, after_far)
+        attend_step(1, near_a, after_near_a)
+        attend_step(2, near_b, after_near_b)
         rs_relay(0, 0)
-        rs_relay(0, 1)
+        attend_step(3, here, after_here)
         along_got(1, 1)
         along_send(1, 2)
+
+    with jax.named_scope("first_norm"):
         for st in (0, 1):
             rs = rs_final(0, st)
             h1 = tok_all[me, half[st]].astype(F32) + rs + R.vfull[0:1]
@@ -513,41 +541,38 @@
         along_got(1, 2)
         along_sent(1)
 
-    def hidden_step(*items):
-        found = [half_pair(y1_all, c32(p), st) for st, p in items]
-        z = mm(jnp.concatenate([x for _, _, x in found], 0), rows(R.win), NN) + R.bi_v[...].astype(F32).reshape(1, FW)
+    def hidden_step(items):
+        places, x = rows_of(y1_all, items)
+        z = mm(x, rows(R.win), NN) + R.bi_v[...].astype(F32).reshape(1, FW)
         cdf = 0.5 * (1.0 + lax.erf(z * 0.7071067811865476))
         low = (z * cdf).astype(BF)
         slope = cdf + z * (jnp.exp(-0.5 * z * z) * 0.3989422804014327)
-        part = mm(low, R.wb_v[...], NN)
-        for i, ((st, p), (a, b, _)) in enumerate(zip(items, found, strict=True)):
-            same, other = slice(i * T, i * T + T // 2), slice(i * T + T // 2, (i + 1) * T)
-            rs_put(1, st, p, part[same], part[other])
-            R.hid[a, half[st]], R.hid[b, half[st]] = low[same], low[other]
-            R.slope[a, half[st]], R.slope[b, half[st]] = slope[same], slope[other]
+        put_parts(1, items, mm(low, R.wb_v[...], NN))
+        put_rows(R.hid, items, places, low)
+        put_rows(R.slope, items, places, slope)
 
     with jax.named_scope("hidden"):
+        ag_near(y1_all, 1, 0)
         for st in (0, 1):
             ag_have(y1_all, 1, st, 0)
-        hidden_step((0, 0), (1, 0))
-        ag_near(y1_all, 1, 0)
+        hidden_step(here)
         for p in (by_y, by_x):
             ag_have(y1_all, 1, 0, p)
-        hidden_step((0, by_y), (0, by_x))
+        hidden_step(near_a)
         ag_near(y1_all, 1, 1)
         ag_far(y1_all, 1, 0)
         for p in (by_y, by_x):
             ag_have(y1_all, 1, 1, p)
             rs_combine(1, 0, p)
-        hidden_step((1, by_y), (1, by_x))
+        hidden_step(near_b)
         ag_far(y1_all, 1, 1)
         ag_have(y1_all, 1, 0, by_both)
-        hidden_step((0, by_both))
+        hidden_step(far[:1])
         for p in (by_y, by_x):
             rs_combine(1, 1, p)
         ag_have(y1_all, 1, 1, by_both)
-        hidden_step((1, by_both))
         rs_combine(1, 0, by_both)
+        hidden_step(far[1:])
         rs_combine(1, 1, by_both)
 
     with jax.named_scope("second_norm"):
@@ -571,7 +596,7 @@
     def grad_back(i):
         x = R.hid[:, :, i * T:(i + 1) * T].reshape(8 * T, T)
         R.zown_b[i] = mm(x, rows(df_all), TN).astype(BF)
-        for c in range(3) if i == 0 else (2 * i + 1, 2 * i + 2):
+        for c in range(4) if i == 0 else (2 * i + 2, 2 * i + 3):
             z_produce(c)
 
     def hidden_back_step(p):
@@ -589,7 +614,9 @@
     with jax.named_scope("hidden_back"):
         for p in range(4):
             hidden_back_step(p)
+        z_until(2.8)
         rs_combine_pair(2, 3)
+        z_until(3.5)
 
     with jax.named_scope("grad_back"):
         for i in range(1, 4):
@@ -654,31 +681,42 @@
     R.dk[...] = jnp.zeros_like(R.dk)
     R.dv[...] = jnp.zeros_like(R.dv)
 
-    def attend_back_step(p):
-        ag_wait(da_all, 3, p, lambda st: z_until(18.0 + 2.5 * st))
-        z_until((14.6, 21.5, 25.0, 27.8)[p])
-        a, b, x = pair(da_all, c32(p))
-        qp = jnp.concatenate([R.q[a], R.q[b]], 0)
+    def attend_back_step(slot, items, times):
+        z_until(times[0])
+        places, x = rows_of(da_all, items)
+        _, qp = rows_of(R.q, items)
         dc = mm(x, R.wo_v[...], NT).astype(BF)
         vv = rows(R.v)
         outs = []
         for h in range(heads):
             dcm, qm = head_mask(h, dc), head_mask(h, qp)
-            low = R.pt[h, p]
+            low = R.pt[h, slot]
             pt = low.astype(F32)
             dpt = mm(vv, dcm, NT)
             ds = (pt * (dpt - jnp.sum(pt * dpt, 0, keepdims=True))).astype(BF)
             outs.append(mm(R.kt[h * HD:(h + 1) * HD, :], ds, NN))
             R.dk[...] += mm(ds, qm, NN)
             R.dv[...] += mm(low, dcm, NN)
-            z_until((16.0, 22.8, 26.2, 28.8)[p] + 1.2 * h)
+            z_until(times[1 + h])
         dq = jnp.concatenate(outs, 0).T.astype(BF) * 0.125
-        R.dqkv[a, :, 0:W] = dq[:T]
-        R.dqkv[b, :, 0:W] = dq[T:]
+        put_rows(R.dqkv, items, places, dq, slice(0, W))
 
     with jax.named_scope("attend_back"):
-        for p in range(4):
-            attend_back_step(p)
+        for st in (0, 1):
+            ag_have(da_all, 3, st, 0)
+        attend_back_step(3, here, (14.6, 16.0, 17.2))
+        for st, slot, items, times in ((0, 1, near_a, (20.2, 21.4, 22.6)), (1, 2, near_b, (24.6, 25.8, 27.0))):
+            ag_near(da_all, 3, st)
+            z_until((18.0, 23.4)[st])
+            if st == 1:
+                ag_far(da_all, 3, 0)
+            for p in (by_y, by_x):
+                ag_have(da_all, 3, st, p)
+            attend_back_step(slot, items, times)
+        ag_far(da_all, 3, 1)
+        for st in (0, 1):
+            ag_have(da_all, 3, st, by_both)
+        attend_back_step(0, far, (28.0, 29.2, 30.4))
         R.dqkv[:, :, W:2 * W] = R.dk[...].astype(BF).reshape(8, T, W)
         R.dqkv[:, :, 2 * W:] = R.dv[...].astype(BF).reshape(8, T, W)
 
@@ -704,7 +742,7 @@
             dqkv_step(p)
 
     with jax.named_scope("grad_out"):
-        R.zown_o[...] = mm(R.ctxt[...], rows(da_all), NN).astype(BF)
+        R.zown_o[...] = mm(rows(R.ctx), rows(da_all), TN).astype(BF)
         z_produce(Z_OUT)
         z_produce(Z_OUT + 1)
         z_until(33.0)
@@ -754,32 +792,39 @@
     with jax.named_scope("input_grad"):
         R.igrad_v[...] = R.dh1[...] + rs_whole(3)
         put_igrad.start()
+    puts = [put_out, put_igrad]
+
+    def put(i, src, dst):
+        puts.append(pltpu.make_async_copy(src, dst, R.put_s.at[i]))
+        puts[-1].start()
+
+    def z_through(c):
+        while any(second and at <= c for _, at, second in steps):
+            z_until(steps[0][0])
+        z_finish(c)
+
     with jax.named_scope("z_last"):
         for t in range(8):
             z_until(51.0 + 2 * t)
             z_deliver(t)
-        z_until(1000.0)
+            if t == 1:
+                for c in range(Z_IN):
+                    z_through(c)
+                put(2, R.zsum_b, R.gb)
+        for c in range(Z_OUT, Z_QKV):
+            z_through(c)
+        put(4, R.zsum_o, R.go)
+        put(5, R.zsum_s, R.gs)
+        for t in range(7):
+            z_through(Z_QKV + t)
+            put(6 + t, R.zsum_w.at[t], R.gw.at[t])
+        all_of(R.grad_i.at[seven], R.din_s.at[0], R.din_s.at[1]).wait()
+        put(3, R.grad_i, R.gi)
+        for c in (Z_ALL - 2, Z_ALL - 1):
+            z_through(c)
+        put(13, R.zsum_w.at[7], R.gw.at[7])
 
     with jax.named_scope("finish"):
-        puts = [put_out, put_igrad]
-
-        def put(i, src, dst):
-            puts.append(pltpu.make_async_copy(src, dst, R.put_s.at[i]))
-            puts[-1].start()
-
-        for c in range(Z_ALL):
-            z_finish(c)
-            if c == Z_IN - 1:
-                put(2, R.zsum_b, R.gb)
-            if c == Z_OUT - 1:
-                all_of(R.grad_i.at[seven], R.din_s.at[0], R.din_s.at[1]).wait()
-                put(3, R.grad_i, R.gi)
-            if c == Z_SMALL:
-                put(4, R.zsum_o, R.go)
-                put(5, R.zsum_s, R.gs)
-            if c >= Z_QKV and c - Z_QKV < 7:
-                put(6 + c - Z_QKV, R.zsum_w.at[c - Z_QKV], R.gw.at[c - Z_QKV])
-        put(13, R.zsum_w.at[7], R.gw.at[7])
         z_sent()
         for buf, r in ((tok_all, 0), (y1_all, 1), (df_all, 2), (da_all, 3)):
             ag_finish(buf, r)
@@ -817,7 +862,7 @@
         wqkv=((8, T, 3 * W), BF), win=((8, T, FW), BF), wb_v=(w_back.shape, BF), wo_v=(w_out.shape, BF),
         cot_v=((T, D), BF), vec=((8, T), F32), vec_all=((8, 8, T), F32), vfull=((8, D), F32), segk=((8, T, T), F32),
         q=((8, T, W), BF), k=((8, T, W), BF), v=((8, T, W), BF), vt=((W, 8 * T), BF), kt=((W, 8 * T), BF),
-        pt=((W // HD, 4, 8 * T, 2 * T), BF), ctxt=((W, 8 * T), BF),
+        pt=((W // HD, 4, 8 * T, 2 * T), BF), ctx=((8, T, W), BF),
         hid=((8, T, FW), BF), slope=((8, T, FW), F32), dz=((8, T, FW), BF),
         n1=((T, D), F32), r1=((T, 128), F32), y1=((T, D), F32), dh2=((T, D), F32), dh1=((T, D), F32),
         sv=((8, D), F32), sv_rcv=((8, 8, T), F32),
@@ -831,7 +876,7 @@
     )
     sems = dict(
         ag_s=(4,), ag_r=(2, 4, 2), ag_f=(2, 4, 2), rs_s=(2,), rs_cr=(2, 4), rs_lr=(2, 4, 2),
-        z_s=(5, 2), z_r=(29, 2), loc=(8,), small_s=(10,), put_s=(14,), vec_s=(2,), qkv_s=(2,), win_s=(2,), share_s=(2,), qshare_s=(2,), along_s=(2, 2, 3), along_r=(2, 2, 3), sv_s=(2,), din_s=(2,), dqkv_s=(2,),
+        z_s=(5, 2), z_r=(30, 2), loc=(8,), small_s=(10,), put_s=(14,), vec_s=(2,), qkv_s=(2,), win_s=(2,), share_s=(2,), qshare_s=(2,), along_s=(2, 2, 3), along_r=(2, 2, 3), sv_s=(2,), din_s=(2,), dqkv_s=(2,),
     )
     names = list(ins) + list(outs) + list(scr) + list(sems)
     res = pl.pallas_call(

time: 161 us -> 158 us (0.981)
  Pallas kernels: 160 us -> 157 us
    pallas_call x1, Pallas kernels: 155 us -> 152 us  [sharded_plan(): pl.pallas_call(partial(layer_kernel, names), out_shape=[jax.ShapeDtypeStr...]
where the time goes in v7:
time: 158 us
  Pallas kernels  157 us (99%)
    pallas_call x1, Pallas kernels, sharded_plan(): pl.pallas_call(partial(layer_kernel, names), out_shape=[jax.ShapeDtypeStr...  152 us
    pallas_call x1, Pallas kernels, sharded_plan(): pl.pallas_call(finish_kernel, out_shape=[jax.ShapeDtypeStruct(*s) for s i...  4.56 us

profile of v7, /device:TPU:0, one launch (start us, length us, event | category | flops | bytes accessed | tf_op | source)
XLA Modules:
  0.0 157.8 jit_solution(6600490935315020250)
XLA Ops:
  0.7 152.4 %layer.1 = (bf16[128,1024]{1,0:T(8,128)(2,1)}, f32[128,1024]{1,0:T(8,128)}, bf16[4,128,1024]{2,1,0:T(8,128)(2,1)}, bf16[8,128,512]{2,1,0:T(8,128)(2,1)}, bf16[12...) custom-call(bf16[128,1024]{1,0:T(8,128)(2,1)} %bitcast.4, bf16[128,1024]{1,0:T(8,128)(2,1)} %bitcast.5, ...), custom_call_target="tpu_custom_call" | custom-call | tf_op jit(solution)/shard_map/layer/pallas_call | solution.py:882
  153.1 4.6 %finish.1 = (bf16[128,1024]{1,0:T(8,128)(2,1)}, f32[128,1024]{1,0:T(8,128)}, f32[128,1024]{1,0:T(8,128)}, f32[128,1024]{1,0:T(8,128)}, f32[128,1024]{1,0:T(8,128...) custom-call(bf16[128,1024]{1,0:T(8,128)(2,1)} %get-tuple-element.41., ...), custom_call_target="tpu_custom_call" | custom-call | tf_op jit(solution)/shard_map/finish/pallas_call | solution.py:896

commit v8 on v7

--- a/solution.py
+++ b/solution.py
@@ -349,7 +349,7 @@
 
     def along(i, k, way):
         sign = 1 if way == 0 else -1
-        q, to = dp - sign * k, dp + sign
+        q, to = dp - sign * k, lax.rem(dp + sign + 4, 4)
         part = (R.wqkv, R.win)[i].at[:, share(q)]
         return rcopy(part, part, R.along_s.at[i, way, k], R.along_r.at[i, way, k], (to, blk, head))
 
@@ -534,7 +534,6 @@
             R.r1[half[st]] = jnp.broadcast_to(r1, (T // 2, 128))
             y1_all[me, half[st]] = y1.astype(BF)
             ag_start(y1_all, 1, st)
-    R.kt[...] = rows(R.k).T
 
     with jax.named_scope("wait_hidden_weights"):
         all_of(R.win.at[seven, half[0]], R.win_s.at[0], R.win_s.at[1]).wait()
@@ -573,6 +572,7 @@
         ag_have(y1_all, 1, 1, by_both)
         rs_combine(1, 0, by_both)
         hidden_step(far[1:])
+        R.kt[...] = rows(R.k).T
         rs_combine(1, 1, by_both)
 
     with jax.named_scope("second_norm"):
@@ -899,7 +899,7 @@
         in_specs=[pl.BlockSpec(memory_space=pltpu.HBM)] * len(loaded),
         out_specs=[pl.BlockSpec(memory_space=pltpu.HBM)] * len(shapes),
         scratch_shapes=[pltpu.VMEM(*s) for s in loaded + stored]
-        + [pltpu.SemaphoreType.DMA((len(loaded) + 4,)), pltpu.SemaphoreType.DMA((len(shapes) + 6,))],
+        + [pltpu.SemaphoreType.DMA((len(loaded) + 8,)), pltpu.SemaphoreType.DMA((len(shapes) + 6,))],
         compiler_params=pltpu.CompilerParams(vmem_limit_bytes=60 << 20),
         name="finish",
     )(*res)
@@ -911,40 +911,44 @@
     loaded, stored, (load_s, store_s) = rest[:7], rest[7:20], rest[20:]
     out, igrad, gb, gi, go, gw, gs = loaded
     qkv, o_o, o_i, o_b, *o_small = stored
-    order = (3, 2, 5, 4, 1, 0, 6)
-    loads = {i: pltpu.make_async_copy(ins[i], loaded[i], load_s.at[i]) for i in order}
-    for i in order:
-        loads[i].start()
+    whole = {i: pltpu.make_async_copy(ins[i], loaded[i], load_s.at[i]) for i in (5, 4, 1, 0, 6)}
+    pieces = [pltpu.make_async_copy(ins[2].at[j], gb.at[j], load_s.at[7 + j]) for j in range(4)]
+    pairs = [pl.ds(2 * j, 2) for j in range(4)]
+    pieces += [pltpu.make_async_copy(ins[3].at[p], gi.at[p], load_s.at[11 + j]) for j, p in enumerate(pairs)]
+    for cp in pieces + list(whole.values()):
+        cp.start()
     stores = []
 
     def store(src, dst):
         stores.append(pltpu.make_async_copy(src, dst, store_s.at[len(stores)]))
         stores[-1].start()
 
-    width = gi.shape[2]
-    loads[3].wait()
-    for j in range(8):
-        o_i[:, j * width:(j + 1) * width] = gi[j].astype(F32)
-    store(o_i, outs[6])
-    loads[2].wait()
-    T = gb.shape[1]
+    T, width = gb.shape[1], gi.shape[2]
     for j in range(4):
-        o_b[j * T:(j + 1) * T, :] = gb[j].astype(F32)
-    store(o_b, outs[7])
-    loads[5].wait()
+        pieces[j].wait()
+        part = pl.ds(j * T, T)
+        o_b[part, :] = gb[j].astype(F32)
+        store(o_b.at[part], outs[7].at[part])
+    for j in range(4):
+        pieces[4 + j].wait()
+        for s in (2 * j, 2 * j + 1):
+            o_i[:, s * width:(s + 1) * width] = gi[s].astype(F32)
+        part = pl.ds(2 * j * width, 2 * width)
+        store(o_i.at[:, part], outs[6].at[:, part])
+    whole[5].wait()
     W = gw.shape[2] // 3
     for j in range(3):
         for s in range(8):
             qkv[j, :, s * W:(s + 1) * W] = gw[s, :, j * W:(j + 1) * W].astype(F32)
         store(qkv.at[j], outs[2 + j])
-    loads[4].wait()
+    whole[4].wait()
     o_o[...] = go[...].astype(F32)
     store(o_o, outs[5])
-    loads[1].wait()
+    whole[1].wait()
     store(igrad, outs[1])
-    loads[0].wait()
+    whole[0].wait()
     store(out, outs[0])
-    loads[6].wait()
+    whole[6].wait()
     v = gs[...].astype(F32)
     bq, bv, bo, bi, bb, g1, s1, g2, s2 = o_small
     for o, i in ((bq, 4), (bv, 5), (bo, 6), (bb, 7), (g1, 2), (s1, 3), (g2, 0), (s2, 1)):

time: 158 us -> 158 us (level)
  no operation moved by 1% of the time
where the time goes in v8:
time: 158 us; the launch traced here: 157 us
  Pallas kernels  157 us (99%)
    pallas_call x1, Pallas kernels, sharded_plan(): pl.pallas_call(partial(layer_kernel, names), out_shape=[jax.ShapeDtypeStr...  152 us
    pallas_call x1, Pallas kernels, sharded_plan(): pl.pallas_call(finish_kernel, out_shape=[jax.ShapeDtypeStruct(*s) for s i...  4.22 us

profile of v8, /device:TPU:0, one launch (start us, length us, event | category | flops | bytes accessed | tf_op | source)
XLA Modules:
  0.0 157.5 jit_solution(4939064782393806740)
XLA Ops:
  0.7 152.4 %layer.1 = (bf16[128,1024]{1,0:T(8,128)(2,1)}, f32[128,1024]{1,0:T(8,128)}, bf16[4,128,1024]{2,1,0:T(8,128)(2,1)}, bf16[8,128,512]{2,1,0:T(8,128)(2,1)}, bf16[12...) custom-call(bf16[128,1024]{1,0:T(8,128)(2,1)} %bitcast.4, bf16[128,1024]{1,0:T(8,128)(2,1)} %bitcast.5, ...), custom_call_target="tpu_custom_call" | custom-call | tf_op jit(solution)/shard_map/layer/pallas_call | solution.py:882
  153.1 4.2 %finish.1 = (bf16[128,1024]{1,0:T(8,128)(2,1)}, f32[128,1024]{1,0:T(8,128)}, f32[128,1024]{1,0:T(8,128)}, f32[128,1024]{1,0:T(8,128)}, f32[128,1024]{1,0:T(8,128...) custom-call(bf16[128,1024]{1,0:T(8,128)(2,1)} %get-tuple-element.41., ...), custom_call_target="tpu_custom_call" | custom-call | tf_op jit(solution)/shard_map/finish/pallas_call | solution.py:896

commit v9 on v8

--- a/solution.py
+++ b/solution.py
@@ -253,14 +253,14 @@
     def rs_whole(r):
         return jnp.concatenate([rs_final(r, 0), rs_final(r, 1)], 0)
 
-    first = ((0, T // 8), (T // 8, T // 8), (T // 4, T // 4), (T // 2, T // 2))
+    first = ((0, T // 8), (T // 8, T // 8), (T // 4, T // 4), (T // 2, T // 4), (3 * T // 4, T // 4))
     chunks = [("b", lambda x, i=i, n=n: x.at[0, pl.ds(i, n)], n) for i, n in first]
     chunks += [("b", lambda x, i=i, h=h: x.at[i, h], T // 2) for i in range(1, 4) for h in half]
     chunks += [("i", lambda x, t=t: x.at[t], T // 2) for t in range(8)]
     chunks += [("o", lambda x, h=h: x.at[h], T // 2) for h in half] + [("s", lambda x: x, 1)]
     chunks += [("w", lambda x, t=t: x.at[t], 3 * T // 8) for t in range(7)]
     chunks += [("w", lambda x, h=h: x.at[7, h], 3 * T // 16) for h in half]
-    Z_IN, Z_OUT, Z_SMALL, Z_QKV, Z_ALL = 10, 18, 20, 21, len(chunks)
+    Z_IN, Z_OUT, Z_SMALL, Z_QKV, Z_ALL = 11, 19, 21, 22, len(chunks)
 
     def zrefs(c):
         k, cut, _ = chunks[c]
@@ -596,7 +596,7 @@
     def grad_back(i):
         x = R.hid[:, :, i * T:(i + 1) * T].reshape(8 * T, T)
         R.zown_b[i] = mm(x, rows(df_all), TN).astype(BF)
-        for c in range(4) if i == 0 else (2 * i + 2, 2 * i + 3):
+        for c in range(5) if i == 0 else (2 * i + 3, 2 * i + 4):
             z_produce(c)
 
     def hidden_back_step(p):
@@ -876,7 +876,7 @@
     )
     sems = dict(
         ag_s=(4,), ag_r=(2, 4, 2), ag_f=(2, 4, 2), rs_s=(2,), rs_cr=(2, 4), rs_lr=(2, 4, 2),
-        z_s=(5, 2), z_r=(30, 2), loc=(8,), small_s=(10,), put_s=(14,), vec_s=(2,), qkv_s=(2,), win_s=(2,), share_s=(2,), qshare_s=(2,), along_s=(2, 2, 3), along_r=(2, 2, 3), sv_s=(2,), din_s=(2,), dqkv_s=(2,),
+        z_s=(5, 2), z_r=(31, 2), loc=(8,), small_s=(10,), put_s=(14,), vec_s=(2,), qkv_s=(2,), win_s=(2,), share_s=(2,), qshare_s=(2,), along_s=(2, 2, 3), along_r=(2, 2, 3), sv_s=(2,), din_s=(2,), dqkv_s=(2,),
     )
     names = list(ins) + list(outs) + list(scr) + list(sems)
     res = pl.pallas_call(

time: 158 us -> 158 us (level)
  no operation moved by 1% of the time
where the time goes in v9:
time: 158 us
  Pallas kernels  157 us (99%)
    pallas_call x1, Pallas kernels, sharded_plan(): pl.pallas_call(partial(layer_kernel, names), out_shape=[jax.ShapeDtypeStr...  152 us
    pallas_call x1, Pallas kernels, sharded_plan(): pl.pallas_call(finish_kernel, out_shape=[jax.ShapeDtypeStruct(*s) for s i...  4.22 us

profile of v9, /device:TPU:0, one launch (start us, length us, event | category | flops | bytes accessed | tf_op | source)
XLA Modules:
  0.0 157.5 jit_solution(3566843335517777393)
XLA Ops:
  0.7 152.4 %layer.1 = (bf16[128,1024]{1,0:T(8,128)(2,1)}, f32[128,1024]{1,0:T(8,128)}, bf16[4,128,1024]{2,1,0:T(8,128)(2,1)}, bf16[8,128,512]{2,1,0:T(8,128)(2,1)}, bf16[12...) custom-call(bf16[128,1024]{1,0:T(8,128)(2,1)} %bitcast.4, bf16[128,1024]{1,0:T(8,128)(2,1)} %bitcast.5, ...), custom_call_target="tpu_custom_call" | custom-call | tf_op jit(solution)/shard_map/layer/pallas_call | solution.py:882
  153.1 4.2 %finish.1 = (bf16[128,1024]{1,0:T(8,128)(2,1)}, f32[128,1024]{1,0:T(8,128)}, f32[128,1024]{1,0:T(8,128)}, f32[128,1024]{1,0:T(8,128)}, f32[128,1024]{1,0:T(8,128...) custom-call(bf16[128,1024]{1,0:T(8,128)(2,1)} %get-tuple-element.41., ...), custom_call_target="tpu_custom_call" | custom-call | tf_op jit(solution)/shard_map/finish/pallas_call | solution.py:896
